TPU v7x, 32 devices: a whole 2x2x4 slice. The times are simulated.
32 devices in a mesh: tm: 8 (over y, x, core), blk: 4 (over z).
Axes of the slice: x: 2, y: 2, z: 4, core: 2. Of those that a mesh axis runs over, the one named last changes fastest.
Arguments:
- dynamics: float32 [256, 256], replicated
- dynamics_mask: int32 [8, 8], replicated, may hold values from 0 to 1, as said below
- obs_op: float32 [256, 256], replicated, may hold values from -0.375 to 0.375
- obs_mask: int32 [8, 8], replicated, may hold values from 0 to 1, as said below
- process_noise: float32 [256], replicated, may hold values from 0.0005 to 0.005
- initial_expectation: float32 [256], replicated, may hold values from -6 to 6
- filter_gains: float32 [128, 256, 256], P('tm', 'blk'), may hold values from -0.01953125 to 0.01953125
- observations: float32 [128, 256], P('tm'), may hold values from -6 to 6
- smooth_gains: float32 [128, 256, 256], P('tm', 'blk')
- filt_cov: float32 [128, 256, 256], P('tm', 'blk')
Outputs:
- smoothed_means: float32 [128, 256], P('tm', 'blk')
- smoothed_cov: float32 [128, 256, 256], P('tm', 'blk')
Inputs may be any that keep to these rules, and one draw needn't show every extreme that they name: `dynamics_mask`: diagonal blocks are 1. `obs_mask`: blocks with equal row and column index are 1.
All inputs are finite; a program needn't handle non-finite values.
Results may differ from a plain program's by a relative error of at most 0.0003.
Values sent between devices are 32-bit elements; how exact they have to be, the bound alone decides.
No kernel may reach another device: no remote copies, remote signals or barrier semaphores. Data moves between devices by JAX's collectives and lax.ppermute only.
A program may use at most 256 MiB of HBM per device.

v0:
```python
import jax
import jax.numpy as jnp
from jax import lax
from jax.sharding import PartitionSpec as P

highest = lax.Precision.HIGHEST


def from_behind(block, axis, distance):
    devices = range(lax.axis_size(axis))
    route = [(i - distance, i) for i in devices if i - distance in devices]
    return lax.ppermute(block, axis, route)


def expand_mask(mask, row_total, col_total):
    row_block = row_total // mask.shape[0]
    col_block = col_total // mask.shape[1]
    return jnp.repeat(jnp.repeat(mask.astype(jnp.float32), row_block, axis=0), col_block, axis=1)


def matmul(left, right):
    return jnp.matmul(left, right, precision=highest)


def filter_join(earlier, latter):
    return (matmul(latter[0], earlier[0]), matmul(latter[0], earlier[1]) + latter[1])


def smooth_join(earlier, latter):
    gain_late = latter[0]
    return (
        matmul(gain_late, earlier[0]),
        matmul(matmul(gain_late, earlier[1]), gain_late.T) + latter[1],
        matmul(gain_late, earlier[2]) + latter[2],
    )


def pack_filter(parts):
    return jnp.concatenate([parts[0], parts[1][None, :]], axis=0)


def unpack_filter(packed, width):
    return (packed[:width], packed[width])


def pack_smooth(parts):
    return jnp.concatenate([parts[0], parts[1], parts[2][None, :]], axis=0)


def unpack_smooth(packed, width):
    return (packed[:width], packed[width : 2 * width], packed[2 * width])


def window_work(
    trans_map,
    process_noise,
    initial_expectation,
    transition_operators,
    step_shifts,
    gain_full,
    cov_full,
    is_final,
    filter_prefix,
    smooth_prefix,
):
    width = trans_map.shape[0]
    step_count = transition_operators.shape[0]
    final_step = jnp.logical_and(is_final, jnp.arange(step_count) == step_count - 1)
    gain_full = jnp.where(final_step[:, None, None], jnp.float32(0.0), gain_full)
    ident_map = jnp.eye(width, dtype=jnp.float32)
    zero_mat = jnp.zeros((width, width), jnp.float32)
    zero_vec = jnp.zeros((width,), jnp.float32)

    def window_filter(running, step_parts):
        return (filter_join(running, step_parts), None)

    filt_window = lax.scan(
        window_filter, (ident_map, zero_vec), (transition_operators, step_shifts)
    )[0]
    filt_before = filter_prefix(filt_window)
    mean_in = matmul(filt_before[0], initial_expectation) + filt_before[1]

    def filter_walk(current, step_parts):
        current = matmul(step_parts[0], current) + step_parts[1]
        return (current, current)

    filt_means = lax.scan(filter_walk, mean_in, (transition_operators, step_shifts))[1]
    predicted = matmul(matmul(trans_map, cov_full), trans_map.T) + jnp.diag(process_noise)
    gain_trans = jnp.swapaxes(gain_full, 1, 2)
    residual_cov = cov_full - matmul(matmul(gain_full, predicted), gain_trans)
    moved_means = jnp.einsum("ij,tj->ti", trans_map, filt_means, precision=highest)
    offsets = filt_means - jnp.einsum("tij,tj->ti", gain_full, moved_means, precision=highest)

    def window_smooth(running, step_parts):
        return (smooth_join(running, step_parts), None)

    smooth_window = lax.scan(
        window_smooth,
        (ident_map, zero_mat, zero_vec),
        (gain_full, residual_cov, offsets),
        reverse=True,
    )[0]
    smooth_after = smooth_prefix(smooth_window)

    def smooth_walk(current, step_parts):
        cov_next, mean_next = current
        gain_now, resid_now, offset_now = step_parts
        cov_now = matmul(matmul(gain_now, cov_next), gain_now.T) + resid_now
        current_mean = matmul(gain_now, mean_next) + offset_now
        return ((cov_now, current_mean), (current_mean, cov_now))

    return lax.scan(
        smooth_walk,
        (smooth_after[1], smooth_after[2]),
        (gain_full, residual_cov, offsets),
        reverse=True,
    )[1]


def per_device(
    dynamics,
    dynamics_mask,
    obs_op,
    obs_mask,
    process_noise,
    initial_expectation,
    filter_gains,
    observations,
    smooth_gains,
    filt_cov,
):
    width = dynamics.shape[0]
    obs_width = obs_op.shape[0]
    row_count = filter_gains.shape[1]
    row_start = lax.axis_index("blk") * row_count
    trans_map = dynamics * expand_mask(dynamics_mask, width, width)
    obs_map = obs_op * expand_mask(obs_mask, obs_width, width)
    obs_dyn = matmul(obs_map, trans_map)
    own_rows = lax.dynamic_slice_in_dim(trans_map, row_start, row_count, 0)
    map_rows = own_rows[None] - matmul(filter_gains, obs_dyn)
    shift_rows = jnp.einsum("tro,to->tr", filter_gains, observations, precision=highest)
    ident_map = jnp.eye(width, dtype=jnp.float32)
    zero_mat = jnp.zeros((width, width), jnp.float32)
    zero_vec = jnp.zeros((width,), jnp.float32)
    transition_operators, step_shifts, gain_full, cov_full = (
        lax.all_gather(map_rows, "blk", axis=1, tiled=True),
        lax.all_gather(shift_rows, "blk", axis=1, tiled=True),
        lax.all_gather(smooth_gains, "blk", axis=1, tiled=True),
        lax.all_gather(filt_cov, "blk", axis=1, tiled=True),
    )
    tm_index = lax.axis_index("tm")
    tm_count = lax.axis_size("tm")

    def before_filter(filt_window):

        def chain_filter(turn_no, running):
            arrived = from_behind(pack_filter(filter_join(running, filt_window)), "tm", 1)
            parts = unpack_filter(arrived, width)
            first_window = tm_index == 0
            return (
                jnp.where(first_window, ident_map, parts[0]),
                jnp.where(first_window, zero_vec, parts[1]),
            )

        return lax.fori_loop(0, tm_count - 1, chain_filter, (ident_map, zero_vec))

    def after_smooth(smooth_window):

        def chain_smooth(turn_no, running):
            arrived = from_behind(pack_smooth(smooth_join(running, smooth_window)), "tm", -1)
            parts = unpack_smooth(arrived, width)
            last_window = tm_index == tm_count - 1
            return (
                jnp.where(last_window, ident_map, parts[0]),
                jnp.where(last_window, zero_mat, parts[1]),
                jnp.where(last_window, zero_vec, parts[2]),
            )

        return lax.fori_loop(0, tm_count - 1, chain_smooth, (ident_map, zero_mat, zero_vec))

    means_out, cov_out = window_work(
        trans_map,
        process_noise,
        initial_expectation,
        transition_operators,
        step_shifts,
        gain_full,
        cov_full,
        tm_index == tm_count - 1,
        before_filter,
        after_smooth,
    )
    means_rows = lax.dynamic_slice_in_dim(means_out, row_start, row_count, 1)
    cov_rows = lax.dynamic_slice_in_dim(cov_out, row_start, row_count, 1)
    return (means_rows, cov_rows)


def solution(mesh):
    return jax.shard_map(
        per_device,
        mesh=mesh,
        in_specs=(
            P(),
            P(),
            P(),
            P(),
            P(),
            P(),
            P("tm", "blk", None),
            P("tm", None),
            P("tm", "blk", None),
            P("tm", "blk", None),
        ),
        out_specs=(P("tm", "blk"), P("tm", "blk", None)),
        check_vma=False,
    )
```

profile of v0, /device:TPU:3, one launch (start us, length us, event | category | flops | bytes accessed | tf_op | source)
XLA Modules:
  0.0 547.2 jit_solution(12352522179231806885)
XLA Ops:
  16.8 10.8 %all-gather = f32[4,64,16]{1,2,0:T(8,128)S(1)} all-gather(f32[1,64,16]{1,2,0:T(8,128)S(1)} %bitcast.258), channel_id=1, replica_groups=mesh['tm'=8,'blk'=4] {'blk'}, dimensions={0}, use_global_device_ids=true | all-gather | bytes 20480 | tf_op jit(solution)/shard_map/all_gather | solution.py:147
  28.5 68.1 %all-gather.9.cloned.1.call-done = f32[16,256,256]{2,1,0:T(8,128)} async-done(((f32[16,64,256]{2,1,0:T(8,128)}), f32[16,256,256]{2,1,0:T(8,128)}) %all-gather.9.cloned.1.call-update) | async-done | bytes 4194320 | tf_op jit(solution)/shard_map/all_gather | solution.py:146
  96.6 43.3 %while.99 = (s32[]{:T(128)}, f32[256,256]{1,0:T(8,128)S(1)}, f32[256]{0:T(256)S(1)}, f32[16,256,256]{2,1,0:T(8,128)}, f32[16,256]{1,0:T(8,128)S(1)}, /*index=5*/s32[]{:T(128)}, s32[]{:T(128)}) while((s32[]{:T(128)}, f32[256,256]{1,0:T(8,128)S(1)}, f32[256]{0:T(256)S(1)}, f32[16,256,256]{2,1,0:T(8,128)}, f32[16,256]{1,0:T(8,128)S(1)}, ...), condition=%wide.region_1.2_spmd.clone, body=%wide.region_0.1_spmd.clone.sunk | while | flops 202113536 | bytes 1583195 | solution.py:77
  139.9 64.7 %while.98 = (s32[]{:T(128)}, f32[256,256]{1,0:T(8,128)S(1)}, f32[256]{0:T(256)S(1)}, pred[]{:T(512)}, f32[256,256]{1,0:T(8,128)S(1)}, /*index=5*/f32[256]{0:T(256)S(1)}, s32[]{:T(128)}) while((s32[]{:T(128)}, f32[256,256]{1,0:T(8,128)S(1)}, f32[256]{0:T(256)S(1)}, pred[]{:T(512)}, f32[256,256]{1,0:T(8,128)S(1)}, ...), condition=%wide.region_3.4_spmd.clone, body=%wide.region_2.3_spmd.clone.sunk | while | flops 202375936 | bytes 3159159 | solution.py:165
  140.7 3.6 collective-permute-start
  148.4 5.3 collective-permute-start
  157.9 5.3 collective-permute-start
  163.2 3.4 collective-permute-done
  167.4 5.3 collective-permute-start
  172.7 3.4 collective-permute-done
  176.9 5.3 collective-permute-start
  186.4 5.3 collective-permute-start
  191.7 3.4 collective-permute-done
  195.9 5.3 collective-permute-start
  201.2 3.4 collective-permute-done
  205.0 21.9 %while.96 = (s32[]{:T(128)}, f32[256]{0:T(256)S(1)}, f32[16,256]{1,0:T(8,128)S(1)}, f32[16,256,256]{2,1,0:T(8,128)}, f32[16,256]{1,0:T(8,128)S(1)}, /*index=5*/s32[]{:T(128)}, s32[]{:T(128)}) while((s32[]{:T(128)}, f32[256]{0:T(256)S(1)}, f32[16,256]{1,0:T(8,128)S(1)}, f32[16,256,256]{2,1,0:T(8,128)}, f32[16,256]{1,0:T(8,128)S(1)}, ...), condition=%wide.region_5.6_spmd, body=%wide.region_4.5_spmd.sunk | while | flops 786690 | bytes 271957 | solution.py:87
  231.9 3.6 fusion.62
  235.5 22.7 %all-gather.7.cloned.1.call-done = f32[16,256,256]{2,1,0:T(8,128)} async-done(((f32[16,64,256]{2,1,0:T(8,128)}), f32[16,256,256]{2,1,0:T(8,128)}) %all-gather.7.cloned.1.call-update) | async-done | bytes 4194320 | tf_op jit(solution)/shard_map/all_gather | solution.py:149
  258.2 5.6 %fusion.58 = f32[256,16,256]{2,0,1:T(8,128)S(1)} fusion(f32[16,256,256]{2,1,0:T(8,128)} %all-gather.7.cloned.1.call-done, f32[256,256]{0,1:T(8,128)S(1)} %bitcast_multiply_fusion.1), kind=kOutput, calls=%fused_computation.81 | convolution fusion | flops 3221225472 | bytes 8650752 | tf_op jit(solution)/shard_map/dot_general | solution.py:22
  263.8 3.4 fusion.51
  267.3 4.6 fusion.53
  271.9 5.5 %convolution_subtract_fusion = f32[16,256,256]{2,1,0:T(8,128)} fusion(f32[16,256,256]{2,1,0:T(8,128)S(1)} %copy-done.6, f32[16,256,256]{2,1,0:T(8,128)S(1)} %fusion.53, f32[16,256,256]{2,1,0:T(8,128)S(1)} %copy-done.5), kind=kOutput, calls=%fused_computation.72 | convolution fusion | flops 3222274048 | bytes 16777216 | tf_op jit(solution)/shard_map/dot_general | solution.py:22
  277.4 88.0 %while.100 = (s32[]{:T(128)}, f32[256,256]{1,0:T(8,128)S(1)}, f32[256,256]{1,0:T(8,128)S(1)}, f32[256]{0:T(256)S(1)}, f32[16,256,256]{2,1,0:T(8,128)}, /*index=5...) while((s32[]{:T(128)}, f32[256,256]{1,0:T(8,128)S(1)}, ...), condition=%wide.region_7.8_spmd.clone, body=%wide.region_6.7_spmd.clone.sunk | while | flops 604897792 | bytes 3418252 | solution.py:97
  365.5 92.3 %while.101 = (s32[]{:T(128)}, f32[256,256]{1,0:T(8,128)S(1)}, f32[256,256]{1,0:T(8,128)S(1)}, f32[256]{0:T(256)S(1)}, pred[]{:T(512)}, /*index=5*/f32[256,256]{1...) while((s32[]{:T(128)}, f32[256,256]{1,0:T(8,128)S(1)}, ...), condition=%wide.region_9.10_spmd.clone, body=%wide.region_8.9_spmd.clone.sunk | while | flops 605422592 | bytes 7091353 | solution.py:179
  369.9 8.9 %collective-permute-done.1 = f32[513,256]{1,0:T(8,128)S(1)} collective-permute-done((f32[513,256]{1,0:T(8,128)S(1)}, f32[513,256]{1,0:T(8,128)S(1)}, u32[]{:S(2)}, u32[]{:S(2)}) %collective-permute-start.1) | collective-permute-done | bytes 525344 | tf_op jit(solution)/shard_map/while/body/eval_jaxpr/ppermute | solution.py:12
  382.4 9.6 %collective-permute-done.1 = f32[513,256]{1,0:T(8,128)S(1)} collective-permute-done((f32[513,256]{1,0:T(8,128)S(1)}, f32[513,256]{1,0:T(8,128)S(1)}, u32[]{:S(2)}, u32[]{:S(2)}) %collective-permute-start.1) | collective-permute-done | bytes 525344 | tf_op jit(solution)/shard_map/while/body/eval_jaxpr/ppermute | solution.py:12
  395.5 9.6 %collective-permute-done.1 = f32[513,256]{1,0:T(8,128)S(1)} collective-permute-done((f32[513,256]{1,0:T(8,128)S(1)}, f32[513,256]{1,0:T(8,128)S(1)}, u32[]{:S(2)}, u32[]{:S(2)}) %collective-permute-start.1) | collective-permute-done | bytes 525344 | tf_op jit(solution)/shard_map/while/body/eval_jaxpr/ppermute | solution.py:12
  408.7 9.6 %collective-permute-done.1 = f32[513,256]{1,0:T(8,128)S(1)} collective-permute-done((f32[513,256]{1,0:T(8,128)S(1)}, f32[513,256]{1,0:T(8,128)S(1)}, u32[]{:S(2)}, u32[]{:S(2)}) %collective-permute-start.1) | collective-permute-done | bytes 525344 | tf_op jit(solution)/shard_map/while/body/eval_jaxpr/ppermute | solution.py:12
  421.8 9.6 %collective-permute-done.1 = f32[513,256]{1,0:T(8,128)S(1)} collective-permute-done((f32[513,256]{1,0:T(8,128)S(1)}, f32[513,256]{1,0:T(8,128)S(1)}, u32[]{:S(2)}, u32[]{:S(2)}) %collective-permute-start.1) | collective-permute-done | bytes 525344 | tf_op jit(solution)/shard_map/while/body/eval_jaxpr/ppermute | solution.py:12
  435.0 9.6 %collective-permute-done.1 = f32[513,256]{1,0:T(8,128)S(1)} collective-permute-done((f32[513,256]{1,0:T(8,128)S(1)}, f32[513,256]{1,0:T(8,128)S(1)}, u32[]{:S(2)}, u32[]{:S(2)}) %collective-permute-start.1) | collective-permute-done | bytes 525344 | tf_op jit(solution)/shard_map/while/body/eval_jaxpr/ppermute | solution.py:12
  448.1 9.6 %collective-permute-done.1 = f32[513,256]{1,0:T(8,128)S(1)} collective-permute-done((f32[513,256]{1,0:T(8,128)S(1)}, f32[513,256]{1,0:T(8,128)S(1)}, u32[]{:S(2)}, u32[]{:S(2)}) %collective-permute-start.1) | collective-permute-done | bytes 525344 | tf_op jit(solution)/shard_map/while/body/eval_jaxpr/ppermute | solution.py:12
  460.2 77.5 %while.97 = (s32[]{:T(128)}, f32[256,256]{1,0:T(8,128)S(1)}, f32[256]{0:T(256)S(1)}, f32[16,256]{1,0:T(8,128)S(1)}, f32[16,256,256]{2,1,0:T(8,128)}, /*index=5*/...) while((s32[]{:T(128)}, f32[256,256]{1,0:T(8,128)S(1)}, ...), condition=%wide.region_11.12_spmd, body=%wide.region_10.11_spmd.sunk | while | flops 403505408 | bytes 2369673 | solution.py:112
  (561 shorter events, 289.6 us)
Async XLA Ops:
  7.2 5.0 copy-start
  7.2 89.4 %all-gather.9.cloned.1.call-start = ((), (), s32[]{:S(2)}) async-start(), calls=%async_computation.2 | async-start | bytes 5242880 | tf_op jit(solution)/shard_map/all_gather | solution.py:146
  11.6 4.2 copy-start.8
  12.2 15.5 %copy-start.9 = (f32[256]{0:T(256)S(1)}, f32[256]{0:T(256)}, u32[]{:S(2)}) copy-start(f32[256]{0:T(256)} %param.26) | copy-start | bytes 3076
  14.2 212.9 %all-gather.5.cloned.1.call-start = ((), (), s32[]{:S(2)}) async-start(), calls=%async_computation | async-start | bytes 5242880 | tf_op jit(solution)/shard_map/all_gather | solution.py:148
  15.0 243.3 %all-gather.7.cloned.1.call-start = ((), (), s32[]{:S(2)}) async-start(), calls=%async_computation.1 | async-start | bytes 5242880 | tf_op jit(solution)/shard_map/all_gather | solution.py:149
  15.7 80.9 %copy-start.1 = (f32[256,256]{1,0:T(8,128)}, f32[256,256]{1,0:T(8,128)S(1)}, u32[]{:S(2)}) copy-start(f32[256,256]{1,0:T(8,128)S(1)} %fusion.61) | copy-start | bytes 786436
  139.9 64.7 %copy-start.10 = (f32[256]{0:T(256)S(1)}, f32[256]{0:T(256)}, u32[]{:S(2)}) copy-start(f32[256]{0:T(256)} %param.27) | copy-start | bytes 3076
  140.7 6.9 %collective-permute-start = (f32[257,256]{1,0:T(8,128)S(1)}, f32[257,256]{1,0:T(8,128)S(1)}, u32[]{:S(2)}, u32[]{:S(2)}) collective-permute-start(f32[257,256]{1,0:T(8,128)S(1)} %pad_maximum_fusion.4), channel_id=1, source_target_pairs={{0,4},{4,8},{8,12},{12,16},{16,20},{20,24},{24,28},{1,5},{5,9},{9,... | collective-permute-start | bytes 789512 | tf_op jit(solution)/shard_map/while/body/eval_jaxpr/ppermute | solution.py:12
  148.4 8.7 %collective-permute-start = (f32[257,256]{1,0:T(8,128)S(1)}, f32[257,256]{1,0:T(8,128)S(1)}, u32[]{:S(2)}, u32[]{:S(2)}) collective-permute-start(f32[257,256]{1,0:T(8,128)S(1)} %pad_maximum_fusion.4), channel_id=1, source_target_pairs={{0,4},{4,8},{8,12},{12,16},{16,20},{20,24},{24,28},{1,5},{5,9},{9,... | collective-permute-start | bytes 789512 | tf_op jit(solution)/shard_map/while/body/eval_jaxpr/ppermute | solution.py:12
  157.9 8.7 %collective-permute-start = (f32[257,256]{1,0:T(8,128)S(1)}, f32[257,256]{1,0:T(8,128)S(1)}, u32[]{:S(2)}, u32[]{:S(2)}) collective-permute-start(f32[257,256]{1,0:T(8,128)S(1)} %pad_maximum_fusion.4), channel_id=1, source_target_pairs={{0,4},{4,8},{8,12},{12,16},{16,20},{20,24},{24,28},{1,5},{5,9},{9,... | collective-permute-start | bytes 789512 | tf_op jit(solution)/shard_map/while/body/eval_jaxpr/ppermute | solution.py:12
  167.4 8.7 %collective-permute-start = (f32[257,256]{1,0:T(8,128)S(1)}, f32[257,256]{1,0:T(8,128)S(1)}, u32[]{:S(2)}, u32[]{:S(2)}) collective-permute-start(f32[257,256]{1,0:T(8,128)S(1)} %pad_maximum_fusion.4), channel_id=1, source_target_pairs={{0,4},{4,8},{8,12},{12,16},{16,20},{20,24},{24,28},{1,5},{5,9},{9,... | collective-permute-start | bytes 789512 | tf_op jit(solution)/shard_map/while/body/eval_jaxpr/ppermute | solution.py:12
  176.9 8.7 %collective-permute-start = (f32[257,256]{1,0:T(8,128)S(1)}, f32[257,256]{1,0:T(8,128)S(1)}, u32[]{:S(2)}, u32[]{:S(2)}) collective-permute-start(f32[257,256]{1,0:T(8,128)S(1)} %pad_maximum_fusion.4), channel_id=1, source_target_pairs={{0,4},{4,8},{8,12},{12,16},{16,20},{20,24},{24,28},{1,5},{5,9},{9,... | collective-permute-start | bytes 789512 | tf_op jit(solution)/shard_map/while/body/eval_jaxpr/ppermute | solution.py:12
  186.4 8.7 %collective-permute-start = (f32[257,256]{1,0:T(8,128)S(1)}, f32[257,256]{1,0:T(8,128)S(1)}, u32[]{:S(2)}, u32[]{:S(2)}) collective-permute-start(f32[257,256]{1,0:T(8,128)S(1)} %pad_maximum_fusion.4), channel_id=1, source_target_pairs={{0,4},{4,8},{8,12},{12,16},{16,20},{20,24},{24,28},{1,5},{5,9},{9,... | collective-permute-start | bytes 789512 | tf_op jit(solution)/shard_map/while/body/eval_jaxpr/ppermute | solution.py:12
  195.9 8.7 %collective-permute-start = (f32[257,256]{1,0:T(8,128)S(1)}, f32[257,256]{1,0:T(8,128)S(1)}, u32[]{:S(2)}, u32[]{:S(2)}) collective-permute-start(f32[257,256]{1,0:T(8,128)S(1)} %pad_maximum_fusion.4), channel_id=1, source_target_pairs={{0,4},{4,8},{8,12},{12,16},{16,20},{20,24},{24,28},{1,5},{5,9},{9,... | collective-permute-start | bytes 789512 | tf_op jit(solution)/shard_map/while/body/eval_jaxpr/ppermute | solution.py:12
  229.9 2.0 copy-start.4
  263.8 3.5 copy-start.5
  263.8 3.5 copy-start.7
  267.3 4.6 copy-start.6
  271.9 5.6 %copy-start.3 = (f32[256,256]{1,0:T(8,128)S(1)}, f32[256,256]{1,0:T(8,128)}, u32[]{:S(2)}) copy-start(f32[256,256]{1,0:T(8,128)} %copy-done.1) | copy-start | bytes 786436
  277.4 88.0 %copy-start.2 = (f32[256,256]{1,0:T(8,128)S(1)}, f32[256,256]{1,0:T(8,128)}, u32[]{:S(2)}) copy-start(f32[256,256]{1,0:T(8,128)} %copy-done.1) | copy-start | bytes 786436
  367.3 11.5 %collective-permute-start.1 = (f32[513,256]{1,0:T(8,128)S(1)}, f32[513,256]{1,0:T(8,128)S(1)}, u32[]{:S(2)}, u32[]{:S(2)}) collective-permute-start(f32[513,256]{1,0:T(8,128)S(1)} %pad_maximum_fusion.5), channel_id=1, source_target_pairs={{4,0},{8,4},{12,8},{16,12},{20,16},{24,20},{28,24},{5,1},{9,5},{13... | collective-permute-start | bytes 1575944 | tf_op jit(solution)/shard_map/while/body/eval_jaxpr/ppermute | solution.py:12
  380.4 11.5 %collective-permute-start.1 = (f32[513,256]{1,0:T(8,128)S(1)}, f32[513,256]{1,0:T(8,128)S(1)}, u32[]{:S(2)}, u32[]{:S(2)}) collective-permute-start(f32[513,256]{1,0:T(8,128)S(1)} %pad_maximum_fusion.5), channel_id=1, source_target_pairs={{4,0},{8,4},{12,8},{16,12},{20,16},{24,20},{28,24},{5,1},{9,5},{13... | collective-permute-start | bytes 1575944 | tf_op jit(solution)/shard_map/while/body/eval_jaxpr/ppermute | solution.py:12
  393.6 11.5 %collective-permute-start.1 = (f32[513,256]{1,0:T(8,128)S(1)}, f32[513,256]{1,0:T(8,128)S(1)}, u32[]{:S(2)}, u32[]{:S(2)}) collective-permute-start(f32[513,256]{1,0:T(8,128)S(1)} %pad_maximum_fusion.5), channel_id=1, source_target_pairs={{4,0},{8,4},{12,8},{16,12},{20,16},{24,20},{28,24},{5,1},{9,5},{13... | collective-permute-start | bytes 1575944 | tf_op jit(solution)/shard_map/while/body/eval_jaxpr/ppermute | solution.py:12
  406.8 11.5 %collective-permute-start.1 = (f32[513,256]{1,0:T(8,128)S(1)}, f32[513,256]{1,0:T(8,128)S(1)}, u32[]{:S(2)}, u32[]{:S(2)}) collective-permute-start(f32[513,256]{1,0:T(8,128)S(1)} %pad_maximum_fusion.5), channel_id=1, source_target_pairs={{4,0},{8,4},{12,8},{16,12},{20,16},{24,20},{28,24},{5,1},{9,5},{13... | collective-permute-start | bytes 1575944 | tf_op jit(solution)/shard_map/while/body/eval_jaxpr/ppermute | solution.py:12
  419.9 11.5 %collective-permute-start.1 = (f32[513,256]{1,0:T(8,128)S(1)}, f32[513,256]{1,0:T(8,128)S(1)}, u32[]{:S(2)}, u32[]{:S(2)}) collective-permute-start(f32[513,256]{1,0:T(8,128)S(1)} %pad_maximum_fusion.5), channel_id=1, source_target_pairs={{4,0},{8,4},{12,8},{16,12},{20,16},{24,20},{28,24},{5,1},{9,5},{13... | collective-permute-start | bytes 1575944 | tf_op jit(solution)/shard_map/while/body/eval_jaxpr/ppermute | solution.py:12
  433.1 11.5 %collective-permute-start.1 = (f32[513,256]{1,0:T(8,128)S(1)}, f32[513,256]{1,0:T(8,128)S(1)}, u32[]{:S(2)}, u32[]{:S(2)}) collective-permute-start(f32[513,256]{1,0:T(8,128)S(1)} %pad_maximum_fusion.5), channel_id=1, source_target_pairs={{4,0},{8,4},{12,8},{16,12},{20,16},{24,20},{28,24},{5,1},{9,5},{13... | collective-permute-start | bytes 1575944 | tf_op jit(solution)/shard_map/while/body/eval_jaxpr/ppermute | solution.py:12
  446.2 11.5 %collective-permute-start.1 = (f32[513,256]{1,0:T(8,128)S(1)}, f32[513,256]{1,0:T(8,128)S(1)}, u32[]{:S(2)}, u32[]{:S(2)}) collective-permute-start(f32[513,256]{1,0:T(8,128)S(1)} %pad_maximum_fusion.5), channel_id=1, source_target_pairs={{4,0},{8,4},{12,8},{16,12},{20,16},{24,20},{28,24},{5,1},{9,5},{13... | collective-permute-start | bytes 1575944 | tf_op jit(solution)/shard_map/while/body/eval_jaxpr/ppermute | solution.py:12
Sparse Core Ops, SparseCore 0:
  14.3 82.1 all-gather.8
  98.1 79.1 all-gather.4
  178.9 79.2 all-gather.6
where the time goes:
time: 553 us; the launch traced here: 547 us
  matrix products  264 us (48%)
  waiting for transfers between devices  182 us (33%)
  starting transfers between devices  49.5 us (9%)
  local copies, waits for them, and re-layouts  16.4 us (3%)
  between operations  14.1 us (3%)
  blocking collectives  10.8 us (2%)
  other arithmetic  6.58 us (1%)
    dot_general x209, matrix products, matmul(): return jnp.matmul(left, right, precision=highest)  259 us
    ppermute x14, waiting for transfers between devices, from_behind(): return lax.ppermute(block, axis, route)  89.9 us
    all_gather x1, waiting for transfers between devices, per_device(): lax.all_gather(map_rows, 'blk', axis=1, tiled=True)  68.1 us
    ppermute x14, starting transfers between devices, from_behind(): return lax.ppermute(block, axis, route)  49.4 us
    all_gather x1, waiting for transfers between devices, per_device(): lax.all_gather(filt_cov, 'blk', axis=1, tiled=True)  22.7 us
  transfers between devices with their start and end apart: 17, of which 16 were waited for; matrix products, arithmetic and copies ran while one was open for 14% of the time, Pallas kernels for 0%

commit v1 on v0

v1 whole, which is shorter than its diff:
```python
import functools

import jax
import jax.numpy as jnp
from jax import lax
from jax.experimental import pallas as pl
from jax.experimental.pallas import tpu as pltpu
from jax.sharding import PartitionSpec as P

highest = lax.Precision.HIGHEST
BOTH = ("tm", "blk")
PAD = 16


def halves(x):
    top = x.astype(jnp.bfloat16)
    return top, (x - top.astype(jnp.float32)).astype(jnp.bfloat16)


def product(left, right, dims):
    def one(a, b):
        return lax.dot_general(a, b, (dims, ((), ())), preferred_element_type=jnp.float32)

    return one(left[0], right[0]) + (one(left[0], right[1]) + one(left[1], right[0]))


def mm(left, right):
    return product(halves(left), halves(right), ((1,), (0,)))


def mm_nt(left, right):
    return product(halves(left), halves(right), ((1,), (1,)))


def rows_of(vec):
    return jnp.broadcast_to(vec, (PAD, vec.shape[-1]))


def expand_mask(mask, row_total, col_total):
    row_block = row_total // mask.shape[0]
    col_block = col_total // mask.shape[1]
    return jnp.repeat(jnp.repeat(mask.astype(jnp.float32), row_block, axis=0), col_block, axis=1)


def fill_rows(target, pieces, half):
    steps, rows = pieces[0].shape[0], pieces[0].shape[1]
    for turn, piece in enumerate(pieces):
        source = jnp.where(half == 0, turn, turn ^ 2)
        target[:, pl.ds(pl.multiple_of(source * rows, rows), rows), :] = piece[...]


def filter_chunk(where, k0, k1, k2, k3, seen, trans_t, dyn_t, packed, maps, shifts, gains):
    width = trans_t.shape[0]
    steps = k0.shape[0]
    fill_rows(gains, (k0, k1, k2, k3), where[0])
    dyn_parts = halves(dyn_t[...])
    running = None
    for step in range(steps):
        gain = halves(gains[step])
        nt = ((1,), (1,))
        seen_rows = rows_of(seen[step : step + 1, :])
        shift = product(halves(seen_rows), gain, nt)
        turned = trans_t[...] - product(dyn_parts, gain, nt)
        if running is None:
            running = (turned, shift)
        else:
            turned = halves(turned)
            running = tuple(product(halves(part), turned, ((1,), (0,))) for part in running)
            running = (running[0], running[1] + shift)
        maps[step] = running[0]
        shifts[step : step + 1, :] = running[1][0:1]
    packed[:width] = running[0]
    packed[width:] = running[1]


def filter_join(where, own, other, before, initial, total, front, state):
    width = own.shape[1]
    late = where[0]

    def follow(early, latter):
        latter_map = halves(latter[:width])
        total_map = product(halves(early[:width]), latter_map, ((1,), (0,)))
        total_shift = product(halves(early[width:]), latter_map, ((1,), (0,))) + latter[width:]
        return total_map, total_shift

    @pl.when(late == 0)
    def _():
        total[:width], total[width:] = follow(own, other)
        front[...] = before[...]

    @pl.when(late != 0)
    def _():
        total[:width], total[width:] = follow(other, own)
        front[:width], front[width:] = follow(other, before)

    state[...] = mm(rows_of(initial[...]), total[:width]) + total[width:]


def filter_last(where, state, initial, before, maps, shifts, means):
    width = before.shape[1]
    steps = maps.shape[0]
    started = jnp.where(where[0] == 0, rows_of(initial[...]), state[...])
    incoming = halves(mm(started, before[:width]) + before[width:])
    for step in range(steps):
        moved = product(incoming, halves(maps[step]), ((1,), (0,)))
        means[step : step + 1, :] = moved[0:1] + shifts[step : step + 1, :]


def smooth_chunk(where, g0, g1, g2, g3, f0, f1, f2, f3, means, trans, noise, packed, maps, covs, offsets, gains, filt, pred):
    width = trans.shape[0]
    steps = g0.shape[0]
    fill_rows(gains, (g0, g1, g2, g3), where[0])
    fill_rows(filt, (f0, f1, f2, f3), where[0])

    @pl.when(where[1] != 0)
    def _():
        gains[steps - 1] = jnp.zeros((width, width), jnp.float32)

    trans_parts = halves(trans[...])
    row_no = lax.broadcasted_iota(jnp.int32, (width, width), 0)
    col_no = lax.broadcasted_iota(jnp.int32, (width, width), 1)
    noise_mat = jnp.where(row_no == col_no, noise[...], 0.0)
    for step in range(steps):
        moved = halves(product(trans_parts, halves(filt[step]), ((1,), (0,))))
        pred[step] = product(moved, trans_parts, ((1,), (1,))) + noise_mat
    cov, mean, chain = None, None, None
    for step in reversed(range(steps)):
        gain = halves(gains[step])
        own_mean = rows_of(means[step : step + 1, :])
        moved_mean = product(halves(own_mean), trans_parts, ((1,), (1,)))
        if cov is None:
            gap, mean_gap, chain = -pred[step], -moved_mean, gains[step]
        else:
            gap, mean_gap = cov - pred[step], mean - moved_mean
            chain = product(gain, halves(chain), ((1,), (0,)))
        gap = halves(product(gain, halves(gap), ((1,), (0,))))
        cov = filt[step] + product(gap, gain, ((1,), (1,)))
        mean = own_mean + product(halves(mean_gap), gain, ((1,), (1,)))
        maps[step] = chain
        covs[step] = cov
        offsets[step : step + 1, :] = mean[0:1]
    packed[:width] = chain
    packed[width : 2 * width] = cov
    packed[2 * width :] = mean


def carry(gain, early_cov, early_mean, cov, mean):
    moved = halves(product(gain, halves(cov), ((1,), (0,))))
    return (
        early_cov + product(moved, gain, ((1,), (1,))),
        early_mean + product(halves(mean), gain, ((1,), (1,))),
    )


def smooth_join(where, own, other, after, total, behind):
    width = own.shape[1]
    late = where[0]

    def follow(early, latter, target):
        gain = halves(early[:width])
        target[:width] = product(gain, halves(latter[:width]), ((1,), (0,)))
        target[width : 2 * width], target[2 * width :] = carry(
            gain,
            early[width : 2 * width],
            early[2 * width :],
            latter[width : 2 * width],
            latter[2 * width :],
        )

    @pl.when(late == 0)
    def _():
        follow(own, other, total)
        follow(after, other, behind)

    @pl.when(late != 0)
    def _():
        follow(other, own, total)
        behind[...] = after[...]


def smooth_last(where, other, after, maps, covs, offsets, p0, p1, p2, p3, start):
    width = after.shape[1]
    steps = maps.shape[0]
    rows = width // 4
    half = where[1]

    @pl.when(where[0] == 0)
    def _():
        start[:width], start[width:] = carry(
            halves(after[:width]),
            after[width : 2 * width],
            after[2 * width :],
            other[:width],
            other[width:],
        )

    @pl.when(where[0] != 0)
    def _():
        start[...] = after[width:]

    begun = halves(start[:width])
    begun_mean = halves(start[width:])
    flip = half != 0
    pieces = (p0, p1, p2, p3)
    mean_rows = []
    for step in range(steps):
        gain = halves(maps[step])
        moved = halves(product(gain, begun, ((1,), (0,))))
        cov = covs[step] + product(moved, gain, ((1,), (1,)))
        mean = product(begun_mean, gain, ((1,), (1,)))
        mean_rows.append(mean[0:1] + offsets[step : step + 1, :])
        for turn, piece in enumerate(pieces):
            block = jnp.where(
                flip,
                cov[rows * (turn ^ 2) : rows * (turn ^ 2) + rows],
                cov[rows * turn : rows * turn + rows],
            )
            piece[step * rows : step * rows + rows] = block
    all_means = jnp.concatenate(mean_rows, axis=0)
    for piece in pieces:
        piece[steps * rows :] = all_means


def call(body, outs, scratch=()):
    def run(where, *operands):
        return pl.pallas_call(
            body,
            out_shape=[jax.ShapeDtypeStruct(shape, jnp.float32) for shape in outs],
            in_specs=[pl.BlockSpec(memory_space=pltpu.SMEM)]
            + [pl.BlockSpec(memory_space=pltpu.VMEM)] * len(operands),
            out_specs=[pl.BlockSpec(memory_space=pltpu.VMEM)] * len(outs),
            scratch_shapes=[pltpu.VMEM(shape, jnp.float32) for shape in scratch],
            compiler_params=pltpu.CompilerParams(vmem_limit_bytes=48 * 1024 * 1024),
        )(jnp.stack([jnp.int32(w) for w in where]), *operands)

    return run


def per_device(
    dynamics,
    dynamics_mask,
    obs_op,
    obs_mask,
    process_noise,
    initial_expectation,
    filter_gains,
    observations,
    smooth_gains,
    filt_cov,
):
    width = dynamics.shape[0]
    obs_width = obs_op.shape[0]
    step_count, row_count = filter_gains.shape[:2]
    steps = step_count // 2
    tm, blk = lax.axis_index("tm"), lax.axis_index("blk")
    tm_count, blk_count = lax.axis_size("tm"), lax.axis_size("blk")
    lines = tm_count // 2
    half = tm % 2
    worker = jnp.logical_or(blk == 1, blk == 2)
    upper = jnp.int32(blk == 2)

    def place(t, z):
        return t * blk_count + z

    def to_workers(array, turn):
        route = [
            (place(2 * line + core, turn ^ (2 * part)), place(2 * line + part, 1 + core))
            for line in range(lines)
            for core in range(2)
            for part in range(2)
        ]
        start = jnp.where(blk == turn, 0, steps)
        return lax.ppermute(lax.dynamic_slice_in_dim(array, start, steps, 0), BOTH, route)

    def from_workers(array, turn):
        route = [
            (place(2 * line + part, 1 + core), place(2 * line + core, turn ^ (2 * part)))
            for line in range(lines)
            for core in range(2)
            for part in range(2)
        ]
        return lax.ppermute(array, BOTH, route)

    levels = [(lambda t, z: (t ^ 1, z), half), (lambda t, z: (t, 3 - z), upper)]
    distance = 2
    while distance < tm_count:
        levels.append((functools.partial(lambda d, t, z: (t ^ d, z), distance), (tm // distance) % 2))
        distance *= 2

    def swap(array, level):
        route = [
            (place(t, z), place(*levels[level][0](t, z))) for t in range(tm_count) for z in (1, 2)
        ]
        return lax.ppermute(array, BOTH, route)

    seen_other = lax.ppermute(observations, "tm", [(t, t ^ 1) for t in range(tm_count)])
    gain_parts = [to_workers(filter_gains, turn) for turn in range(4)]
    smooth_parts = [to_workers(smooth_gains, turn) for turn in range(4)]
    cov_parts = [to_workers(filt_cov, turn) for turn in range(4)]
    seen = jnp.where(half == upper, observations, seen_other)
    seen = lax.dynamic_slice_in_dim(seen, half * steps, steps, 0)

    trans_map = dynamics * expand_mask(dynamics_mask, width, width)
    obs_map = obs_op * expand_mask(obs_mask, obs_width, width)
    obs_dyn = jnp.matmul(obs_map, trans_map, precision=highest)
    initial = initial_expectation[None, :]
    noise = process_noise[None, :]

    packed_filter = (width + PAD, width)
    packed_smooth = (2 * width + PAD, width)
    stack = (steps, width, width)
    short = (steps, width)

    total, maps, shifts = call(filter_chunk, [packed_filter, stack, short], [stack])(
        [half], *gain_parts, seen, trans_map.T, obs_dyn.T
    )
    ident = jnp.eye(width, dtype=jnp.float32)
    front = jnp.concatenate([ident, jnp.zeros((PAD, width), jnp.float32)], axis=0)
    for level in range(len(levels) - 1):
        total, front, state = call(filter_join, [packed_filter, packed_filter, (PAD, width)])(
            [levels[level][1]], total, swap(total, level), front, initial
        )
    (means,) = call(filter_last, [short])(
        [levels[-1][1]], swap(state, len(levels) - 1), initial, front, maps, shifts
    )

    final = jnp.logical_and(tm // 2 == lines - 1, jnp.logical_and(half == 1, blk == 2))
    total, maps, covs, offsets = call(smooth_chunk, [packed_smooth, stack, stack, short], [stack] * 3)(
        [half, final], *smooth_parts, *cov_parts, means, trans_map, noise
    )
    behind = jnp.concatenate([ident, jnp.zeros((width + PAD, width), jnp.float32)], axis=0)
    for level in range(len(levels) - 1):
        total, behind = call(smooth_join, [packed_smooth, packed_smooth])(
            [levels[level][1]], total, swap(total, level), behind
        )
    piece = (steps * row_count + steps, width)
    pieces = call(smooth_last, [piece] * 4, [(width + PAD, width)])(
        [levels[-1][1], half], swap(total[width:], len(levels) - 1), behind, maps, covs, offsets
    )
    arrived = [from_workers(pieces[turn], turn) for turn in range(4)]

    def pick(offset):
        chosen = arrived[0]
        for turn in range(1, 4):
            chosen = jnp.where(blk ^ offset == turn, arrived[turn], chosen)
        return chosen

    chosen = [pick(0), pick(2)]
    cov_out = jnp.concatenate(
        [part[: steps * row_count].reshape(steps, row_count, width) for part in chosen], axis=0
    )
    mean_out = jnp.concatenate([part[steps * row_count :] for part in chosen], axis=0)
    mean_out = lax.dynamic_slice_in_dim(mean_out, blk * row_count, row_count, 1)
    return mean_out, cov_out


def solution(mesh):
    return jax.shard_map(
        per_device,
        mesh=mesh,
        in_specs=(
            P(),
            P(),
            P(),
            P(),
            P(),
            P(),
            P("tm", "blk", None),
            P("tm", None),
            P("tm", "blk", None),
            P("tm", "blk", None),
        ),
        out_specs=(P("tm", "blk"), P("tm", "blk", None)),
        check_vma=False,
    )
```

time: 553 us -> 207 us (0.37)
  the two profiles are of different devices: /device:TPU:3 before, /device:TPU:0 now
where the time goes in v1:
time: 207 us; the launch traced here: 206 us
  waiting for transfers between devices  95.8 us (46%)
  starting transfers between devices  58.2 us (28%)
  Pallas kernels  30.3 us (15%)
  local copies, waits for them, and re-layouts  16.6 us (8%)
  other arithmetic  3.33 us (2%)
    ppermute x4, waiting for transfers between devices, from_workers(): return lax.ppermute(array, BOTH, route)  65.9 us
    ppermute x12, starting transfers between devices, to_workers(): lax.ppermute(lax.dynamic_slice_in_dim(array, start, steps, 0), BOTH, route)  45.6 us
    pallas_call x10, Pallas kernels, run(): pl.pallas_call(body, out_shape=[jax.ShapeDtypeStruct(shape, jnp.float32)...  30.3 us
    ppermute x12, waiting for transfers between devices, to_workers(): lax.ppermute(lax.dynamic_slice_in_dim(array, start, steps, 0), BOTH, route)  29.9 us
    unnamed x43, local copies, waits for them, and re-layouts  8.34 us
    dynamic_slice x3, local copies, waits for them, and re-layouts, to_workers(): lax.dynamic_slice_in_dim(array, start, steps, 0)  7.34 us
    ppermute x8, starting transfers between devices, swap(): return lax.ppermute(array, BOTH, route)  6.25 us
    ppermute x4, starting transfers between devices, from_workers(): return lax.ppermute(array, BOTH, route)  4.74 us
  transfers between devices with their start and end apart: 25, of which 6 were waited for; matrix products, arithmetic and copies ran while one was open for 3% of the time, Pallas kernels for 2%

profile of v1, /device:TPU:0, one launch (start us, length us, event | category | flops | bytes accessed | tf_op | source)
XLA Modules:
  0.0 206.0 jit_solution(14237991989767385116)
XLA Ops:
  0.7 3.0 %constant_dynamic-slice_fusion = (f32[8,64,256]{2,1,0:T(8,128)}, f32[8,64,256]{2,1,0:T(8,128)}, f32[8,64,256]{2,1,0:T(8,128)}, f32[8,64,256]{2,1,0:T(8,128)}) fusion(f32[16,64,256]{2,1,0:T(8,128)} %param.16, s32[]{:T(128)S(6)} %select_n.117, s32[]{:T(128)S(6)} %select_n.115, s32[]{:T(128)S(6)} %select_n.114, s32[]{:T(128)S(6)} %select_n.116), kind=kLoop, calls=%fused_computation.10 | loop fusion | bytes 4194320 | tf_op jit(solution)/shard_map/dynamic_slice | solution.py:273
  3.7 4.4 %collective-permute-start.10 = (f32[8,64,256]{2,1,0:T(8,128)}, f32[8,64,256]{2,1,0:T(8,128)S(1)}, u32[]{:S(2)}, u32[]{:S(2)}) collective-permute-start(f32[8,64,256]{2,1,0:T(8,128)} %get-tuple-element.53), channel_id=1, source_target_pairs={{2,1},{0,5},{6,2},{4,6},{10,9},{8,13},{14,10},{12,14},{18,17},{16,... | collective-permute-start | bytes 1572872 | tf_op jit(solution)/shard_map/ppermute | solution.py:273
  8.8 3.1 %collective-permute-start.8 = (f32[8,64,256]{2,1,0:T(8,128)}, f32[8,64,256]{2,1,0:T(8,128)S(1)}, u32[]{:S(2)}, u32[]{:S(2)}) collective-permute-start(f32[8,64,256]{2,1,0:T(8,128)} %get-tuple-element.52), channel_id=1, source_target_pairs={{0,1},{2,5},{4,2},{6,6},{8,9},{10,13},{12,10},{14,14},{16,17},{18,... | collective-permute-start | bytes 1572872 | tf_op jit(solution)/shard_map/ppermute | solution.py:273
  12.6 1.6 collective-permute-start.12
  15.9 4.4 %collective-permute-done.10.k2 = f32[8,64,256]{2,1,0:T(8,128)S(1)} collective-permute-done((f32[8,64,256]{2,1,0:T(8,128)}, f32[8,64,256]{2,1,0:T(8,128)S(1)}, u32[]{:S(2)}, u32[]{:S(2)}) %collective-permute-start.10) | collective-permute-done | bytes 524320 | tf_op jit(solution)/shard_map/ppermute | solution.py:273
  21.1 10.4 %collective-permute-done.8.k0 = f32[8,64,256]{2,1,0:T(8,128)S(1)} collective-permute-done((f32[8,64,256]{2,1,0:T(8,128)}, f32[8,64,256]{2,1,0:T(8,128)S(1)}, u32[]{:S(2)}, u32[]{:S(2)}) %collective-permute-start.8) | collective-permute-done | bytes 524320 | tf_op jit(solution)/shard_map/ppermute | solution.py:273
  36.2 4.3 %shard_map.113 = (f32[272,256]{1,0:T(8,128)S(1)}, f32[8,256,256]{2,1,0:T(8,128)S(1)}, f32[8,256]{1,0:T(8,128)S(1)}) custom-call(s32[1]{0:T(128)} %bitcast.1.where, f32[8,64,256]{2,1,0:T(8,128)S(1)} %copy-done.4, f32[8,64,256]{2,1,0:T(8,128)S(1)} %copy-done.6, f32[8,64,256]{2,1,0:T(8,128)S(1)} %collective-permute-done.10.k2, f32[8,64,256]{2,1,0:T(8,128)S(1)} %copy-done.2, ...), custom_call_target="tpu_custom_call" | custom-call | tf_op jit(solution)/shard_map/pallas_call | solution.py:226
  41.3 1.1 shard_map.114
  43.1 1.4 constant_dynamic-slice_fusion.8
  44.5 10.5 %collective-permute-start = (f32[8,64,256]{2,1,0:T(8,128)}, f32[8,64,256]{2,1,0:T(8,128)S(1)}, u32[]{:S(2)}, u32[]{:S(2)}) collective-permute-start(f32[8,64,256]{2,1,0:T(8,128)} %get-tuple-element.60), channel_id=1, source_target_pairs={{0,1},{2,5},{4,2},{6,6},{8,9},{10,13},{12,10},{14,14},{16,17},{18,... | collective-permute-start | bytes 1572872 | tf_op jit(solution)/shard_map/ppermute | solution.py:273
  55.7 5.5 %collective-permute-start.2 = (f32[8,64,256]{2,1,0:T(8,128)}, f32[8,64,256]{2,1,0:T(8,128)}, u32[]{:S(2)}, u32[]{:S(2)}) collective-permute-start(f32[8,64,256]{2,1,0:T(8,128)} %get-tuple-element.61), channel_id=1, source_target_pairs={{2,1},{0,5},{6,2},{4,6},{10,9},{8,13},{14,10},{12,14},{18,17},{16,... | collective-permute-start | bytes 1572872 | tf_op jit(solution)/shard_map/ppermute | solution.py:273
  63.1 1.4 collective-permute-start.15
  64.5 1.5 collective-permute-start.3
  66.9 2.1 %shard_map.116 = (f32[272,256]{1,0:T(8,128)}, f32[272,256]{1,0:T(8,128)S(1)}, f32[16,256]{1,0:T(8,128)S(1)}) custom-call(s32[1]{0:T(128)} %bitcast.2.where, f32[272,256]{1,0:T(8,128)} %get-tuple-element.28.own, f32[272,256]{1,0:T(8,128)} %collective-permute-done.15.other, f32[272,256]{1,0:T(8,128)S(1)} %copy-done.10, f32[1,256]{1,0:T(1,128)S(1)} %bitcast.22), custom_call_target="tpu_custom_call" | custom-call | tf_op jit(solution)/shard_map/pallas_call | solution.py:226
  69.7 3.0 %constant_dynamic-slice_fusion.4 = (f32[8,64,256]{2,1,0:T(8,128)}, f32[8,64,256]{2,1,0:T(8,128)}, f32[8,64,256]{2,1,0:T(8,128)}, f32[8,64,256]{2,1,0:T(8,128)}) fusion(f32[16,64,256]{2,1,0:T(8,128)} %param.19, s32[]{:T(128)S(6)} %select_n.117, s32[]{:T(128)S(6)} %select_n.115, s32[]{:T(128)S(6)} %select_n.114, s32[]{:T(128)S(6)} %select_n.116), kind=kLoop, calls=%fused_computation.14 | loop fusion | bytes 4194320 | tf_op jit(solution)/shard_map/dynamic_slice | solution.py:273
  72.7 12.4 %collective-permute-start.4 = (f32[8,64,256]{2,1,0:T(8,128)}, f32[8,64,256]{2,1,0:T(8,128)}, u32[]{:S(2)}, u32[]{:S(2)}) collective-permute-start(f32[8,64,256]{2,1,0:T(8,128)} %get-tuple-element.56), channel_id=1, source_target_pairs={{0,1},{2,5},{4,2},{6,6},{8,9},{10,13},{12,10},{14,14},{16,17},{18,... | collective-permute-start | bytes 1572872 | tf_op jit(solution)/shard_map/ppermute | solution.py:273
  85.1 1.5 collective-permute-start.5
  86.5 3.3 %collective-permute-start.6 = (f32[8,64,256]{2,1,0:T(8,128)}, f32[8,64,256]{2,1,0:T(8,128)}, u32[]{:S(2)}, u32[]{:S(2)}) collective-permute-start(f32[8,64,256]{2,1,0:T(8,128)} %get-tuple-element.57), channel_id=1, source_target_pairs={{2,1},{0,5},{6,2},{4,6},{10,9},{8,13},{14,10},{12,14},{18,17},{16,... | collective-permute-start | bytes 1572872 | tf_op jit(solution)/shard_map/ppermute | solution.py:273
  89.8 1.5 collective-permute-start.7
  93.0 3.8 %collective-permute-done.4.f0 = f32[8,64,256]{2,1,0:T(8,128)} collective-permute-done((f32[8,64,256]{2,1,0:T(8,128)}, f32[8,64,256]{2,1,0:T(8,128)}, u32[]{:S(2)}, u32[]{:S(2)}) %collective-permute-start.4) | collective-permute-done | bytes 524320 | tf_op jit(solution)/shard_map/ppermute | solution.py:273
  96.9 11.2 %collective-permute-done.6.f2 = f32[8,64,256]{2,1,0:T(8,128)} collective-permute-done((f32[8,64,256]{2,1,0:T(8,128)}, f32[8,64,256]{2,1,0:T(8,128)}, u32[]{:S(2)}, u32[]{:S(2)}) %collective-permute-start.6) | collective-permute-done | bytes 524320 | tf_op jit(solution)/shard_map/ppermute | solution.py:273
  108.1 11.0 %shard_map.118 = (f32[528,256]{1,0:T(8,128)S(1)}, f32[8,256,256]{2,1,0:T(8,128)}, f32[8,256,256]{2,1,0:T(8,128)}, f32[8,256]{1,0:T(8,128)S(1)}) custom-call(s32[2]{0:T(128)S(1)} %pad_add_fusion.1.where, f32[8,64,256]{2,1,0:T(8,128)S(1)} %collective-permute-done.g0, f32[8,64,256]{2,1,0:T(8,128)S(1)} %collective-permute-done.1.g1, ...), custom_call_target="tpu_custom_call" | custom-call | tf_op jit(solution)/shard_map/pallas_call | solution.py:226
  119.8 1.1 shard_map.119
  121.8 1.1 shard_map.120
  123.7 1.1 shard_map.121
  125.6 6.6 %shard_map.122 = (f32[520,256]{1,0:T(8,128)S(1)}, f32[520,256]{1,0:T(8,128)S(1)}, f32[520,256]{1,0:T(8,128)S(1)}, f32[520,256]{1,0:T(8,128)S(1)}) custom-call(s32[2]{0:T(128)S(1)} %pad_add_fusion.where, f32[272,256]{1,0:T(8,128)S(1)} %collective-permute-done.20.other, f32[528,256]{1,0:T(8,128)S(1)} %get-tuple-element.40.after, f32[8,256,256]{2,1,0:T(8,128)S(1)} %copy-done, ...), custom_call_target="tpu_custom_call" | custom-call | tf_op jit(solution)/shard_map/pallas_call | solution.py:226
  132.9 1.3 collective-permute-start.22
  134.2 1.5 collective-permute-start.23
  135.7 1.3 collective-permute-start.24
  137.0 63.2 %collective-permute-done.22 = f32[520,256]{1,0:T(8,128)S(1)} collective-permute-done((f32[520,256]{1,0:T(8,128)S(1)}, f32[520,256]{1,0:T(8,128)S(1)}, u32[]{:S(2)}, u32[]{:S(2)}) %collective-permute-start.22) | collective-permute-done | bytes 532512 | tf_op jit(solution)/shard_map/ppermute | solution.py:282
  200.2 2.6 %collective-permute-done.24 = f32[520,256]{1,0:T(8,128)} collective-permute-done((f32[520,256]{1,0:T(8,128)S(1)}, f32[520,256]{1,0:T(8,128)}, u32[]{:S(2)}, u32[]{:S(2)}) %collective-permute-start.24) | collective-permute-done | bytes 532512 | tf_op jit(solution)/shard_map/ppermute | solution.py:282
  202.8 1.4 select_select_fusion
  (102 shorter events, 21.3 us)
Async XLA Ops:
  0.7 11.9 %copy-start.18 = (f32[16,256]{1,0:T(8,128)S(1)}, f32[16,256]{1,0:T(8,128)}, u32[]{:S(2)}) copy-start(f32[16,256]{1,0:T(8,128)} %param.17) | copy-start | bytes 49156
  0.7 13.5 %copy-start.19 = (s32[8,8]{1,0:T(8,128)S(1)}, s32[8,8]{1,0:T(8,128)}, u32[]{:S(2)}) copy-start(s32[8,8]{1,0:T(8,128)} %param.11) | copy-start | bytes 772
  0.7 13.9 %copy-start.17 = (f32[256,256]{1,0:T(8,128)S(1)}, f32[256,256]{1,0:T(8,128)}, u32[]{:S(2)}) copy-start(f32[256,256]{1,0:T(8,128)} %param.12) | copy-start | bytes 786436
  0.7 14.0 %copy-start.20 = (s32[8,8]{1,0:T(8,128)S(1)}, s32[8,8]{1,0:T(8,128)}, u32[]{:S(2)}) copy-start(s32[8,8]{1,0:T(8,128)} %param.13) | copy-start | bytes 772
  0.7 14.3 %copy-start.16 = (f32[256,256]{1,0:T(8,128)S(1)}, f32[256,256]{1,0:T(8,128)}, u32[]{:S(2)}) copy-start(f32[256,256]{1,0:T(8,128)} %param.10) | copy-start | bytes 786436
  3.7 16.6 %collective-permute-start.10 = (f32[8,64,256]{2,1,0:T(8,128)}, f32[8,64,256]{2,1,0:T(8,128)S(1)}, u32[]{:S(2)}, u32[]{:S(2)}) collective-permute-start(f32[8,64,256]{2,1,0:T(8,128)} %get-tuple-element.53), channel_id=1, source_target_pairs={{2,1},{0,5},{6,2},{4,6},{10,9},{8,13},{14,10},{12,14},{18,17},{16,... | collective-permute-start | bytes 1572872 | tf_op jit(solution)/shard_map/ppermute | solution.py:273
  8.1 12.2 %collective-permute-start.11 = (f32[8,64,256]{2,1,0:T(8,128)}, f32[8,64,256]{2,1,0:T(8,128)S(1)}, u32[]{:S(2)}, u32[]{:S(2)}) collective-permute-start(f32[8,64,256]{2,1,0:T(8,128)} %get-tuple-element.50), channel_id=1, source_target_pairs={{3,1},{1,5},{7,2},{5,6},{11,9},{9,13},{15,10},{13,14},{19,17},{17,... | collective-permute-start | bytes 1572872 | tf_op jit(solution)/shard_map/ppermute | solution.py:273
  8.8 22.8 %collective-permute-start.8 = (f32[8,64,256]{2,1,0:T(8,128)}, f32[8,64,256]{2,1,0:T(8,128)S(1)}, u32[]{:S(2)}, u32[]{:S(2)}) collective-permute-start(f32[8,64,256]{2,1,0:T(8,128)} %get-tuple-element.52), channel_id=1, source_target_pairs={{0,1},{2,5},{4,2},{6,6},{8,9},{10,13},{12,10},{14,14},{16,17},{18,... | collective-permute-start | bytes 1572872 | tf_op jit(solution)/shard_map/ppermute | solution.py:273
  11.8 20.5 %collective-permute-start.9 = (f32[8,64,256]{2,1,0:T(8,128)}, f32[8,64,256]{2,1,0:T(8,128)S(1)}, u32[]{:S(2)}, u32[]{:S(2)}) collective-permute-start(f32[8,64,256]{2,1,0:T(8,128)} %get-tuple-element.51), channel_id=1, source_target_pairs={{1,1},{3,5},{5,2},{7,6},{9,9},{11,13},{13,10},{15,14},{17,17},{19,... | collective-permute-start | bytes 1572872 | tf_op jit(solution)/shard_map/ppermute | solution.py:273
  12.6 3.3 %collective-permute-start.12 = (f32[16,256]{1,0:T(8,128)S(1)}, f32[16,256]{1,0:T(8,128)S(1)}, u32[]{:S(2)}, u32[]{:S(2)}) collective-permute-start(f32[16,256]{1,0:T(8,128)S(1)} %copy-done.18), channel_id=1, source_target_pairs={{0,4},{4,0},{8,12},{12,8},{16,20},{20,16},{24,28},{28,24},{1,5},{5... | collective-permute-start | bytes 49160 | tf_op jit(solution)/shard_map/ppermute | solution.py:296
  15.7 25.6 %copy-start.11 = (f32[256]{0:T(256)S(1)}, f32[256]{0:T(256)}, u32[]{:S(2)}) copy-start(f32[256]{0:T(256)} %param.15) | copy-start | bytes 3076
  40.5 0.7 collective-permute-start.13
  42.4 18.8 %collective-permute-start.14 = (f32[272,256]{1,0:T(8,128)S(1)}, f32[272,256]{1,0:T(8,128)S(1)}, u32[]{:S(2)}, u32[]{:S(2)}) collective-permute-start(f32[272,256]{1,0:T(8,128)S(1)} %get-tuple-element.26.own), channel_id=1, source_target_pairs={{1,2},{2,1},{5,6},{6,5},{9,10},{10,9},{13,14},{14,13},{17,18},{18,... | collective-permute-start | bytes 835592 | tf_op jit(solution)/shard_map/ppermute | solution.py:294
  44.5 28.2 %collective-permute-start = (f32[8,64,256]{2,1,0:T(8,128)}, f32[8,64,256]{2,1,0:T(8,128)S(1)}, u32[]{:S(2)}, u32[]{:S(2)}) collective-permute-start(f32[8,64,256]{2,1,0:T(8,128)} %get-tuple-element.60), channel_id=1, source_target_pairs={{0,1},{2,5},{4,2},{6,6},{8,9},{10,13},{12,10},{14,14},{16,17},{18,... | collective-permute-start | bytes 1572872 | tf_op jit(solution)/shard_map/ppermute | solution.py:273
  55.0 30.0 %collective-permute-start.1 = (f32[8,64,256]{2,1,0:T(8,128)}, f32[8,64,256]{2,1,0:T(8,128)S(1)}, u32[]{:S(2)}, u32[]{:S(2)}) collective-permute-start(f32[8,64,256]{2,1,0:T(8,128)} %get-tuple-element.59), channel_id=1, source_target_pairs={{1,1},{3,5},{5,2},{7,6},{9,9},{11,13},{13,10},{15,14},{17,17},{19,... | collective-permute-start | bytes 1572872 | tf_op jit(solution)/shard_map/ppermute | solution.py:273
  55.7 30.8 %collective-permute-start.2 = (f32[8,64,256]{2,1,0:T(8,128)}, f32[8,64,256]{2,1,0:T(8,128)}, u32[]{:S(2)}, u32[]{:S(2)}) collective-permute-start(f32[8,64,256]{2,1,0:T(8,128)} %get-tuple-element.61), channel_id=1, source_target_pairs={{2,1},{0,5},{6,2},{4,6},{10,9},{8,13},{14,10},{12,14},{18,17},{16,... | collective-permute-start | bytes 1572872 | tf_op jit(solution)/shard_map/ppermute | solution.py:273
  63.1 2.8 %collective-permute-start.15 = (f32[272,256]{1,0:T(8,128)}, f32[272,256]{1,0:T(8,128)}, u32[]{:S(2)}, u32[]{:S(2)}) collective-permute-start(f32[272,256]{1,0:T(8,128)} %get-tuple-element.28.own), channel_id=1, source_target_pairs={{1,9},{2,10},{5,13},{6,14},{9,1},{10,2},{13,5},{14,6},{17,25},{18,... | collective-permute-start | bytes 835592 | tf_op jit(solution)/shard_map/ppermute | solution.py:294
  64.5 28.6 %collective-permute-start.3 = (f32[8,64,256]{2,1,0:T(8,128)}, f32[8,64,256]{2,1,0:T(8,128)}, u32[]{:S(2)}, u32[]{:S(2)}) collective-permute-start(f32[8,64,256]{2,1,0:T(8,128)} %get-tuple-element.58), channel_id=1, source_target_pairs={{3,1},{1,5},{7,2},{5,6},{11,9},{9,13},{15,10},{13,14},{19,17},{17,... | collective-permute-start | bytes 1572872 | tf_op jit(solution)/shard_map/ppermute | solution.py:273
  69.0 20.8 %collective-permute-start.16 = (f32[16,256]{1,0:T(8,128)S(1)}, f32[16,256]{1,0:T(8,128)S(1)}, u32[]{:S(2)}, u32[]{:S(2)}) collective-permute-start(f32[16,256]{1,0:T(8,128)S(1)} %get-tuple-element.30), channel_id=1, source_target_pairs={{1,17},{2,18},{5,21},{6,22},{9,25},{10,26},{13,29},{14,30},{17,1},... | collective-permute-start | bytes 49160 | tf_op jit(solution)/shard_map/ppermute | solution.py:294
  72.7 35.4 %copy-start.12 = (f32[256]{0:T(256)S(1)}, f32[256]{0:T(256)}, u32[]{:S(2)}) copy-start(f32[256]{0:T(256)} %param.14) | copy-start | bytes 3076
  72.7 24.2 %collective-permute-start.4 = (f32[8,64,256]{2,1,0:T(8,128)}, f32[8,64,256]{2,1,0:T(8,128)}, u32[]{:S(2)}, u32[]{:S(2)}) collective-permute-start(f32[8,64,256]{2,1,0:T(8,128)} %get-tuple-element.56), channel_id=1, source_target_pairs={{0,1},{2,5},{4,2},{6,6},{8,9},{10,13},{12,10},{14,14},{16,17},{18,... | collective-permute-start | bytes 1572872 | tf_op jit(solution)/shard_map/ppermute | solution.py:273
  85.1 11.8 %collective-permute-start.5 = (f32[8,64,256]{2,1,0:T(8,128)}, f32[8,64,256]{2,1,0:T(8,128)}, u32[]{:S(2)}, u32[]{:S(2)}) collective-permute-start(f32[8,64,256]{2,1,0:T(8,128)} %get-tuple-element.55), channel_id=1, source_target_pairs={{1,1},{3,5},{5,2},{7,6},{9,9},{11,13},{13,10},{15,14},{17,17},{19,... | collective-permute-start | bytes 1572872 | tf_op jit(solution)/shard_map/ppermute | solution.py:273
  86.5 21.6 %collective-permute-start.6 = (f32[8,64,256]{2,1,0:T(8,128)}, f32[8,64,256]{2,1,0:T(8,128)}, u32[]{:S(2)}, u32[]{:S(2)}) collective-permute-start(f32[8,64,256]{2,1,0:T(8,128)} %get-tuple-element.57), channel_id=1, source_target_pairs={{2,1},{0,5},{6,2},{4,6},{10,9},{8,13},{14,10},{12,14},{18,17},{16,... | collective-permute-start | bytes 1572872 | tf_op jit(solution)/shard_map/ppermute | solution.py:273
  89.8 18.3 %collective-permute-start.7 = (f32[8,64,256]{2,1,0:T(8,128)}, f32[8,64,256]{2,1,0:T(8,128)}, u32[]{:S(2)}, u32[]{:S(2)}) collective-permute-start(f32[8,64,256]{2,1,0:T(8,128)} %get-tuple-element.54), channel_id=1, source_target_pairs={{3,1},{1,5},{7,2},{5,6},{11,9},{9,13},{15,10},{13,14},{19,17},{17,... | collective-permute-start | bytes 1572872 | tf_op jit(solution)/shard_map/ppermute | solution.py:273
  119.1 0.7 collective-permute-start.17
  121.0 0.8 collective-permute-start.18
  123.0 0.7 collective-permute-start.19
  124.8 0.8 collective-permute-start.20
  132.2 4.8 %collective-permute-start.21 = (f32[520,256]{1,0:T(8,128)S(1)}, f32[520,256]{1,0:T(8,128)S(1)}, u32[]{:S(2)}, u32[]{:S(2)}) collective-permute-start(f32[520,256]{1,0:T(8,128)S(1)} %get-tuple-element.44), channel_id=1, source_target_pairs={{1,3},{5,1},{2,7},{6,5},{9,11},{13,9},{10,15},{14,13},{17,19},{21,... | collective-permute-start | bytes 1597448 | tf_op jit(solution)/shard_map/ppermute | solution.py:282
  132.9 67.3 %collective-permute-start.22 = (f32[520,256]{1,0:T(8,128)S(1)}, f32[520,256]{1,0:T(8,128)S(1)}, u32[]{:S(2)}, u32[]{:S(2)}) collective-permute-start(f32[520,256]{1,0:T(8,128)S(1)} %get-tuple-element.45), channel_id=1, source_target_pairs={{1,2},{5,0},{2,6},{6,4},{9,10},{13,8},{10,14},{14,12},{17,18},{21,... | collective-permute-start | bytes 1597448 | tf_op jit(solution)/shard_map/ppermute | solution.py:282
  134.2 66.0 %collective-permute-start.23 = (f32[520,256]{1,0:T(8,128)S(1)}, f32[520,256]{1,0:T(8,128)}, u32[]{:S(2)}, u32[]{:S(2)}) collective-permute-start(f32[520,256]{1,0:T(8,128)S(1)} %get-tuple-element.46), channel_id=1, source_target_pairs={{1,1},{5,3},{2,5},{6,7},{9,9},{13,11},{10,13},{14,15},{17,17},{21,... | collective-permute-start | bytes 1597448 | tf_op jit(solution)/shard_map/ppermute | solution.py:282
  135.7 67.2 %collective-permute-start.24 = (f32[520,256]{1,0:T(8,128)S(1)}, f32[520,256]{1,0:T(8,128)}, u32[]{:S(2)}, u32[]{:S(2)}) collective-permute-start(f32[520,256]{1,0:T(8,128)S(1)} %get-tuple-element.47), channel_id=1, source_target_pairs={{1,0},{5,2},{2,4},{6,6},{9,8},{13,10},{10,12},{14,14},{17,16},{21,... | collective-permute-start | bytes 1597448 | tf_op jit(solution)/shard_map/ppermute | solution.py:282
  (14 other events, 38.2 us)

commit v2 on v1

v2 whole, which is shorter than its diff:
```python
import functools
import math

import jax
import jax.numpy as jnp
from jax import lax
from jax.experimental import pallas as pl
from jax.experimental.pallas import tpu as pltpu
from jax.sharding import PartitionSpec as P

highest = lax.Precision.HIGHEST
BOTH = ("tm", "blk")
PAD = 16
SPARE = 6 * 1024 * 1024


def halves(x):
    top = x.astype(jnp.bfloat16)
    return top, (x - top.astype(jnp.float32)).astype(jnp.bfloat16)


def product(left, right, dims):
    def one(a, b):
        return lax.dot_general(a, b, (dims, ((), ())), preferred_element_type=jnp.float32)

    rows = left[0].shape[0]
    both = one(jnp.concatenate(left, axis=0), right[0])
    return both[:rows] + (both[rows:] + one(left[0], right[1]))


def mm(left, right):
    return product(halves(left), halves(right), ((1,), (0,)))


def mm_nt(left, right):
    return product(halves(left), halves(right), ((1,), (1,)))


def under(above, below):
    return tuple(jnp.concatenate([a, b], axis=0) for a, b in zip(above, below))


def rows_of(vec):
    return jnp.broadcast_to(vec, (PAD, vec.shape[-1]))


def expand_mask(mask, row_total, col_total):
    row_block = row_total // mask.shape[0]
    col_block = col_total // mask.shape[1]
    return jnp.repeat(jnp.repeat(mask.astype(jnp.float32), row_block, axis=0), col_block, axis=1)


def fill_rows(target, pieces, half):
    rows = pieces[0].shape[1]
    for turn, piece in enumerate(pieces):
        source = jnp.where(half == 0, turn, turn ^ 2)
        target[:, pl.ds(pl.multiple_of(source * rows, rows), rows), :] = piece[...]


def filter_chunk(where, k0, k1, k2, k3, seen, trans_t, dyn_t, packed, maps, shifts, gains):
    width = trans_t.shape[0]
    steps = k0.shape[0]
    fill_rows(gains, (k0, k1, k2, k3), where[0])
    dyn_parts = halves(dyn_t[...])
    running = [None, None]
    for step in range(steps // 2):
        for part in range(2):
            spot = step + part * (steps // 2)
            gain = halves(gains[spot])
            seen_rows = halves(rows_of(seen[spot : spot + 1, :]))
            turned = product(under(dyn_parts, seen_rows), gain, ((1,), (1,)))
            shift = turned[width:]
            turned = trans_t[...] - turned[:width]
            if step == 0:
                running[part] = (turned, shift)
            else:
                running[part] = filter_follow(*running[part], turned, shift)
            maps[spot] = running[part][0]
            shifts[spot : spot + 1, :] = running[part][1][0:1]
    packed[:width], packed[width:] = filter_follow(*running[0], *running[1])


def filter_follow(early_map, early_shift, late_map, late_shift):
    width = late_map.shape[0]
    moved = product(
        under(halves(early_map), halves(early_shift)), halves(late_map), ((1,), (0,))
    )
    return moved[:width], moved[width:] + late_shift


def filter_join(where, own, other, initial, *rest):
    total, state = rest[-2:]
    width = own.shape[1]

    def follow(early, latter):
        total[:width], total[width:] = filter_follow(
            early[:width], early[width:], latter[:width], latter[width:]
        )

    @pl.when(where[0] == 0)
    def _():
        follow(own, other)

    @pl.when(where[0] != 0)
    def _():
        follow(other, own)

    state[...] = mm(rows_of(initial[...]), total[:width]) + total[width:]


def filter_front(where, other, before, front):
    width = before.shape[1]

    @pl.when(where[0] == 0)
    def _():
        front[...] = before[...]

    @pl.when(where[0] != 0)
    def _():
        front[:width], front[width:] = filter_follow(
            other[:width], other[width:], before[:width], before[width:]
        )


def filter_reach(where, state, initial, before, own, reached, onward):
    width = before.shape[1]
    started = jnp.where(where[0] == 0, rows_of(initial[...]), state[...])
    reached[...] = mm(started, before[:width]) + before[width:]
    onward[...] = mm(reached[...], own[:width]) + own[width:]


def filter_last(where, reached, onward, maps, shifts, means):
    steps = maps.shape[0]
    middle = steps // 2
    incoming = jnp.where(where[0] == 0, reached[...], onward[...])
    between = mm(incoming, maps[middle - 1]) + shifts[middle - 1 : middle, :]
    starts = (halves(incoming), halves(between))
    for step in range(steps):
        moved = product(starts[step // middle], halves(maps[step]), ((1,), (0,)))
        means[step : step + 1, :] = moved[0:1] + shifts[step : step + 1, :]


def smooth_chunk(
    where, g0, g1, g2, g3, f0, f1, f2, f3, means, trans, noise, packed, maps, covs, offsets, gains, filt, pred
):
    width = trans.shape[0]
    steps = g0.shape[0]
    middle = steps // 2
    fill_rows(gains, (g0, g1, g2, g3), where[0])
    fill_rows(filt, (f0, f1, f2, f3), where[0])
    gains[steps - 1] = jnp.where(where[1] != 0, 0.0, gains[steps - 1])
    trans_parts = halves(trans[...])
    row_no = lax.broadcasted_iota(jnp.int32, (width, width), 0)
    col_no = lax.broadcasted_iota(jnp.int32, (width, width), 1)
    noise_mat = jnp.where(row_no == col_no, noise[...], 0.0)
    moved_means = mm_nt(jnp.concatenate([means[...]] * (PAD // steps), axis=0), trans[...])
    for step in range(steps):
        moved = halves(product(trans_parts, halves(filt[step]), ((1,), (0,))))
        pred[step] = product(moved, trans_parts, ((1,), (1,))) + noise_mat
    state = [None, None]
    for step in reversed(range(middle)):
        for part in range(2):
            spot = step + part * middle
            gain = halves(gains[spot])
            own_mean = rows_of(means[spot : spot + 1, :])
            moved_mean = rows_of(moved_means[spot : spot + 1, :])
            if state[part] is None:
                gap, mean_gap, chain = -pred[spot], -moved_mean, gains[spot]
            else:
                cov, mean, chain = state[part]
                gap, mean_gap = cov - pred[spot], mean - moved_mean
                chain = product(gain, halves(chain), ((1,), (0,)))
            gap = halves(product(gain, halves(gap), ((1,), (0,))))
            moved = product(under(gap, halves(mean_gap)), gain, ((1,), (1,)))
            cov = filt[spot] + moved[:width]
            mean = own_mean + moved[width:]
            state[part] = (cov, mean, chain)
            maps[spot] = chain
            covs[spot] = cov
            offsets[spot : spot + 1, :] = mean[0:1]
    (early_cov, early_mean, early_chain), (cov, mean, chain) = state
    gain = halves(early_chain)
    packed[:width] = product(gain, halves(chain), ((1,), (0,)))
    packed[width : 2 * width], packed[2 * width :] = carry_parts(gain, early_cov, early_mean, cov, mean)


def carry_parts(gain, early_cov, early_mean, cov, mean):
    width = cov.shape[0]
    moved = halves(product(gain, halves(cov), ((1,), (0,))))
    moved = product(under(moved, halves(mean)), gain, ((1,), (1,)))
    return early_cov + moved[:width], early_mean + moved[width:]


def carry(gain, early, latter):
    width = early.shape[1]
    moved = halves(product(gain, halves(latter[:width]), ((1,), (0,))))
    return early + product(under(moved, halves(latter[width:])), gain, ((1,), (1,)))


def smooth_follow(early, latter, target):
    width = early.shape[1]
    gain = halves(early[:width])
    target[:width] = product(gain, halves(latter[:width]), ((1,), (0,)))
    target[width:] = carry(gain, early[width:], latter[width:])


def smooth_join(where, own, other, total):
    @pl.when(where[0] == 0)
    def _():
        smooth_follow(own, other, total)

    @pl.when(where[0] != 0)
    def _():
        smooth_follow(other, own, total)


def smooth_behind(where, other, after, behind):
    @pl.when(where[0] == 0)
    def _():
        smooth_follow(after, other, behind)

    @pl.when(where[0] != 0)
    def _():
        behind[...] = after[...]


def smooth_reach(where, other, after, reached):
    width = after.shape[1]

    @pl.when(where[0] == 0)
    def _():
        reached[...] = carry(halves(after[:width]), after[width:], other[...])

    @pl.when(where[0] != 0)
    def _():
        reached[...] = after[width:]


def smooth_last(where, own, other, next_total, maps, covs, offsets, p0, p1, p2, p3, start):
    width = maps.shape[1]
    steps = maps.shape[0]
    middle = steps // 2
    rows = width // 4
    half = where[0]

    @pl.when(half == 0)
    def _():
        start[...] = carry(halves(next_total[:width]), next_total[width:], own[...])

    @pl.when(half != 0)
    def _():
        start[...] = other[...]

    late = (start[:width], start[width:])
    early = carry_parts(
        halves(maps[middle]), covs[middle], rows_of(offsets[middle : middle + 1, :]), *late
    )
    starts = [(halves(cov), halves(mean)) for cov, mean in (early, late)]
    pieces = (p0, p1, p2, p3)
    mean_rows = [None] * steps
    for step in reversed(range(steps)):
        gain = halves(maps[step])
        begun, begun_mean = starts[step // middle]
        moved = halves(product(gain, begun, ((1,), (0,))))
        moved = product(under(moved, begun_mean), gain, ((1,), (1,)))
        cov = covs[step] + moved[:width]
        mean_rows[step] = moved[width : width + 1] + offsets[step : step + 1, :]
        for turn, piece in enumerate(pieces):
            swapped = turn ^ 2
            piece[step * rows : step * rows + rows] = jnp.where(
                half == 0,
                cov[rows * turn : rows * turn + rows],
                cov[rows * swapped : rows * swapped + rows],
            )
    all_means = jnp.concatenate(mean_rows, axis=0)
    for piece in pieces:
        piece[steps * rows :] = all_means


def share_halves(where, whole, *rest):
    first, second, sems = rest[-3:]
    steps = first.shape[0]
    flip = where[0]
    copies = [
        pltpu.make_async_copy(whole.at[pl.ds(flip * steps, steps)], first, sems.at[0]),
        pltpu.make_async_copy(whole.at[pl.ds((1 - flip) * steps, steps)], second, sems.at[1]),
    ]
    for copy in copies:
        copy.start()
    for copy in copies:
        copy.wait()


def place_halves(where, a0, a1, a2, a3, mean, cov, seen, sems):
    blk = where[0]
    rows = cov.shape[0] // 2
    short = mean.shape[0] // 2
    wide = mean.shape[1]
    parts = (a0, a1, a2, a3)
    for turn in range(4):

        @pl.when(blk == turn)
        def _(turn=turn):
            copies = []
            for part in range(2):
                source = parts[turn ^ (2 * part)]
                copies.append(
                    pltpu.make_async_copy(
                        source.at[pl.ds(rows, short)], seen.at[pl.ds(part * short, short)], sems.at[part]
                    )
                )
                copies.append(
                    pltpu.make_async_copy(
                        source.at[pl.ds(0, rows)], cov.at[pl.ds(part * rows, rows)], sems.at[2 + part]
                    )
                )
            for copy in copies:
                copy.start()
            for copy in copies:
                copy.wait()
            mean[...] = seen[:, wide * turn : wide * turn + wide]


def call(body, outs, scratch=(), sems=(), far=(), far_outs=()):
    def space(flag):
        return pl.BlockSpec(memory_space=pl.ANY if flag else pltpu.VMEM)

    def run(where, *operands):
        count = len(operands)
        held = [outs[n] for n in range(len(outs)) if n not in far_outs] + list(scratch)
        held += [op.shape for n, op in enumerate(operands) if n not in far and n - count not in far]
        grant = 4 * sum(math.prod(shape) for shape in held) + SPARE
        return pl.pallas_call(
            body,
            out_shape=[jax.ShapeDtypeStruct(shape, jnp.float32) for shape in outs],
            in_specs=[pl.BlockSpec(memory_space=pltpu.SMEM)]
            + [space(n in far or n - count in far) for n in range(count)],
            out_specs=[space(n in far_outs) for n in range(len(outs))],
            scratch_shapes=[pltpu.VMEM(shape, jnp.float32) for shape in scratch]
            + ([pltpu.SemaphoreType.DMA(sems)] if sems else []),
            compiler_params=pltpu.CompilerParams(vmem_limit_bytes=grant),
        )(jnp.stack([jnp.int32(w) for w in where]), *operands)

    return run


def per_device(
    dynamics,
    dynamics_mask,
    obs_op,
    obs_mask,
    process_noise,
    initial_expectation,
    filter_gains,
    observations,
    smooth_gains,
    filt_cov,
):
    width = dynamics.shape[0]
    obs_width = obs_op.shape[0]
    step_count, row_count = filter_gains.shape[:2]
    steps = step_count // 2
    tm, blk = lax.axis_index("tm"), lax.axis_index("blk")
    tm_count, blk_count = lax.axis_size("tm"), lax.axis_size("blk")
    lines = tm_count // 2
    half = tm % 2
    worker = jnp.logical_or(blk == 1, blk == 2)
    upper = jnp.int32(blk == 2)

    def place(t, z):
        return t * blk_count + z

    def to_workers(array, *after):
        shape = (steps,) + array.shape[1:]
        shares = call(
            share_halves, [shape] * 2, sems=(2,), far=range(1 + len(after)), far_outs=range(2)
        )([jnp.int32(blk >= 2)], array, *after)
        arrived = []
        for turn in range(4):
            route = [
                (place(2 * line + core, turn ^ (2 * part)), place(2 * line + part, 1 + core))
                for line in range(lines)
                for core in range(2)
                for part in range(2)
            ]
            arrived.append(lax.ppermute(shares[turn // 2], BOTH, route))
        return arrived

    def from_workers(array, turn):
        route = [
            (place(2 * line + part, 1 + core), place(2 * line + core, turn ^ (2 * part)))
            for line in range(lines)
            for core in range(2)
            for part in range(2)
        ]
        return lax.ppermute(array, BOTH, route)

    levels = [(lambda t, z: (t ^ 1, z), half), (lambda t, z: (t, 3 - z), upper)]
    distance = 2
    while distance < tm_count:
        levels.append((functools.partial(lambda d, t, z: (t ^ d, z), distance), (tm // distance) % 2))
        distance *= 2

    def swap(array, level, cores=(0, 1)):
        route = [
            (place(t, z), place(*levels[level][0](t, z)))
            for t in range(tm_count)
            for z in (1, 2)
            if t % 2 in cores
        ]
        return lax.ppermute(array, BOTH, route)

    seen_other = lax.ppermute(observations, "tm", [(t, t ^ 1) for t in range(tm_count)])
    gain_parts = to_workers(filter_gains)
    smooth_parts = to_workers(smooth_gains)
    seen = jnp.where(half == upper, observations, seen_other)
    seen = lax.dynamic_slice_in_dim(seen, half * steps, steps, 0)

    trans_map = dynamics * expand_mask(dynamics_mask, width, width)
    obs_map = obs_op * expand_mask(obs_mask, obs_width, width)
    obs_dyn = jnp.matmul(obs_map, trans_map, precision=highest)
    initial = initial_expectation[None, :]
    noise = process_noise[None, :]

    packed_filter = (width + PAD, width)
    packed_smooth = (2 * width + PAD, width)
    stack = (steps, width, width)
    short = (steps, width)

    chunk, maps, shifts = call(filter_chunk, [packed_filter, stack, short], [stack])(
        [half], *gain_parts, seen, trans_map.T, obs_dyn.T
    )
    ident = jnp.eye(width, dtype=jnp.float32)
    front = jnp.concatenate([ident, jnp.zeros((PAD, width), jnp.float32)], axis=0)
    total, arrived = chunk, swap(chunk, 0, (1,))
    for level in range(len(levels) - 1):
        late = levels[level][1] if level else 0
        after = (smooth_parts[:2], smooth_parts[2:])[level] if level < 2 else []
        total, state = call(
            filter_join, [packed_filter, (PAD, width)], far=range(-len(after), 0)
        )([late], total, arrived, initial, *after)
        if level:
            (front,) = call(filter_front, [packed_filter])([late], arrived, front)
        else:
            cov_parts = to_workers(filt_cov, state)
        if level < len(levels) - 2:
            arrived = swap(total, level + 1, (0,))
    reached, onward = call(filter_reach, [(PAD, width)] * 2)(
        [levels[-1][1]], swap(state, len(levels) - 1, (0,)), initial, front, chunk
    )
    (means,) = call(filter_last, [short])(
        [half], reached, swap(onward, 0, (0,)), maps, shifts
    )

    final = jnp.logical_and(tm // 2 == lines - 1, jnp.logical_and(half == 1, blk == 2))
    total, maps, covs, offsets = call(
        smooth_chunk, [packed_smooth, stack, stack, short], [stack] * 3
    )([half, final], *smooth_parts, *cov_parts, means, trans_map, noise)
    behind = jnp.concatenate([ident, jnp.zeros((width + PAD, width), jnp.float32)], axis=0)
    next_total = swap(total, 0, (1,))
    (total,) = call(smooth_join, [packed_smooth])([0], total, next_total)
    for level in range(1, len(levels) - 1):
        arrived = swap(total, level, (0,))
        late = levels[level][1]
        (total,) = call(smooth_join, [packed_smooth])([late], total, arrived)
        (behind,) = call(smooth_behind, [packed_smooth])([late], arrived, behind)
    arrived = swap(total[width:], len(levels) - 1, (0,))
    (reached,) = call(smooth_reach, [packed_filter])([levels[-1][1]], arrived, behind)
    piece = (steps * row_count + steps, width)
    pieces = call(smooth_last, [piece] * 4, [packed_filter])(
        [half], reached, swap(reached, 0, (0,)), next_total, maps, covs, offsets
    )
    arrived = [from_workers(pieces[turn], turn) for turn in range(4)]

    mean_out, cov_out = call(
        place_halves,
        [(step_count, row_count), (step_count * row_count, width)],
        [(step_count, width)],
        sems=(4,),
        far=range(4),
        far_outs=[1],
    )([blk], *arrived)
    return mean_out, cov_out.reshape(step_count, row_count, width)


def solution(mesh):
    return jax.shard_map(
        per_device,
        mesh=mesh,
        in_specs=(
            P(),
            P(),
            P(),
            P(),
            P(),
            P(),
            P("tm", "blk", None),
            P("tm", None),
            P("tm", "blk", None),
            P("tm", "blk", None),
        ),
        out_specs=(P("tm", "blk"), P("tm", "blk", None)),
        check_vma=False,
    )
```

time: 207 us -> 175 us (0.85)
  waiting for transfers between devices: 95.8 us -> 78.7 us
  starting transfers between devices: 58.2 us -> 48.5 us
  local copies, waits for them, and re-layouts: 16.6 us -> 12.8 us
    ppermute x12, waiting for transfers between devices: 29.9 us -> 11.7 us  [to_workers(): arrived.append(lax.ppermute(shares[turn // 2], BOTH, route))]
    ppermute x12, starting transfers between devices: 45.6 us -> 36.8 us  [to_workers(): arrived.append(lax.ppermute(shares[turn // 2], BOTH, route))]
    dynamic_slice x3 -> x0, local copies, waits for them, and re-layouts: 7.34 us -> none  [to_workers(): lax.dynamic_slice_in_dim(array, start, steps, 0)]
    ppermute x8 -> x10, starting transfers between devices: 6.25 us -> 7.79 us  [swap(): return lax.ppermute(array, BOTH, route)]
    unnamed x43 -> x53, local copies, waits for them, and re-layouts: 8.34 us -> 9.67 us
    pallas_call x10 -> x20, Pallas kernels: 30.3 us -> 29.9 us  [run(): pl.pallas_call(body, out_shape=[jax.ShapeDtypeStruct(shape, jnp.float32)...]
  transfers between devices with their start and end apart: 25 -> 27, of which waited for: 6 -> 5; matrix products, arithmetic and copies ran while one was open for 3% -> 3% of each run, Pallas kernels for 2% -> 8%
where the time goes in v2:
time: 175 us; the launch traced here: 174 us
  waiting for transfers between devices  78.7 us (45%)
  starting transfers between devices  48.5 us (28%)
  Pallas kernels  29.9 us (17%)
  local copies, waits for them, and re-layouts  12.8 us (7%)
    ppermute x4, waiting for transfers between devices, from_workers(): return lax.ppermute(array, BOTH, route)  67 us
    ppermute x12, starting transfers between devices, to_workers(): arrived.append(lax.ppermute(shares[turn // 2], BOTH, route))  36.8 us
    pallas_call x20, Pallas kernels, run(): pl.pallas_call(body, out_shape=[jax.ShapeDtypeStruct(shape, jnp.float32)...  29.9 us
    ppermute x12, waiting for transfers between devices, to_workers(): arrived.append(lax.ppermute(shares[turn // 2], BOTH, route))  11.7 us
    unnamed x53, local copies, waits for them, and re-layouts  9.67 us
    ppermute x10, starting transfers between devices, swap(): return lax.ppermute(array, BOTH, route)  7.79 us
    ppermute x4, starting transfers between devices, from_workers(): return lax.ppermute(array, BOTH, route)  3.97 us
  transfers between devices with their start and end apart: 27, of which 5 were waited for; matrix products, arithmetic and copies ran while one was open for 3% of the time, Pallas kernels for 8%

profile of v2, /device:TPU:0, one launch (start us, length us, event | category | flops | bytes accessed | tf_op | source)
XLA Modules:
  0.0 173.6 jit_solution(14765837249939153370)
XLA Ops:
  0.7 1.2 copy-done.10
  1.9 1.0 shard_map.114
  2.9 5.0 %collective-permute-start.4 = (f32[8,64,256]{2,1,0:T(8,128)}, f32[8,64,256]{2,1,0:T(8,128)S(1)}, u32[]{:S(2)}, u32[]{:S(2)}) collective-permute-start(f32[8,64,256]{2,1,0:T(8,128)} %get-tuple-element.29), channel_id=1, source_target_pairs={{0,1},{2,5},{4,2},{6,6},{8,9},{10,13},{12,10},{14,14},{16,17},{18,... | collective-permute-start | bytes 1572872 | tf_op jit(solution)/shard_map/ppermute | solution.py:386
  8.6 5.2 %collective-permute-start.6 = (f32[8,64,256]{2,1,0:T(8,128)}, f32[8,64,256]{2,1,0:T(8,128)}, u32[]{:S(2)}, u32[]{:S(2)}) collective-permute-start(f32[8,64,256]{2,1,0:T(8,128)} %get-tuple-element.30), channel_id=1, source_target_pairs={{2,1},{0,5},{6,2},{4,6},{10,9},{8,13},{14,10},{12,14},{18,17},{16,... | collective-permute-start | bytes 1572872 | tf_op jit(solution)/shard_map/ppermute | solution.py:386
  13.8 1.5 collective-permute-start.7
  19.3 1.7 collective-permute-start
  23.1 8.2 %collective-permute-done.6.k2 = f32[8,64,256]{2,1,0:T(8,128)} collective-permute-done((f32[8,64,256]{2,1,0:T(8,128)}, f32[8,64,256]{2,1,0:T(8,128)}, u32[]{:S(2)}, u32[]{:S(2)}) %collective-permute-start.6) | collective-permute-done | bytes 524320 | tf_op jit(solution)/shard_map/ppermute | solution.py:386
  31.3 0.9 copy-done.9
  32.3 1.0 copy-done.14
  33.3 1.0 copy-done.16
  34.4 4.3 %shard_map.115 = (f32[272,256]{1,0:T(8,128)S(1)}, f32[8,256,256]{2,1,0:T(8,128)S(1)}, f32[8,256]{1,0:T(8,128)S(1)}) custom-call(s32[1]{0:T(128)} %bitcast.1.where, f32[8,64,256]{2,1,0:T(8,128)S(1)} %copy-done.14, f32[8,64,256]{2,1,0:T(8,128)S(1)} %copy-done.16, f32[8,64,256]{2,1,0:T(8,128)} %collective-permute-done.6.k2, ...), custom_call_target="tpu_custom_call" | custom-call | tf_op jit(solution)/shard_map/pallas_call | solution.py:333
  39.4 7.8 %collective-permute-start.2 = (f32[8,64,256]{2,1,0:T(8,128)S(1)}, f32[8,64,256]{2,1,0:T(8,128)S(1)}, u32[]{:S(2)}, u32[]{:S(2)}) collective-permute-start(f32[8,64,256]{2,1,0:T(8,128)S(1)} %copy-done.20), channel_id=1, source_target_pairs={{2,1},{0,5},{6,2},{4,6},{10,9},{8,13},{14,10},{12,14},{18,17},{16,... | collective-permute-start | bytes 1572872 | tf_op jit(solution)/shard_map/ppermute | solution.py:386
  49.0 1.1 shard_map.117
  50.1 5.8 %collective-permute-start.10 = (f32[8,64,256]{2,1,0:T(8,128)}, f32[8,64,256]{2,1,0:T(8,128)}, u32[]{:S(2)}, u32[]{:S(2)}) collective-permute-start(f32[8,64,256]{2,1,0:T(8,128)} %get-tuple-element.33), channel_id=1, source_target_pairs={{0,1},{2,5},{4,2},{6,6},{8,9},{10,13},{12,10},{14,14},{16,17},{18,... | collective-permute-start | bytes 1572872 | tf_op jit(solution)/shard_map/ppermute | solution.py:386
  55.9 1.5 collective-permute-start.11
  57.4 2.0 %collective-permute-done.2.rest_0_.g2 = f32[8,64,256]{2,1,0:T(8,128)S(1)} collective-permute-done((f32[8,64,256]{2,1,0:T(8,128)S(1)}, f32[8,64,256]{2,1,0:T(8,128)S(1)}, u32[]{:S(2)}, u32[]{:S(2)}) %collective-permute-start.2) | collective-permute-done | bytes 524320 | tf_op jit(solution)/shard_map/ppermute | solution.py:386
  59.4 4.9 %collective-permute-start.12 = (f32[8,64,256]{2,1,0:T(8,128)}, f32[8,64,256]{2,1,0:T(8,128)}, u32[]{:S(2)}, u32[]{:S(2)}) collective-permute-start(f32[8,64,256]{2,1,0:T(8,128)} %get-tuple-element.34), channel_id=1, source_target_pairs={{2,1},{0,5},{6,2},{4,6},{10,9},{8,13},{14,10},{12,14},{18,17},{16,... | collective-permute-start | bytes 1572872 | tf_op jit(solution)/shard_map/ppermute | solution.py:386
  64.3 1.5 collective-permute-start.13
  65.8 1.1 shard_map.118
  67.6 1.4 collective-permute-start.15
  69.0 2.1 %shard_map.119 = (f32[272,256]{1,0:T(8,128)}, f32[16,256]{1,0:T(8,128)S(1)}) custom-call(s32[1]{0:T(128)} %bitcast.3.where, f32[272,256]{1,0:T(8,128)} %get-tuple-element.36.own, f32[272,256]{1,0:T(8,128)} %collective-permute-done.15.other, f32[1,256]{1,0:T(1,128)S(1)} %bitcast.23), custom_call_target="tpu_custom_call" | custom-call | tf_op jit(solution)/shard_map/pallas_call | solution.py:333
  72.4 1.7 concatenate.6.before
  74.2 1.0 copy-done.5
  75.1 1.0 copy-done.8
  76.1 1.1 shard_map.121.before
  79.9 1.4 collective-permute-done.12.f2
  81.3 7.9 %shard_map.124 = (f32[528,256]{1,0:T(8,128)S(1)}, f32[8,256,256]{2,1,0:T(8,128)S(1)}, f32[8,256,256]{2,1,0:T(8,128)S(1)}, f32[8,256]{1,0:T(8,128)S(1)}) custom-call(s32[2]{0:T(128)S(1)} %pad_add_fusion.where, f32[8,64,256]{2,1,0:T(8,128)S(1)} %collective-permute-done.rest_0_.g0, f32[8,64,256]{2,1,0:T(8,128)S(1)} %collective-permute-done.1.rest_1_.g1, ...), custom_call_target="tpu_custom_call" | custom-call | tf_op jit(solution)/shard_map/pallas_call | solution.py:333
  97.4 3.4 %shard_map.131 = (f32[520,256]{1,0:T(8,128)S(1)}, f32[520,256]{1,0:T(8,128)S(1)}, f32[520,256]{1,0:T(8,128)S(1)}, f32[520,256]{1,0:T(8,128)S(1)}) custom-call(s32[1]{0:T(128)} %bitcast.1.where, f32[272,256]{1,0:T(8,128)S(1)} %shard_map.130.own, f32[272,256]{1,0:T(8,128)S(1)} %collective-permute-done.22.other, ...), custom_call_target="tpu_custom_call" | custom-call | tf_op jit(solution)/shard_map/pallas_call | solution.py:333
  100.9 1.3 collective-permute-start.23
  102.9 1.3 collective-permute-start.25
  104.9 66.8 %collective-permute-done.23.a0 = f32[520,256]{1,0:T(8,128)S(1)} collective-permute-done((f32[520,256]{1,0:T(8,128)S(1)}, f32[520,256]{1,0:T(8,128)S(1)}, u32[]{:S(2)}, u32[]{:S(2)}) %collective-permute-start.23) | collective-permute-done | bytes 532512 | tf_op jit(solution)/shard_map/ppermute | solution.py:396
  171.8 1.6 shard_map.132
  (115 shorter events, 23.7 us)
Async XLA Ops:
  0.6 15.9 %copy-start.25 = (s32[8,8]{1,0:T(8,128)S(1)}, s32[8,8]{1,0:T(8,128)}, u32[]{:S(2)}) copy-start(s32[8,8]{1,0:T(8,128)} %param.13) | copy-start | bytes 772
  1.9 15.7 %copy-start.11 = (f32[16,64,256]{2,1,0:T(8,128)S(1)}, f32[16,64,256]{2,1,0:T(8,128)}, u32[]{:S(2)}) copy-start(f32[16,64,256]{2,1,0:T(8,128)} %whole.3) | copy-start | bytes 3145732
  2.9 18.0 %collective-permute-start.4 = (f32[8,64,256]{2,1,0:T(8,128)}, f32[8,64,256]{2,1,0:T(8,128)S(1)}, u32[]{:S(2)}, u32[]{:S(2)}) collective-permute-start(f32[8,64,256]{2,1,0:T(8,128)} %get-tuple-element.29), channel_id=1, source_target_pairs={{0,1},{2,5},{4,2},{6,6},{8,9},{10,13},{12,10},{14,14},{16,17},{18,... | collective-permute-start | bytes 1572872 | tf_op jit(solution)/shard_map/ppermute | solution.py:386
  7.9 14.4 %collective-permute-start.5 = (f32[8,64,256]{2,1,0:T(8,128)}, f32[8,64,256]{2,1,0:T(8,128)S(1)}, u32[]{:S(2)}, u32[]{:S(2)}) collective-permute-start(f32[8,64,256]{2,1,0:T(8,128)} %get-tuple-element.29), channel_id=1, source_target_pairs={{1,1},{3,5},{5,2},{7,6},{9,9},{11,13},{13,10},{15,14},{17,17},{19,... | collective-permute-start | bytes 1572872 | tf_op jit(solution)/shard_map/ppermute | solution.py:386
  8.6 22.8 %collective-permute-start.6 = (f32[8,64,256]{2,1,0:T(8,128)}, f32[8,64,256]{2,1,0:T(8,128)}, u32[]{:S(2)}, u32[]{:S(2)}) collective-permute-start(f32[8,64,256]{2,1,0:T(8,128)} %get-tuple-element.30), channel_id=1, source_target_pairs={{2,1},{0,5},{6,2},{4,6},{10,9},{8,13},{14,10},{12,14},{18,17},{16,... | collective-permute-start | bytes 1572872 | tf_op jit(solution)/shard_map/ppermute | solution.py:386
  13.8 17.5 %collective-permute-start.7 = (f32[8,64,256]{2,1,0:T(8,128)}, f32[8,64,256]{2,1,0:T(8,128)}, u32[]{:S(2)}, u32[]{:S(2)}) collective-permute-start(f32[8,64,256]{2,1,0:T(8,128)} %get-tuple-element.30), channel_id=1, source_target_pairs={{3,1},{1,5},{7,2},{5,6},{11,9},{9,13},{15,10},{13,14},{19,17},{17,... | collective-permute-start | bytes 1572872 | tf_op jit(solution)/shard_map/ppermute | solution.py:386
  15.3 4.0 %collective-permute-start.8 = (f32[16,256]{1,0:T(8,128)}, f32[16,256]{1,0:T(8,128)S(1)}, u32[]{:S(2)}, u32[]{:S(2)}) collective-permute-start(f32[16,256]{1,0:T(8,128)} %param.17), channel_id=1, source_target_pairs={{0,4},{4,0},{8,12},{12,8},{16,20},{20,16},{24,28},{28,24},{1,5},{5... | collective-permute-start | bytes 49160 | tf_op jit(solution)/shard_map/ppermute | solution.py:413
  19.2 28.7 %copy-start.17 = (f32[256]{0:T(256)S(1)}, f32[256]{0:T(256)}, u32[]{:S(2)}) copy-start(f32[256]{0:T(256)} %param.15) | copy-start | bytes 3076
  19.2 20.1 %copy-start.20 = (f32[8,64,256]{2,1,0:T(8,128)S(1)}, f32[8,64,256]{2,1,0:T(8,128)}, u32[]{:S(2)}) copy-start(f32[8,64,256]{2,1,0:T(8,128)} %copy-done.19) | copy-start | bytes 1572868
  19.3 28.6 %collective-permute-start = (f32[8,64,256]{2,1,0:T(8,128)}, f32[8,64,256]{2,1,0:T(8,128)S(1)}, u32[]{:S(2)}, u32[]{:S(2)}) collective-permute-start(f32[8,64,256]{2,1,0:T(8,128)} %get-tuple-element.27), channel_id=1, source_target_pairs={{0,1},{2,5},{4,2},{6,6},{8,9},{10,13},{12,10},{14,14},{16,17},{18,... | collective-permute-start | bytes 1572872 | tf_op jit(solution)/shard_map/ppermute | solution.py:386
  21.0 26.9 %collective-permute-start.1 = (f32[8,64,256]{2,1,0:T(8,128)}, f32[8,64,256]{2,1,0:T(8,128)S(1)}, u32[]{:S(2)}, u32[]{:S(2)}) collective-permute-start(f32[8,64,256]{2,1,0:T(8,128)} %get-tuple-element.27), channel_id=1, source_target_pairs={{1,1},{3,5},{5,2},{7,6},{9,9},{11,13},{13,10},{15,14},{17,17},{19,... | collective-permute-start | bytes 1572872 | tf_op jit(solution)/shard_map/ppermute | solution.py:386
  38.7 28.1 %copy-start.6 = (f32[272,256]{1,0:T(8,128)}, f32[272,256]{1,0:T(8,128)S(1)}, u32[]{:S(2)}) copy-start(f32[272,256]{1,0:T(8,128)S(1)} %get-tuple-element.31.own) | copy-start | bytes 835588
  38.7 9.2 %collective-permute-start.9 = (f32[272,256]{1,0:T(8,128)S(1)}, f32[272,256]{1,0:T(8,128)S(1)}, u32[]{:S(2)}, u32[]{:S(2)}) collective-permute-start(f32[272,256]{1,0:T(8,128)S(1)} %get-tuple-element.31.own), channel_id=1, source_target_pairs={{5,1},{6,2},{13,9},{14,10},{21,17},{22,18},{29,25},{30,26}} | collective-permute-start | bytes 835592 | tf_op jit(solution)/shard_map/ppermute | solution.py:411
  39.4 20.0 %collective-permute-start.2 = (f32[8,64,256]{2,1,0:T(8,128)S(1)}, f32[8,64,256]{2,1,0:T(8,128)S(1)}, u32[]{:S(2)}, u32[]{:S(2)}) collective-permute-start(f32[8,64,256]{2,1,0:T(8,128)S(1)} %copy-done.20), channel_id=1, source_target_pairs={{2,1},{0,5},{6,2},{4,6},{10,9},{8,13},{14,10},{12,14},{18,17},{16,... | collective-permute-start | bytes 1572872 | tf_op jit(solution)/shard_map/ppermute | solution.py:386
  47.2 17.1 %collective-permute-start.3 = (f32[8,64,256]{2,1,0:T(8,128)S(1)}, f32[8,64,256]{2,1,0:T(8,128)S(1)}, u32[]{:S(2)}, u32[]{:S(2)}) collective-permute-start(f32[8,64,256]{2,1,0:T(8,128)S(1)} %copy-done.20), channel_id=1, source_target_pairs={{3,1},{1,5},{7,2},{5,6},{11,9},{9,13},{15,10},{13,14},{19,17},{17,... | collective-permute-start | bytes 1572872 | tf_op jit(solution)/shard_map/ppermute | solution.py:386
  48.3 17.4 %collective-permute-start.14 = (f32[272,256]{1,0:T(8,128)S(1)}, f32[272,256]{1,0:T(8,128)S(1)}, u32[]{:S(2)}, u32[]{:S(2)}) collective-permute-start(f32[272,256]{1,0:T(8,128)S(1)} %get-tuple-element.35.own), channel_id=1, source_target_pairs={{1,2},{2,1},{9,10},{10,9},{17,18},{18,17},{25,26},{26,25}} | collective-permute-start | bytes 835592 | tf_op jit(solution)/shard_map/ppermute | solution.py:411
  50.1 29.7 %collective-permute-start.10 = (f32[8,64,256]{2,1,0:T(8,128)}, f32[8,64,256]{2,1,0:T(8,128)}, u32[]{:S(2)}, u32[]{:S(2)}) collective-permute-start(f32[8,64,256]{2,1,0:T(8,128)} %get-tuple-element.33), channel_id=1, source_target_pairs={{0,1},{2,5},{4,2},{6,6},{8,9},{10,13},{12,10},{14,14},{16,17},{18,... | collective-permute-start | bytes 1572872 | tf_op jit(solution)/shard_map/ppermute | solution.py:386
  55.9 23.9 %collective-permute-start.11 = (f32[8,64,256]{2,1,0:T(8,128)}, f32[8,64,256]{2,1,0:T(8,128)}, u32[]{:S(2)}, u32[]{:S(2)}) collective-permute-start(f32[8,64,256]{2,1,0:T(8,128)} %get-tuple-element.33), channel_id=1, source_target_pairs={{1,1},{3,5},{5,2},{7,6},{9,9},{11,13},{13,10},{15,14},{17,17},{19,... | collective-permute-start | bytes 1572872 | tf_op jit(solution)/shard_map/ppermute | solution.py:386
  59.4 21.9 %collective-permute-start.12 = (f32[8,64,256]{2,1,0:T(8,128)}, f32[8,64,256]{2,1,0:T(8,128)}, u32[]{:S(2)}, u32[]{:S(2)}) collective-permute-start(f32[8,64,256]{2,1,0:T(8,128)} %get-tuple-element.34), channel_id=1, source_target_pairs={{2,1},{0,5},{6,2},{4,6},{10,9},{8,13},{14,10},{12,14},{18,17},{16,... | collective-permute-start | bytes 1572872 | tf_op jit(solution)/shard_map/ppermute | solution.py:386
  64.3 17.0 %collective-permute-start.13 = (f32[8,64,256]{2,1,0:T(8,128)}, f32[8,64,256]{2,1,0:T(8,128)}, u32[]{:S(2)}, u32[]{:S(2)}) collective-permute-start(f32[8,64,256]{2,1,0:T(8,128)} %get-tuple-element.34), channel_id=1, source_target_pairs={{3,1},{1,5},{7,2},{5,6},{11,9},{9,13},{15,10},{13,14},{19,17},{17,... | collective-permute-start | bytes 1572872 | tf_op jit(solution)/shard_map/ppermute | solution.py:386
  67.6 1.4 collective-permute-start.15
  71.1 6.1 %collective-permute-start.16 = (f32[16,256]{1,0:T(8,128)S(1)}, f32[16,256]{1,0:T(8,128)S(1)}, u32[]{:S(2)}, u32[]{:S(2)}) collective-permute-start(f32[16,256]{1,0:T(8,128)S(1)} %get-tuple-element.37), channel_id=1, source_target_pairs={{1,17},{2,18},{9,25},{10,26},{17,1},{18,2},{25,9},{26,10}} | collective-permute-start | bytes 49160 | tf_op jit(solution)/shard_map/ppermute | solution.py:411
  78.5 0.9 collective-permute-start.17
  89.2 0.7 collective-permute-start.18
  90.7 0.8 collective-permute-start.19
  92.3 0.7 collective-permute-start.20
  93.8 2.3 %collective-permute-start.21 = (f32[272,256]{1,0:T(8,128)S(1)}, f32[272,256]{1,0:T(8,128)S(1)}, u32[]{:S(2)}, u32[]{:S(2)}) collective-permute-start(f32[272,256]{1,0:T(8,128)S(1)} %slice.4), channel_id=1, source_target_pairs={{1,17},{2,18},{9,25},{10,26},{17,1},{18,2},{25,9},{26,10}} | collective-permute-start | bytes 835592 | tf_op jit(solution)/shard_map/ppermute | solution.py:411
  96.7 0.7 collective-permute-start.22
  100.9 70.8 %collective-permute-start.23 = (f32[520,256]{1,0:T(8,128)S(1)}, f32[520,256]{1,0:T(8,128)S(1)}, u32[]{:S(2)}, u32[]{:S(2)}) collective-permute-start(f32[520,256]{1,0:T(8,128)S(1)} %get-tuple-element.46), channel_id=1, source_target_pairs={{1,0},{5,2},{2,4},{6,6},{9,8},{13,10},{10,12},{14,14},{17,16},{21,... | collective-permute-start | bytes 1597448 | tf_op jit(solution)/shard_map/ppermute | solution.py:396
  102.2 69.5 %collective-permute-start.24 = (f32[520,256]{1,0:T(8,128)S(1)}, f32[520,256]{1,0:T(8,128)S(1)}, u32[]{:S(2)}, u32[]{:S(2)}) collective-permute-start(f32[520,256]{1,0:T(8,128)S(1)} %get-tuple-element.47), channel_id=1, source_target_pairs={{1,1},{5,3},{2,5},{6,7},{9,9},{13,11},{10,13},{14,15},{17,17},{21,... | collective-permute-start | bytes 1597448 | tf_op jit(solution)/shard_map/ppermute | solution.py:396
  102.9 69.0 %collective-permute-start.25 = (f32[520,256]{1,0:T(8,128)S(1)}, f32[520,256]{1,0:T(8,128)S(1)}, u32[]{:S(2)}, u32[]{:S(2)}) collective-permute-start(f32[520,256]{1,0:T(8,128)S(1)} %get-tuple-element.48), channel_id=1, source_target_pairs={{1,2},{5,0},{2,6},{6,4},{9,10},{13,8},{10,14},{14,12},{17,18},{21,... | collective-permute-start | bytes 1597448 | tf_op jit(solution)/shard_map/ppermute | solution.py:396
  104.2 67.7 %collective-permute-start.26 = (f32[520,256]{1,0:T(8,128)S(1)}, f32[520,256]{1,0:T(8,128)S(1)}, u32[]{:S(2)}, u32[]{:S(2)}) collective-permute-start(f32[520,256]{1,0:T(8,128)S(1)} %get-tuple-element.49), channel_id=1, source_target_pairs={{1,3},{5,1},{2,7},{6,5},{9,11},{13,9},{10,15},{14,13},{17,19},{21,... | collective-permute-start | bytes 1597448 | tf_op jit(solution)/shard_map/ppermute | solution.py:396
  (21 other events, 93.7 us)

commit v3 on v2

--- a/solution.py
+++ b/solution.py
@@ -11,7 +11,8 @@
 highest = lax.Precision.HIGHEST
 BOTH = ("tm", "blk")
 PAD = 16
-SPARE = 6 * 1024 * 1024
+CUTS = 4
+SPARE = 4 * 1024 * 1024
 
 
 def halves(x):
@@ -50,23 +51,22 @@
     return jnp.repeat(jnp.repeat(mask.astype(jnp.float32), row_block, axis=0), col_block, axis=1)
 
 
-def fill_rows(target, pieces, half):
-    rows = pieces[0].shape[1]
-    for turn, piece in enumerate(pieces):
-        source = jnp.where(half == 0, turn, turn ^ 2)
-        target[:, pl.ds(pl.multiple_of(source * rows, rows), rows), :] = piece[...]
-
-
-def filter_chunk(where, k0, k1, k2, k3, seen, trans_t, dyn_t, packed, maps, shifts, gains):
+def whole(pieces, step, half, latter=0):
+    parts = [piece[step + latter * (piece.shape[0] - pieces[0].shape[0])] for piece in pieces]
+    straight = jnp.concatenate(parts, axis=0)
+    return jnp.where(half == 0, straight, jnp.concatenate(parts[2:] + parts[:2], axis=0))
+
+
+def filter_chunk(where, k0, k1, k2, k3, seen, trans_t, dyn_t, *rest):
+    packed, maps, shifts = rest[-3:]
     width = trans_t.shape[0]
     steps = k0.shape[0]
-    fill_rows(gains, (k0, k1, k2, k3), where[0])
     dyn_parts = halves(dyn_t[...])
     running = [None, None]
     for step in range(steps // 2):
         for part in range(2):
             spot = step + part * (steps // 2)
-            gain = halves(gains[spot])
+            gain = halves(whole((k0, k1, k2, k3), spot, where[0]))
             seen_rows = halves(rows_of(seen[spot : spot + 1, :]))
             turned = product(under(dyn_parts, seen_rows), gain, ((1,), (1,)))
             shift = turned[width:]
@@ -108,25 +108,15 @@
     state[...] = mm(rows_of(initial[...]), total[:width]) + total[width:]
 
 
-def filter_front(where, other, before, front):
-    width = before.shape[1]
-
-    @pl.when(where[0] == 0)
-    def _():
-        front[...] = before[...]
-
-    @pl.when(where[0] != 0)
-    def _():
-        front[:width], front[width:] = filter_follow(
-            other[:width], other[width:], before[:width], before[width:]
-        )
-
-
-def filter_reach(where, state, initial, before, own, reached, onward):
-    width = before.shape[1]
-    started = jnp.where(where[0] == 0, rows_of(initial[...]), state[...])
-    reached[...] = mm(started, before[:width]) + before[width:]
-    onward[...] = mm(reached[...], own[:width]) + own[width:]
+def filter_reach(where, state, initial, own, *rest):
+    reached, onward = rest[-2:]
+    width = own.shape[1]
+    current = jnp.where(where[0] == 0, rows_of(initial[...]), state[...])
+    for n, other in enumerate(rest[:-2]):
+        moved = mm(current, other[:width]) + other[width:]
+        current = jnp.where(where[1 + n] == 0, current, moved)
+    reached[...] = current
+    onward[...] = mm(current, own[:width]) + own[width:]
 
 
 def filter_last(where, reached, onward, maps, shifts, means):
@@ -140,48 +130,79 @@
         means[step : step + 1, :] = moved[0:1] + shifts[step : step + 1, :]
 
 
-def smooth_chunk(
-    where, g0, g1, g2, g3, f0, f1, f2, f3, means, trans, noise, packed, maps, covs, offsets, gains, filt, pred
-):
+def predict(where, f0, f1, f2, f3, trans, noise, after, filt, pred):
     width = trans.shape[0]
-    steps = g0.shape[0]
-    middle = steps // 2
-    fill_rows(gains, (g0, g1, g2, g3), where[0])
-    fill_rows(filt, (f0, f1, f2, f3), where[0])
-    gains[steps - 1] = jnp.where(where[1] != 0, 0.0, gains[steps - 1])
+    steps = f0.shape[0]
     trans_parts = halves(trans[...])
     row_no = lax.broadcasted_iota(jnp.int32, (width, width), 0)
     col_no = lax.broadcasted_iota(jnp.int32, (width, width), 1)
     noise_mat = jnp.where(row_no == col_no, noise[...], 0.0)
-    moved_means = mm_nt(jnp.concatenate([means[...]] * (PAD // steps), axis=0), trans[...])
     for step in range(steps):
-        moved = halves(product(trans_parts, halves(filt[step]), ((1,), (0,))))
+        now = whole((f0, f1, f2, f3), step, where[0])
+        filt[step] = now
+        moved = halves(product(trans_parts, halves(now), ((1,), (0,))))
         pred[step] = product(moved, trans_parts, ((1,), (1,))) + noise_mat
+
+
+def smooth_chunk(where, g0, g1, g2, g3, filt, pred, after, packed, maps, covs):
+    width = filt.shape[1]
+    steps = g0.shape[0]
+    middle = steps // 2
     state = [None, None]
     for step in reversed(range(middle)):
         for part in range(2):
             spot = step + part * middle
-            gain = halves(gains[spot])
-            own_mean = rows_of(means[spot : spot + 1, :])
-            moved_mean = rows_of(moved_means[spot : spot + 1, :])
+            gain_now = whole((g0, g1, g2, g3), spot, where[0], 1)
+            if spot == steps - 1:
+                gain_now = jnp.where(where[1] != 0, 0.0, gain_now)
+            gain = halves(gain_now)
             if state[part] is None:
-                gap, mean_gap, chain = -pred[spot], -moved_mean, gains[spot]
+                gap, chain = -pred[spot], gain_now
             else:
-                cov, mean, chain = state[part]
-                gap, mean_gap = cov - pred[spot], mean - moved_mean
+                cov, chain = state[part]
+                gap = cov - pred[spot]
                 chain = product(gain, halves(chain), ((1,), (0,)))
             gap = halves(product(gain, halves(gap), ((1,), (0,))))
-            moved = product(under(gap, halves(mean_gap)), gain, ((1,), (1,)))
-            cov = filt[spot] + moved[:width]
-            mean = own_mean + moved[width:]
-            state[part] = (cov, mean, chain)
+            cov = filt[spot] + product(gap, gain, ((1,), (1,)))
+            state[part] = (cov, chain)
             maps[spot] = chain
             covs[spot] = cov
-            offsets[spot : spot + 1, :] = mean[0:1]
-    (early_cov, early_mean, early_chain), (cov, mean, chain) = state
+    (early_cov, early_chain), (cov, chain) = state
     gain = halves(early_chain)
     packed[:width] = product(gain, halves(chain), ((1,), (0,)))
-    packed[width : 2 * width], packed[2 * width :] = carry_parts(gain, early_cov, early_mean, cov, mean)
+    moved = halves(product(gain, halves(cov), ((1,), (0,))))
+    packed[width:] = early_cov + product(moved, gain, ((1,), (1,)))
+
+
+def smooth_offsets(where, g0, g1, g2, g3, means, trans, maps, offsets, delta):
+    steps = g0.shape[0]
+    middle = steps // 2
+    moved_means = mm_nt(jnp.concatenate([means[...]] * (PAD // steps), axis=0), trans[...])
+    state = [None, None]
+    for step in reversed(range(middle)):
+        for part in range(2):
+            spot = step + part * middle
+            gain_now = whole((g0, g1, g2, g3), spot, where[0], 1)
+            if spot == steps - 1:
+                gain_now = jnp.where(where[1] != 0, 0.0, gain_now)
+            gap = -rows_of(moved_means[spot : spot + 1, :])
+            if state[part] is not None:
+                gap = state[part] + gap
+            state[part] = rows_of(means[spot : spot + 1, :]) + mm_nt(gap, gain_now)
+            offsets[spot : spot + 1, :] = state[part][0:1]
+    delta[...] = state[0] + mm_nt(state[1], maps[0])
+
+
+def smooth_join_cov(where, own, other, total):
+    width = own.shape[1]
+    gain = halves(own[:width])
+    total[:width] = product(gain, halves(other[:width]), ((1,), (0,)))
+    moved = halves(product(gain, halves(other[width:]), ((1,), (0,))))
+    total[width:] = own[width:] + product(moved, gain, ((1,), (1,)))
+
+
+def smooth_join_delta(where, own, delta, other, total):
+    total[...] = delta[...] + mm_nt(other[...], own[: own.shape[1]])
 
 
 def carry_parts(gain, early_cov, early_mean, cov, mean):
@@ -277,18 +298,20 @@
         piece[steps * rows :] = all_means
 
 
-def share_halves(where, whole, *rest):
-    first, second, sems = rest[-3:]
-    steps = first.shape[0]
-    flip = where[0]
-    copies = [
-        pltpu.make_async_copy(whole.at[pl.ds(flip * steps, steps)], first, sems.at[0]),
-        pltpu.make_async_copy(whole.at[pl.ds((1 - flip) * steps, steps)], second, sems.at[1]),
-    ]
-    for copy in copies:
-        copy.start()
-    for copy in copies:
-        copy.wait()
+def share_half(where, *refs):
+    share = refs[-1]
+    wholes = refs[:-1]
+    steps = wholes[0].shape[0] // 2
+
+    @pl.when(where[0] == 0)
+    def _():
+        for n in range(share.shape[0] // steps):
+            share[n * steps : n * steps + steps] = wholes[n][:steps]
+
+    @pl.when(where[0] != 0)
+    def _():
+        for n in range(share.shape[0] // steps):
+            share[n * steps : n * steps + steps] = wholes[n][steps:]
 
 
 def place_halves(where, a0, a1, a2, a3, mean, cov, seen, sems):
@@ -297,6 +320,7 @@
     short = mean.shape[0] // 2
     wide = mean.shape[1]
     parts = (a0, a1, a2, a3)
+    cut = rows // CUTS
     for turn in range(4):
 
         @pl.when(blk == turn)
@@ -304,32 +328,27 @@
             copies = []
             for part in range(2):
                 source = parts[turn ^ (2 * part)]
-                copies.append(
-                    pltpu.make_async_copy(
-                        source.at[pl.ds(rows, short)], seen.at[pl.ds(part * short, short)], sems.at[part]
-                    )
-                )
-                copies.append(
-                    pltpu.make_async_copy(
-                        source.at[pl.ds(0, rows)], cov.at[pl.ds(part * rows, rows)], sems.at[2 + part]
-                    )
-                )
-            for copy in copies:
-                copy.start()
+                pairs = [(source.at[pl.ds(rows, short)], seen.at[pl.ds(part * short, short)])]
+                for n in range(CUTS):
+                    spot = pl.ds(part * rows + n * cut, cut)
+                    pairs.append((source.at[pl.ds(n * cut, cut)], cov.at[spot]))
+                for n, pair in enumerate(pairs):
+                    copies.append(pltpu.make_async_copy(*pair, sems.at[part, n]))
+                    copies[-1].start()
             for copy in copies:
                 copy.wait()
             mean[...] = seen[:, wide * turn : wide * turn + wide]
 
 
-def call(body, outs, scratch=(), sems=(), far=(), far_outs=()):
+def call(body, outs, scratch=(), sems=(), far=(), far_outs=(), alias=(), grant=None):
     def space(flag):
         return pl.BlockSpec(memory_space=pl.ANY if flag else pltpu.VMEM)
 
     def run(where, *operands):
         count = len(operands)
-        held = [outs[n] for n in range(len(outs)) if n not in far_outs] + list(scratch)
+        held = [outs[n] for n in range(len(outs)) if n not in far_outs and n not in [b for _, b in alias]] + list(scratch)
         held += [op.shape for n, op in enumerate(operands) if n not in far and n - count not in far]
-        grant = 4 * sum(math.prod(shape) for shape in held) + SPARE
+        limit = grant or 4 * sum(math.prod(shape) for shape in held) + SPARE
         return pl.pallas_call(
             body,
             out_shape=[jax.ShapeDtypeStruct(shape, jnp.float32) for shape in outs],
@@ -338,7 +357,8 @@
             out_specs=[space(n in far_outs) for n in range(len(outs))],
             scratch_shapes=[pltpu.VMEM(shape, jnp.float32) for shape in scratch]
             + ([pltpu.SemaphoreType.DMA(sems)] if sems else []),
-            compiler_params=pltpu.CompilerParams(vmem_limit_bytes=grant),
+            input_output_aliases={1 + a: b for a, b in alias},
+            compiler_params=pltpu.CompilerParams(vmem_limit_bytes=limit),
         )(jnp.stack([jnp.int32(w) for w in where]), *operands)
 
     return run
@@ -370,21 +390,19 @@
     def place(t, z):
         return t * blk_count + z
 
-    def to_workers(array, *after):
-        shape = (steps,) + array.shape[1:]
-        shares = call(
-            share_halves, [shape] * 2, sems=(2,), far=range(1 + len(after)), far_outs=range(2)
-        )([jnp.int32(blk >= 2)], array, *after)
-        arrived = []
-        for turn in range(4):
-            route = [
-                (place(2 * line + core, turn ^ (2 * part)), place(2 * line + part, 1 + core))
-                for line in range(lines)
-                for core in range(2)
-                for part in range(2)
-            ]
-            arrived.append(lax.ppermute(shares[turn // 2], BOTH, route))
-        return arrived
+    def share(arrays, latter):
+        flip = jnp.int32((blk >= 2) != latter)
+        shape = (steps * len(arrays),) + arrays[0].shape[1:]
+        return call(share_half, [shape])([flip], *arrays)[0]
+
+    def to_workers(array, turn):
+        pairs = [
+            (place(2 * line + core, turn ^ (2 * part)), place(2 * line + part, 1 + core))
+            for line in range(lines)
+            for core in range(2)
+            for part in range(2)
+        ]
+        return lax.ppermute(array, BOTH, pairs)
 
     def from_workers(array, turn):
         route = [
@@ -411,8 +429,11 @@
         return lax.ppermute(array, BOTH, route)
 
     seen_other = lax.ppermute(observations, "tm", [(t, t ^ 1) for t in range(tm_count)])
-    gain_parts = to_workers(filter_gains)
-    smooth_parts = to_workers(smooth_gains)
+    gain_shares = [share([filter_gains], latter) for latter in (False, True)]
+    gain_parts = [to_workers(gain_shares[turn // 2], turn) for turn in range(4)]
+    cov_shares = [share([filt_cov], latter) for latter in (False, True)]
+    cov_parts = [to_workers(cov_shares[turn // 2], turn) for turn in range(4)]
+    late_shares = [share([smooth_gains], latter) for latter in (False, True)]
     seen = jnp.where(half == upper, observations, seen_other)
     seen = lax.dynamic_slice_in_dim(seen, half * steps, steps, 0)
 
@@ -427,43 +448,62 @@
     stack = (steps, width, width)
     short = (steps, width)
 
-    chunk, maps, shifts = call(filter_chunk, [packed_filter, stack, short], [stack])(
-        [half], *gain_parts, seen, trans_map.T, obs_dyn.T
-    )
-    ident = jnp.eye(width, dtype=jnp.float32)
-    front = jnp.concatenate([ident, jnp.zeros((PAD, width), jnp.float32)], axis=0)
-    total, arrived = chunk, swap(chunk, 0, (1,))
+    chunk, maps, shifts = call(filter_chunk, [packed_filter, stack, short], far=[-2, -1])(
+        [half], *gain_parts, seen, trans_map.T, obs_dyn.T, *late_shares
+    )
+    total, arrived, others = chunk, swap(chunk, 0, (1,)), []
     for level in range(len(levels) - 1):
-        late = levels[level][1] if level else 0
-        after = (smooth_parts[:2], smooth_parts[2:])[level] if level < 2 else []
+        after = (cov_parts[:2], cov_parts[2:])[level] if level < 2 else []
         total, state = call(
             filter_join, [packed_filter, (PAD, width)], far=range(-len(after), 0)
-        )([late], total, arrived, initial, *after)
+        )([levels[level][1] if level else 0], total, arrived, initial, *after)
+        if level == 1:
+            filt, pred = call(predict, [stack] * 2, far=[-1])(
+                [half], *cov_parts, trans_map, noise, state
+            )
         if level:
-            (front,) = call(filter_front, [packed_filter])([late], arrived, front)
+            others.insert(0, (levels[level][1], arrived))
         else:
-            cov_parts = to_workers(filt_cov, state)
+            *late_shares, total = lax.optimization_barrier((*late_shares, total))
+            smooth_parts = [to_workers(late_shares[turn // 2], turn) for turn in range(4)]
         if level < len(levels) - 2:
             arrived = swap(total, level + 1, (0,))
     reached, onward = call(filter_reach, [(PAD, width)] * 2)(
-        [levels[-1][1]], swap(state, len(levels) - 1, (0,)), initial, front, chunk
+        [levels[-1][1]] + [late for late, _ in others],
+        swap(state, len(levels) - 1, (0,)),
+        initial,
+        chunk,
+        *[arrived for _, arrived in others],
     )
     (means,) = call(filter_last, [short])(
         [half], reached, swap(onward, 0, (0,)), maps, shifts
     )
 
     final = jnp.logical_and(tm // 2 == lines - 1, jnp.logical_and(half == 1, blk == 2))
-    total, maps, covs, offsets = call(
-        smooth_chunk, [packed_smooth, stack, stack, short], [stack] * 3
-    )([half, final], *smooth_parts, *cov_parts, means, trans_map, noise)
-    behind = jnp.concatenate([ident, jnp.zeros((width + PAD, width), jnp.float32)], axis=0)
-    next_total = swap(total, 0, (1,))
-    (total,) = call(smooth_join, [packed_smooth])([0], total, next_total)
+    plain = (2 * width, width)
+    first, maps, covs = call(smooth_chunk, [plain, stack, stack], alias=[(5, 1), (4, 2)], far=[-1])(
+        [half, final], *smooth_parts, filt, pred, means
+    )
+    offsets, delta = call(smooth_offsets, [short, (PAD, width)])(
+        [half, final], *smooth_parts, means, trans_map, maps
+    )
+    next_cov = swap(first, 0, (1,))
+    (total,) = call(smooth_join_cov, [plain])([0], first, next_cov)
+    next_delta = swap(delta, 0, (1,))
+    (delta,) = call(smooth_join_delta, [(PAD, width)])([0], first, delta, next_delta)
+    behind = None
     for level in range(1, len(levels) - 1):
         arrived = swap(total, level, (0,))
+        if behind is None:
+            arrived = jnp.concatenate([arrived, swap(delta, level, (0,))], axis=0)
+            total = jnp.concatenate([total, delta], axis=0)
         late = levels[level][1]
         (total,) = call(smooth_join, [packed_smooth])([late], total, arrived)
-        (behind,) = call(smooth_behind, [packed_smooth])([late], arrived, behind)
+        if behind is None:
+            behind = jnp.where(late == 0, arrived, jnp.eye(*packed_smooth, dtype=jnp.float32))
+        else:
+            (behind,) = call(smooth_behind, [packed_smooth])([late], arrived, behind)
+    next_total = jnp.concatenate([next_cov, next_delta], axis=0)
     arrived = swap(total[width:], len(levels) - 1, (0,))
     (reached,) = call(smooth_reach, [packed_filter])([levels[-1][1]], arrived, behind)
     piece = (steps * row_count + steps, width)
@@ -476,7 +516,7 @@
         place_halves,
         [(step_count, row_count), (step_count * row_count, width)],
         [(step_count, width)],
-        sems=(4,),
+        sems=(2, CUTS + 1),
         far=range(4),
         far_outs=[1],
     )([blk], *arrived)

time: 175 us -> 172 us (0.983)
  waiting for transfers between devices: 78.7 us -> 73.1 us
  starting transfers between devices: 48.5 us -> 53.3 us
  local copies, waits for them, and re-layouts: 12.8 us -> 8.46 us
  Pallas kernels: 29.9 us -> 32.3 us
    ppermute x12, waiting for transfers between devices: 11.7 us -> 8.13 us  [to_workers(): return lax.ppermute(array, BOTH, pairs)]
    unnamed x53 -> x46, local copies, waits for them, and re-layouts: 9.67 us -> 6.97 us
    ppermute x12, starting transfers between devices: 36.8 us -> 39.5 us  [to_workers(): return lax.ppermute(array, BOTH, pairs)]
    pallas_call x20 -> x23, Pallas kernels: 29.9 us -> 32.3 us  [run(): pl.pallas_call(body, out_shape=[jax.ShapeDtypeStruct(shape, jnp.float32)...]
    ppermute x4, waiting for transfers between devices: 67 us -> 64.9 us  [from_workers(): return lax.ppermute(array, BOTH, route)]
    ppermute x10 -> x12, starting transfers between devices: 7.79 us -> 8.26 us  [swap(): return lax.ppermute(array, BOTH, route)]
  transfers between devices with their start and end apart: 27 -> 29, of which waited for: 5 -> 5; matrix products, arithmetic and copies ran while one was open for 3% -> 2% of each run, Pallas kernels for 8% -> 10%
where the time goes in v3:
time: 172 us; the launch traced here: 171 us
  waiting for transfers between devices  73.1 us (42%)
  starting transfers between devices  53.3 us (31%)
  Pallas kernels  32.3 us (19%)
  local copies, waits for them, and re-layouts  8.46 us (5%)
    ppermute x4, waiting for transfers between devices, from_workers(): return lax.ppermute(array, BOTH, route)  64.9 us
    ppermute x12, starting transfers between devices, to_workers(): return lax.ppermute(array, BOTH, pairs)  39.5 us
    pallas_call x23, Pallas kernels, run(): pl.pallas_call(body, out_shape=[jax.ShapeDtypeStruct(shape, jnp.float32)...  32.3 us
    ppermute x12, starting transfers between devices, swap(): return lax.ppermute(array, BOTH, route)  8.26 us
    ppermute x12, waiting for transfers between devices, to_workers(): return lax.ppermute(array, BOTH, pairs)  8.13 us
    unnamed x46, local copies, waits for them, and re-layouts  6.97 us
    ppermute x4, starting transfers between devices, from_workers(): return lax.ppermute(array, BOTH, route)  3.97 us
  transfers between devices with their start and end apart: 29, of which 5 were waited for; matrix products, arithmetic and copies ran while one was open for 2% of the time, Pallas kernels for 10%

profile of v3, /device:TPU:0, one launch (start us, length us, event | category | flops | bytes accessed | tf_op | source)
XLA Modules:
  0.0 170.6 jit_solution(619093184217556144)
XLA Ops:
  0.7 1.2 copy-done.2
  2.7 4.4 %collective-permute-start.2 = (f32[8,64,256]{2,1,0:T(8,128)}, f32[8,64,256]{2,1,0:T(8,128)S(1)}, u32[]{:S(2)}, u32[]{:S(2)}) collective-permute-start(f32[8,64,256]{2,1,0:T(8,128)} %shard_map.116), channel_id=1, source_target_pairs={{2,1},{0,5},{6,2},{4,6},{10,9},{8,13},{14,10},{12,14},{18,17},{16,... | collective-permute-start | bytes 1572872 | tf_op jit(solution)/shard_map/ppermute | solution.py:405
  7.1 1.5 collective-permute-start.3
  9.4 3.2 %collective-permute-start = (f32[8,64,256]{2,1,0:T(8,128)}, f32[8,64,256]{2,1,0:T(8,128)}, u32[]{:S(2)}, u32[]{:S(2)}) collective-permute-start(f32[8,64,256]{2,1,0:T(8,128)} %shard_map.115), channel_id=1, source_target_pairs={{0,1},{2,5},{4,2},{6,6},{8,9},{10,13},{12,10},{14,14},{16,17},{18,... | collective-permute-start | bytes 1572872 | tf_op jit(solution)/shard_map/ppermute | solution.py:405
  12.6 1.4 collective-permute-start.1
  14.1 1.6 collective-permute-start.4
  18.1 1.0 mul.10.trans
  19.3 0.9 shard_map.118
  20.2 4.3 %collective-permute-start.6 = (f32[8,64,256]{2,1,0:T(8,128)}, f32[8,64,256]{2,1,0:T(8,128)S(1)}, u32[]{:S(2)}, u32[]{:S(2)}) collective-permute-start(f32[8,64,256]{2,1,0:T(8,128)} %shard_map.118), channel_id=1, source_target_pairs={{0,1},{2,5},{4,2},{6,6},{8,9},{10,13},{12,10},{14,14},{16,17},{18,... | collective-permute-start | bytes 1572872 | tf_op jit(solution)/shard_map/ppermute | solution.py:405
  26.6 4.0 %collective-permute-done.k0 = f32[8,64,256]{2,1,0:T(8,128)} collective-permute-done((f32[8,64,256]{2,1,0:T(8,128)}, f32[8,64,256]{2,1,0:T(8,128)}, u32[]{:S(2)}, u32[]{:S(2)}) %collective-permute-start) | collective-permute-done | bytes 524320 | tf_op jit(solution)/shard_map/ppermute | solution.py:405
  30.6 1.0 copy-done.15
  31.6 4.3 %shard_map.117 = (f32[272,256]{1,0:T(8,128)S(1)}, f32[8,256,256]{2,1,0:T(8,128)S(1)}, f32[8,256]{1,0:T(8,128)S(1)}) custom-call(s32[1]{0:T(128)} %bitcast.1.where, f32[8,64,256]{2,1,0:T(8,128)} %collective-permute-done.k0, f32[8,64,256]{2,1,0:T(8,128)} %collective-permute-done.1.k1, f32[8,64,256]{2,1,0:T(8,128)S(1)} %copy-done.15, ...), custom_call_target="tpu_custom_call" | custom-call | tf_op jit(solution)/shard_map/pallas_call | solution.py:352
  36.7 7.1 %collective-permute-start.12 = (f32[8,64,256]{2,1,0:T(8,128)S(1)}, f32[8,64,256]{2,1,0:T(8,128)S(1)}, u32[]{:S(2)}, u32[]{:S(2)}) collective-permute-start(f32[8,64,256]{2,1,0:T(8,128)S(1)} %shard_map.120), channel_id=1, source_target_pairs={{2,1},{0,5},{6,2},{4,6},{10,9},{8,13},{14,10},{12,14},{18,17},{16,... | collective-permute-start | bytes 1572872 | tf_op jit(solution)/shard_map/ppermute | solution.py:405
  44.5 1.0 shard_map.119
  46.2 6.3 %collective-permute-start.10 = (f32[8,64,256]{2,1,0:T(8,128)}, f32[8,64,256]{2,1,0:T(8,128)}, u32[]{:S(2)}, u32[]{:S(2)}) collective-permute-start(f32[8,64,256]{2,1,0:T(8,128)} %shard_map.114.rest_1_), channel_id=1, source_target_pairs={{2,1},{0,5},{6,2},{4,6},{10,9},{8,13},{14,10},{12,14},{18,17},{16,... | collective-permute-start | bytes 1572872 | tf_op jit(solution)/shard_map/ppermute | solution.py:405
  52.5 1.5 collective-permute-start.11
  54.4 7.0 %collective-permute-start.8 = (f32[8,64,256]{2,1,0:T(8,128)}, f32[8,64,256]{2,1,0:T(8,128)}, u32[]{:S(2)}, u32[]{:S(2)}) collective-permute-start(f32[8,64,256]{2,1,0:T(8,128)} %shard_map.113.rest_0_), channel_id=1, source_target_pairs={{0,1},{2,5},{4,2},{6,6},{8,9},{10,13},{12,10},{14,14},{16,17},{18,... | collective-permute-start | bytes 1572872 | tf_op jit(solution)/shard_map/ppermute | solution.py:405
  61.4 1.5 collective-permute-start.9
  64.9 1.0 shard_map.123
  66.6 1.0 shard_map.124
  68.6 1.0 copy-done.7
  69.6 1.0 copy-done.9
  70.6 2.1 %shard_map.122 = (f32[8,256,256]{2,1,0:T(8,128)S(1)}, f32[8,256,256]{2,1,0:T(8,128)S(1)}) custom-call(s32[1]{0:T(128)} %bitcast.1.where, f32[8,64,256]{2,1,0:T(8,128)S(1)} %collective-permute-done.6.rest_0_.f0, f32[8,64,256]{2,1,0:T(8,128)S(1)} %collective-permute-done.7.rest_1_.f1, f32[8,64,256]{2,1,0:T(8,128)S(1)} %copy-done.7, ...), custom_call_target="tpu_custom_call" | custom-call | tf_op jit(solution)/shard_map/pallas_call | solution.py:352
  73.3 3.7 %collective-permute-done.8.g0 = f32[8,64,256]{2,1,0:T(8,128)} collective-permute-done((f32[8,64,256]{2,1,0:T(8,128)}, f32[8,64,256]{2,1,0:T(8,128)}, u32[]{:S(2)}, u32[]{:S(2)}) %collective-permute-start.8) | collective-permute-done | bytes 524320 | tf_op jit(solution)/shard_map/ppermute | solution.py:405
  77.0 6.2 %shard_map.126 = (f32[512,256]{1,0:T(8,128)S(1)}, f32[8,256,256]{2,1,0:T(8,128)S(1)}, f32[8,256,256]{2,1,0:T(8,128)S(1)}) custom-call(s32[2]{0:T(128)S(1)} %pad_add_fusion.where, f32[8,64,256]{2,1,0:T(8,128)} %collective-permute-done.8.g0, f32[8,64,256]{2,1,0:T(8,128)} %collective-permute-done.9.g1, ...), custom_call_target="tpu_custom_call", output_to_operand_aliasing={{1}: (6, {}), {2}: (5, {})} | custom-call | tf_op jit(solution)/shard_map/pallas_call | solution.py:352
  86.1 2.7 %shard_map.128 = (f32[8,256]{1,0:T(8,128)S(1)}, f32[16,256]{1,0:T(8,128)S(1)}) custom-call(s32[2]{0:T(128)S(1)} %pad_add_fusion.where, f32[8,64,256]{2,1,0:T(8,128)} %collective-permute-done.8.g0, f32[8,64,256]{2,1,0:T(8,128)} %collective-permute-done.9.g1, f32[8,64,256]{2,1,0:T(8,128)} %collective-permute-done.10.g2, ...), custom_call_target="tpu_custom_call" | custom-call | tf_op jit(solution)/shard_map/pallas_call | solution.py:352
  96.4 3.4 %shard_map.134 = (f32[520,256]{1,0:T(8,128)S(1)}, f32[520,256]{1,0:T(8,128)S(1)}, f32[520,256]{1,0:T(8,128)S(1)}, f32[520,256]{1,0:T(8,128)S(1)}) custom-call(s32[1]{0:T(128)} %bitcast.1.where, f32[272,256]{1,0:T(8,128)S(1)} %shard_map.133.own, f32[272,256]{1,0:T(8,128)S(1)} %collective-permute-done.24.other, f32[528,256]{1,0:T(8,128)S(1)} %pad_maximum_fusion.1.next_total, ...), custom_call_target="tpu_custom_call" | custom-call | tf_op jit(solution)/shard_map/pallas_call | solution.py:352
  99.8 1.3 collective-permute-start.25
  101.8 1.3 collective-permute-start.27
  103.8 63.1 %collective-permute-done.25.a0 = f32[520,256]{1,0:T(8,128)S(1)} collective-permute-done((f32[520,256]{1,0:T(8,128)S(1)}, f32[520,256]{1,0:T(8,128)S(1)}, u32[]{:S(2)}, u32[]{:S(2)}) %collective-permute-start.25) | collective-permute-done | bytes 532512 | tf_op jit(solution)/shard_map/ppermute | solution.py:414
  167.0 1.8 %collective-permute-done.27.a2 = f32[520,256]{1,0:T(8,128)S(1)} collective-permute-done((f32[520,256]{1,0:T(8,128)S(1)}, f32[520,256]{1,0:T(8,128)S(1)}, u32[]{:S(2)}, u32[]{:S(2)}) %collective-permute-start.27) | collective-permute-done | bytes 532512 | tf_op jit(solution)/shard_map/ppermute | solution.py:414
  168.8 1.6 shard_map.135
  (117 shorter events, 24.6 us)
Async XLA Ops:
  1.9 13.8 %copy-start.4 = (f32[16,64,256]{2,1,0:T(8,128)S(1)}, f32[16,64,256]{2,1,0:T(8,128)}, u32[]{:S(2)}) copy-start(f32[16,64,256]{2,1,0:T(8,128)} %refs_0_.7) | copy-start | bytes 3145732
  2.7 21.7 %collective-permute-start.2 = (f32[8,64,256]{2,1,0:T(8,128)}, f32[8,64,256]{2,1,0:T(8,128)S(1)}, u32[]{:S(2)}, u32[]{:S(2)}) collective-permute-start(f32[8,64,256]{2,1,0:T(8,128)} %shard_map.116), channel_id=1, source_target_pairs={{2,1},{0,5},{6,2},{4,6},{10,9},{8,13},{14,10},{12,14},{18,17},{16,... | collective-permute-start | bytes 1572872 | tf_op jit(solution)/shard_map/ppermute | solution.py:405
  7.1 19.5 %collective-permute-start.3 = (f32[8,64,256]{2,1,0:T(8,128)}, f32[8,64,256]{2,1,0:T(8,128)}, u32[]{:S(2)}, u32[]{:S(2)}) collective-permute-start(f32[8,64,256]{2,1,0:T(8,128)} %shard_map.116), channel_id=1, source_target_pairs={{3,1},{1,5},{7,2},{5,6},{11,9},{9,13},{15,10},{13,14},{19,17},{17,... | collective-permute-start | bytes 1572872 | tf_op jit(solution)/shard_map/ppermute | solution.py:405
  9.4 21.1 %collective-permute-start = (f32[8,64,256]{2,1,0:T(8,128)}, f32[8,64,256]{2,1,0:T(8,128)}, u32[]{:S(2)}, u32[]{:S(2)}) collective-permute-start(f32[8,64,256]{2,1,0:T(8,128)} %shard_map.115), channel_id=1, source_target_pairs={{0,1},{2,5},{4,2},{6,6},{8,9},{10,13},{12,10},{14,14},{16,17},{18,... | collective-permute-start | bytes 1572872 | tf_op jit(solution)/shard_map/ppermute | solution.py:405
  12.6 17.9 %collective-permute-start.1 = (f32[8,64,256]{2,1,0:T(8,128)}, f32[8,64,256]{2,1,0:T(8,128)}, u32[]{:S(2)}, u32[]{:S(2)}) collective-permute-start(f32[8,64,256]{2,1,0:T(8,128)} %shard_map.115), channel_id=1, source_target_pairs={{1,1},{3,5},{5,2},{7,6},{9,9},{11,13},{13,10},{15,14},{17,17},{19,... | collective-permute-start | bytes 1572872 | tf_op jit(solution)/shard_map/ppermute | solution.py:405
  14.1 6.1 %collective-permute-start.4 = (f32[16,256]{1,0:T(8,128)S(1)}, f32[16,256]{1,0:T(8,128)S(1)}, u32[]{:S(2)}, u32[]{:S(2)}) collective-permute-start(f32[16,256]{1,0:T(8,128)S(1)} %copy-done.19), channel_id=1, source_target_pairs={{0,4},{4,0},{8,12},{12,8},{16,20},{20,16},{24,28},{28,24},{1,5},{5... | collective-permute-start | bytes 49160 | tf_op jit(solution)/shard_map/ppermute | solution.py:431
  20.2 24.3 %collective-permute-start.6 = (f32[8,64,256]{2,1,0:T(8,128)}, f32[8,64,256]{2,1,0:T(8,128)S(1)}, u32[]{:S(2)}, u32[]{:S(2)}) collective-permute-start(f32[8,64,256]{2,1,0:T(8,128)} %shard_map.118), channel_id=1, source_target_pairs={{0,1},{2,5},{4,2},{6,6},{8,9},{10,13},{12,10},{14,14},{16,17},{18,... | collective-permute-start | bytes 1572872 | tf_op jit(solution)/shard_map/ppermute | solution.py:405
  25.3 19.2 %collective-permute-start.7 = (f32[8,64,256]{2,1,0:T(8,128)}, f32[8,64,256]{2,1,0:T(8,128)S(1)}, u32[]{:S(2)}, u32[]{:S(2)}) collective-permute-start(f32[8,64,256]{2,1,0:T(8,128)} %shard_map.118), channel_id=1, source_target_pairs={{1,1},{3,5},{5,2},{7,6},{9,9},{11,13},{13,10},{15,14},{17,17},{19,... | collective-permute-start | bytes 1572872 | tf_op jit(solution)/shard_map/ppermute | solution.py:405
  35.9 27.4 %copy-start.10 = (f32[8,256,256]{2,1,0:T(8,128)}, f32[8,256,256]{2,1,0:T(8,128)S(1)}, u32[]{:S(2)}) copy-start(f32[8,256,256]{2,1,0:T(8,128)S(1)} %get-tuple-element.39.maps) | copy-start | bytes 6291460
  35.9 8.5 %collective-permute-start.5 = (f32[272,256]{1,0:T(8,128)S(1)}, f32[272,256]{1,0:T(8,128)S(1)}, u32[]{:S(2)}, u32[]{:S(2)}) collective-permute-start(f32[272,256]{1,0:T(8,128)S(1)} %get-tuple-element.27.own), channel_id=1, source_target_pairs={{5,1},{6,2},{13,9},{14,10},{21,17},{22,18},{29,25},{30,26}} | collective-permute-start | bytes 835592 | tf_op jit(solution)/shard_map/ppermute | solution.py:429
  36.7 17.7 %collective-permute-start.12 = (f32[8,64,256]{2,1,0:T(8,128)S(1)}, f32[8,64,256]{2,1,0:T(8,128)S(1)}, u32[]{:S(2)}, u32[]{:S(2)}) collective-permute-start(f32[8,64,256]{2,1,0:T(8,128)S(1)} %shard_map.120), channel_id=1, source_target_pairs={{2,1},{0,5},{6,2},{4,6},{10,9},{8,13},{14,10},{12,14},{18,17},{16,... | collective-permute-start | bytes 1572872 | tf_op jit(solution)/shard_map/ppermute | solution.py:405
  43.7 17.7 %collective-permute-start.13 = (f32[8,64,256]{2,1,0:T(8,128)S(1)}, f32[8,64,256]{2,1,0:T(8,128)S(1)}, u32[]{:S(2)}, u32[]{:S(2)}) collective-permute-start(f32[8,64,256]{2,1,0:T(8,128)S(1)} %shard_map.120), channel_id=1, source_target_pairs={{3,1},{1,5},{7,2},{5,6},{11,9},{9,13},{15,10},{13,14},{19,17},{17,... | collective-permute-start | bytes 1572872 | tf_op jit(solution)/shard_map/ppermute | solution.py:405
  44.5 24.1 %copy-start.17 = (f32[256]{0:T(256)S(1)}, f32[256]{0:T(256)}, u32[]{:S(2)}) copy-start(f32[256]{0:T(256)} %param.14) | copy-start | bytes 3076
  45.6 17.3 %collective-permute-start.14 = (f32[272,256]{1,0:T(8,128)S(1)}, f32[272,256]{1,0:T(8,128)S(1)}, u32[]{:S(2)}, u32[]{:S(2)}) collective-permute-start(f32[272,256]{1,0:T(8,128)S(1)} %get-tuple-element.31.own), channel_id=1, source_target_pairs={{1,2},{2,1},{9,10},{10,9},{17,18},{18,17},{25,26},{26,25}} | collective-permute-start | bytes 835592 | tf_op jit(solution)/shard_map/ppermute | solution.py:429
  46.2 27.0 %collective-permute-start.10 = (f32[8,64,256]{2,1,0:T(8,128)}, f32[8,64,256]{2,1,0:T(8,128)}, u32[]{:S(2)}, u32[]{:S(2)}) collective-permute-start(f32[8,64,256]{2,1,0:T(8,128)} %shard_map.114.rest_1_), channel_id=1, source_target_pairs={{2,1},{0,5},{6,2},{4,6},{10,9},{8,13},{14,10},{12,14},{18,17},{16,... | collective-permute-start | bytes 1572872 | tf_op jit(solution)/shard_map/ppermute | solution.py:405
  52.5 20.7 %collective-permute-start.11 = (f32[8,64,256]{2,1,0:T(8,128)}, f32[8,64,256]{2,1,0:T(8,128)}, u32[]{:S(2)}, u32[]{:S(2)}) collective-permute-start(f32[8,64,256]{2,1,0:T(8,128)} %shard_map.114.rest_1_), channel_id=1, source_target_pairs={{3,1},{1,5},{7,2},{5,6},{11,9},{9,13},{15,10},{13,14},{19,17},{17,... | collective-permute-start | bytes 1572872 | tf_op jit(solution)/shard_map/ppermute | solution.py:405
  54.4 22.6 %collective-permute-start.8 = (f32[8,64,256]{2,1,0:T(8,128)}, f32[8,64,256]{2,1,0:T(8,128)}, u32[]{:S(2)}, u32[]{:S(2)}) collective-permute-start(f32[8,64,256]{2,1,0:T(8,128)} %shard_map.113.rest_0_), channel_id=1, source_target_pairs={{0,1},{2,5},{4,2},{6,6},{8,9},{10,13},{12,10},{14,14},{16,17},{18,... | collective-permute-start | bytes 1572872 | tf_op jit(solution)/shard_map/ppermute | solution.py:405
  61.4 15.6 %collective-permute-start.9 = (f32[8,64,256]{2,1,0:T(8,128)}, f32[8,64,256]{2,1,0:T(8,128)}, u32[]{:S(2)}, u32[]{:S(2)}) collective-permute-start(f32[8,64,256]{2,1,0:T(8,128)} %shard_map.113.rest_0_), channel_id=1, source_target_pairs={{1,1},{3,5},{5,2},{7,6},{9,9},{11,13},{13,10},{15,14},{17,17},{19,... | collective-permute-start | bytes 1572872 | tf_op jit(solution)/shard_map/ppermute | solution.py:405
  64.1 0.7 collective-permute-start.15
  65.9 0.7 collective-permute-start.16
  67.6 5.1 %collective-permute-start.17 = (f32[16,256]{1,0:T(8,128)S(1)}, f32[16,256]{1,0:T(8,128)S(1)}, u32[]{:S(2)}, u32[]{:S(2)}) collective-permute-start(f32[16,256]{1,0:T(8,128)S(1)} %get-tuple-element.38), channel_id=1, source_target_pairs={{1,5},{2,6},{9,13},{10,14},{17,21},{18,22},{25,29},{26,30}} | collective-permute-start | bytes 49160 | tf_op jit(solution)/shard_map/ppermute | solution.py:429
  83.2 0.7 collective-permute-start.18
  85.4 5.0 %collective-permute-start.20 = (f32[512,256]{1,0:T(8,128)S(1)}, f32[512,256]{1,0:T(8,128)S(1)}, u32[]{:S(2)}, u32[]{:S(2)}) collective-permute-start(f32[512,256]{1,0:T(8,128)S(1)} %shard_map.127), channel_id=1, source_target_pairs={{1,2},{2,1},{9,10},{10,9},{17,18},{18,17},{25,26},{26,25}} | collective-permute-start | bytes 1572872 | tf_op jit(solution)/shard_map/ppermute | solution.py:429
  88.9 0.7 collective-permute-start.19
  89.7 0.8 collective-permute-start.21
  91.3 0.7 collective-permute-start.22
  93.5 1.5 collective-permute-start.23
  95.7 0.7 collective-permute-start.24
  99.8 67.1 %collective-permute-start.25 = (f32[520,256]{1,0:T(8,128)S(1)}, f32[520,256]{1,0:T(8,128)S(1)}, u32[]{:S(2)}, u32[]{:S(2)}) collective-permute-start(f32[520,256]{1,0:T(8,128)S(1)} %get-tuple-element.46), channel_id=1, source_target_pairs={{1,0},{5,2},{2,4},{6,6},{9,8},{13,10},{10,12},{14,14},{17,16},{21,... | collective-permute-start | bytes 1597448 | tf_op jit(solution)/shard_map/ppermute | solution.py:414
  101.1 65.8 %collective-permute-start.26 = (f32[520,256]{1,0:T(8,128)S(1)}, f32[520,256]{1,0:T(8,128)S(1)}, u32[]{:S(2)}, u32[]{:S(2)}) collective-permute-start(f32[520,256]{1,0:T(8,128)S(1)} %get-tuple-element.47), channel_id=1, source_target_pairs={{1,1},{5,3},{2,5},{6,7},{9,9},{13,11},{10,13},{14,15},{17,17},{21,... | collective-permute-start | bytes 1597448 | tf_op jit(solution)/shard_map/ppermute | solution.py:414
  101.8 66.9 %collective-permute-start.27 = (f32[520,256]{1,0:T(8,128)S(1)}, f32[520,256]{1,0:T(8,128)S(1)}, u32[]{:S(2)}, u32[]{:S(2)}) collective-permute-start(f32[520,256]{1,0:T(8,128)S(1)} %get-tuple-element.48), channel_id=1, source_target_pairs={{1,2},{5,0},{2,6},{6,4},{9,10},{13,8},{10,14},{14,12},{17,18},{21,... | collective-permute-start | bytes 1597448 | tf_op jit(solution)/shard_map/ppermute | solution.py:414
  103.1 65.6 %collective-permute-start.28 = (f32[520,256]{1,0:T(8,128)S(1)}, f32[520,256]{1,0:T(8,128)S(1)}, u32[]{:S(2)}, u32[]{:S(2)}) collective-permute-start(f32[520,256]{1,0:T(8,128)S(1)} %get-tuple-element.49), channel_id=1, source_target_pairs={{1,3},{5,1},{2,7},{6,5},{9,11},{13,9},{10,15},{14,13},{17,19},{21,... | collective-permute-start | bytes 1597448 | tf_op jit(solution)/shard_map/ppermute | solution.py:414
  (19 other events, 74.7 us)

commit v4 on v3

--- a/solution.py
+++ b/solution.py
@@ -193,7 +193,7 @@
     delta[...] = state[0] + mm_nt(state[1], maps[0])
 
 
-def smooth_join_cov(where, own, other, total):
+def smooth_join_cov(where, own, other, after, total):
     width = own.shape[1]
     gain = halves(own[:width])
     total[:width] = product(gain, halves(other[:width]), ((1,), (0,)))
@@ -453,7 +453,10 @@
     )
     total, arrived, others = chunk, swap(chunk, 0, (1,)), []
     for level in range(len(levels) - 1):
-        after = (cov_parts[:2], cov_parts[2:])[level] if level < 2 else []
+        after = (cov_parts[:2], cov_parts)[level] if level < 2 else []
+        after = after + [maps]
+        if level == len(levels) - 2:
+            after = after + [pred]
         total, state = call(
             filter_join, [packed_filter, (PAD, width)], far=range(-len(after), 0)
         )([levels[level][1] if level else 0], total, arrived, initial, *after)
@@ -482,13 +485,13 @@
     final = jnp.logical_and(tm // 2 == lines - 1, jnp.logical_and(half == 1, blk == 2))
     plain = (2 * width, width)
     first, maps, covs = call(smooth_chunk, [plain, stack, stack], alias=[(5, 1), (4, 2)], far=[-1])(
-        [half, final], *smooth_parts, filt, pred, means
+        [half, final], *smooth_parts, filt, pred, reached
     )
     offsets, delta = call(smooth_offsets, [short, (PAD, width)])(
         [half, final], *smooth_parts, means, trans_map, maps
     )
     next_cov = swap(first, 0, (1,))
-    (total,) = call(smooth_join_cov, [plain])([0], first, next_cov)
+    (total,) = call(smooth_join_cov, [plain], far=[-1])([0], first, next_cov, delta)
     next_delta = swap(delta, 0, (1,))
     (delta,) = call(smooth_join_delta, [(PAD, width)])([0], first, delta, next_delta)
     behind = None

time: 172 us -> 169 us (0.983)
  local copies, waits for them, and re-layouts: 8.46 us -> 5.34 us
  waiting for transfers between devices: 73.1 us -> 70.8 us
    ppermute x4, waiting for transfers between devices: 64.9 us -> 56.9 us  [from_workers(): return lax.ppermute(array, BOTH, route)]
    ppermute x12, waiting for transfers between devices: 8.13 us -> 13.8 us  [to_workers(): return lax.ppermute(array, BOTH, pairs)]
    unnamed x46 -> x52, local copies, waits for them, and re-layouts: 6.97 us -> 3.87 us
    ppermute x12, starting transfers between devices: 39.5 us -> 42.1 us  [to_workers(): return lax.ppermute(array, BOTH, pairs)]
  transfers between devices with their start and end apart: 29 -> 29, of which waited for: 5 -> 6; matrix products, arithmetic and copies ran while one was open for 2% -> 1% of each run, Pallas kernels for 10% -> 11%
where the time goes in v4:
time: 169 us; the launch traced here: 167 us
  waiting for transfers between devices  70.8 us (42%)
  starting transfers between devices  55 us (33%)
  Pallas kernels  33.6 us (20%)
  local copies, waits for them, and re-layouts  5.34 us (3%)
    ppermute x4, waiting for transfers between devices, from_workers(): return lax.ppermute(array, BOTH, route)  56.9 us
    ppermute x12, starting transfers between devices, to_workers(): return lax.ppermute(array, BOTH, pairs)  42.1 us
    pallas_call x23, Pallas kernels, run(): pl.pallas_call(body, out_shape=[jax.ShapeDtypeStruct(shape, jnp.float32)...  33.6 us
    ppermute x12, waiting for transfers between devices, to_workers(): return lax.ppermute(array, BOTH, pairs)  13.8 us
    ppermute x12, starting transfers between devices, swap(): return lax.ppermute(array, BOTH, route)  8.96 us
    ppermute x4, starting transfers between devices, from_workers(): return lax.ppermute(array, BOTH, route)  3.97 us
    unnamed x52, local copies, waits for them, and re-layouts  3.87 us
  transfers between devices with their start and end apart: 29, of which 6 were waited for; matrix products, arithmetic and copies ran while one was open for 1% of the time, Pallas kernels for 11%

profile of v4, /device:TPU:0, one launch (start us, length us, event | category | flops | bytes accessed | tf_op | source)
XLA Modules:
  0.0 167.2 jit_solution(2501448850368993476)
XLA Ops:
  0.6 1.2 copy-done.4
  2.7 1.5 collective-permute-start.1
  4.2 9.6 %collective-permute-start = (f32[8,64,256]{2,1,0:T(8,128)}, f32[8,64,256]{2,1,0:T(8,128)}, u32[]{:S(2)}, u32[]{:S(2)}) collective-permute-start(f32[8,64,256]{2,1,0:T(8,128)} %shard_map.115), channel_id=1, source_target_pairs={{0,1},{2,5},{4,2},{6,6},{8,9},{10,13},{12,10},{14,14},{16,17},{18,... | collective-permute-start | bytes 1572872 | tf_op jit(solution)/shard_map/ppermute | solution.py:405
  14.6 1.5 collective-permute-start.3
  16.1 2.5 %collective-permute-start.2 = (f32[8,64,256]{2,1,0:T(8,128)}, f32[8,64,256]{2,1,0:T(8,128)}, u32[]{:S(2)}, u32[]{:S(2)}) collective-permute-start(f32[8,64,256]{2,1,0:T(8,128)} %shard_map.116), channel_id=1, source_target_pairs={{2,1},{0,5},{6,2},{4,6},{10,9},{8,13},{14,10},{12,14},{18,17},{16,... | collective-permute-start | bytes 1572872 | tf_op jit(solution)/shard_map/ppermute | solution.py:405
  22.3 1.3 collective-permute-start.6
  24.2 1.4 collective-permute-done.k0
  26.4 9.0 %collective-permute-start.12 = (f32[8,64,256]{2,1,0:T(8,128)S(1)}, f32[8,64,256]{2,1,0:T(8,128)S(1)}, u32[]{:S(2)}, u32[]{:S(2)}) collective-permute-start(f32[8,64,256]{2,1,0:T(8,128)S(1)} %shard_map.120), channel_id=1, source_target_pairs={{2,1},{0,5},{6,2},{4,6},{10,9},{8,13},{14,10},{12,14},{18,17},{16,... | collective-permute-start | bytes 1572872 | tf_op jit(solution)/shard_map/ppermute | solution.py:405
  35.4 1.5 collective-permute-done.2.k2
  36.9 4.5 %shard_map.117 = (f32[272,256]{1,0:T(8,128)S(1)}, f32[8,256,256]{2,1,0:T(8,128)S(1)}, f32[8,256]{1,0:T(8,128)S(1)}) custom-call(s32[1]{0:T(128)} %bitcast.1.where, f32[8,64,256]{2,1,0:T(8,128)} %collective-permute-done.k0, f32[8,64,256]{2,1,0:T(8,128)} %collective-permute-done.1.k1, f32[8,64,256]{2,1,0:T(8,128)} %collective-permute-done.2.k2, ...), custom_call_target="tpu_custom_call" | custom-call | tf_op jit(solution)/shard_map/pallas_call | solution.py:352
  42.1 6.0 %collective-permute-done.6.rest_0_.f0 = f32[8,64,256]{2,1,0:T(8,128)S(1)} collective-permute-done((f32[8,64,256]{2,1,0:T(8,128)S(1)}, f32[8,64,256]{2,1,0:T(8,128)S(1)}, u32[]{:S(2)}, u32[]{:S(2)}) %collective-permute-start.6) | collective-permute-done | bytes 524320 | tf_op jit(solution)/shard_map/ppermute | solution.py:405
  48.0 1.1 shard_map.119
  49.8 1.5 collective-permute-start.9
  51.2 10.3 %collective-permute-start.8 = (f32[8,64,256]{2,1,0:T(8,128)}, f32[8,64,256]{2,1,0:T(8,128)}, u32[]{:S(2)}, u32[]{:S(2)}) collective-permute-start(f32[8,64,256]{2,1,0:T(8,128)} %shard_map.113.rest_0_), channel_id=1, source_target_pairs={{0,1},{2,5},{4,2},{6,6},{8,9},{10,13},{12,10},{14,14},{16,17},{18,... | collective-permute-start | bytes 1572872 | tf_op jit(solution)/shard_map/ppermute | solution.py:405
  61.6 1.5 collective-permute-start.11
  63.0 2.1 %collective-permute-start.10 = (f32[8,64,256]{2,1,0:T(8,128)}, f32[8,64,256]{2,1,0:T(8,128)}, u32[]{:S(2)}, u32[]{:S(2)}) collective-permute-start(f32[8,64,256]{2,1,0:T(8,128)} %shard_map.114.rest_1_), channel_id=1, source_target_pairs={{2,1},{0,5},{6,2},{4,6},{10,9},{8,13},{14,10},{12,14},{18,17},{16,... | collective-permute-start | bytes 1572872 | tf_op jit(solution)/shard_map/ppermute | solution.py:405
  65.1 1.0 shard_map.121
  66.2 1.4 collective-permute-start.15
  67.6 1.2 copy-done.11
  68.8 1.0 copy-done.13
  69.9 2.1 %shard_map.122 = (f32[8,256,256]{2,1,0:T(8,128)S(1)}, f32[8,256,256]{2,1,0:T(8,128)S(1)}) custom-call(s32[1]{0:T(128)} %bitcast.1.where, f32[8,64,256]{2,1,0:T(8,128)S(1)} %collective-permute-done.6.rest_0_.f0, f32[8,64,256]{2,1,0:T(8,128)S(1)} %collective-permute-done.7.rest_1_.f1, f32[8,64,256]{2,1,0:T(8,128)S(1)} %copy-done.13, ...), custom_call_target="tpu_custom_call" | custom-call | tf_op jit(solution)/shard_map/pallas_call | solution.py:352
  72.0 2.1 %shard_map.123 = (f32[272,256]{1,0:T(8,128)}, f32[16,256]{1,0:T(8,128)S(1)}) custom-call(s32[1]{0:T(128)} %bitcast.3.where, f32[272,256]{1,0:T(8,128)} %get-tuple-element.36.own, f32[272,256]{1,0:T(8,128)} %collective-permute-done.15.other.rest_0_, f32[1,256]{1,0:T(1,128)S(1)} %bitcast.24, f32[8,256,256]{2,1,0:T(8,128)S(1)} %copy-done.1, ...), custom_call_target="tpu_custom_call" | custom-call | tf_op jit(solution)/shard_map/pallas_call | solution.py:352
  75.1 1.4 shard_map.124
  76.5 4.9 %collective-permute-done.10.g2 = f32[8,64,256]{2,1,0:T(8,128)} collective-permute-done((f32[8,64,256]{2,1,0:T(8,128)}, f32[8,64,256]{2,1,0:T(8,128)}, u32[]{:S(2)}, u32[]{:S(2)}) %collective-permute-start.10) | collective-permute-done | bytes 524320 | tf_op jit(solution)/shard_map/ppermute | solution.py:405
  81.5 6.2 %shard_map.125 = (f32[512,256]{1,0:T(8,128)S(1)}, f32[8,256,256]{2,1,0:T(8,128)S(1)}, f32[8,256,256]{2,1,0:T(8,128)S(1)}) custom-call(s32[2]{0:T(128)S(1)} %pad_add_fusion.where, f32[8,64,256]{2,1,0:T(8,128)} %collective-permute-done.8.g0, f32[8,64,256]{2,1,0:T(8,128)} %collective-permute-done.9.g1, ...), custom_call_target="tpu_custom_call", output_to_operand_aliasing={{1}: (6, {}), {2}: (5, {})} | custom-call | tf_op jit(solution)/shard_map/pallas_call | solution.py:352
  89.5 2.8 %shard_map.127 = (f32[8,256]{1,0:T(8,128)S(1)}, f32[16,256]{1,0:T(8,128)S(1)}) custom-call(s32[2]{0:T(128)S(1)} %pad_add_fusion.where, f32[8,64,256]{2,1,0:T(8,128)} %collective-permute-done.8.g0, f32[8,64,256]{2,1,0:T(8,128)} %collective-permute-done.9.g1, f32[8,64,256]{2,1,0:T(8,128)} %collective-permute-done.10.g2, ...), custom_call_target="tpu_custom_call" | custom-call | tf_op jit(solution)/shard_map/pallas_call | solution.py:352
  101.3 3.2 %shard_map.134 = (f32[520,256]{1,0:T(8,128)S(1)}, f32[520,256]{1,0:T(8,128)S(1)}, f32[520,256]{1,0:T(8,128)S(1)}, f32[520,256]{1,0:T(8,128)S(1)}) custom-call(s32[1]{0:T(128)} %bitcast.1.where, f32[272,256]{1,0:T(8,128)S(1)} %shard_map.133.own, f32[272,256]{1,0:T(8,128)S(1)} %collective-permute-done.24.other, f32[528,256]{1,0:T(8,128)S(1)} %pad_maximum_fusion.1.next_total, ...), custom_call_target="tpu_custom_call" | custom-call | tf_op jit(solution)/shard_map/pallas_call | solution.py:352
  104.5 1.3 collective-permute-start.25
  106.5 1.3 collective-permute-start.27
  108.5 55.2 %collective-permute-done.25.a0 = f32[520,256]{1,0:T(8,128)S(1)} collective-permute-done((f32[520,256]{1,0:T(8,128)S(1)}, f32[520,256]{1,0:T(8,128)S(1)}, u32[]{:S(2)}, u32[]{:S(2)}) %collective-permute-start.25) | collective-permute-done | bytes 532512 | tf_op jit(solution)/shard_map/ppermute | solution.py:414
  163.7 1.7 collective-permute-done.27.a2
  165.4 1.6 shard_map.135
  (123 shorter events, 20.9 us)
Async XLA Ops:
  2.7 19.6 %collective-permute-start.1 = (f32[8,64,256]{2,1,0:T(8,128)}, f32[8,64,256]{2,1,0:T(8,128)}, u32[]{:S(2)}, u32[]{:S(2)}) collective-permute-start(f32[8,64,256]{2,1,0:T(8,128)} %shard_map.115), channel_id=1, source_target_pairs={{1,1},{3,5},{5,2},{7,6},{9,9},{11,13},{13,10},{15,14},{17,17},{19,... | collective-permute-start | bytes 1572872 | tf_op jit(solution)/shard_map/ppermute | solution.py:405
  4.2 21.5 %collective-permute-start = (f32[8,64,256]{2,1,0:T(8,128)}, f32[8,64,256]{2,1,0:T(8,128)}, u32[]{:S(2)}, u32[]{:S(2)}) collective-permute-start(f32[8,64,256]{2,1,0:T(8,128)} %shard_map.115), channel_id=1, source_target_pairs={{0,1},{2,5},{4,2},{6,6},{8,9},{10,13},{12,10},{14,14},{16,17},{18,... | collective-permute-start | bytes 1572872 | tf_op jit(solution)/shard_map/ppermute | solution.py:405
  14.6 11.7 %collective-permute-start.3 = (f32[8,64,256]{2,1,0:T(8,128)}, f32[8,64,256]{2,1,0:T(8,128)}, u32[]{:S(2)}, u32[]{:S(2)}) collective-permute-start(f32[8,64,256]{2,1,0:T(8,128)} %shard_map.116), channel_id=1, source_target_pairs={{3,1},{1,5},{7,2},{5,6},{11,9},{9,13},{15,10},{13,14},{19,17},{17,... | collective-permute-start | bytes 1572872 | tf_op jit(solution)/shard_map/ppermute | solution.py:405
  16.1 20.8 %collective-permute-start.2 = (f32[8,64,256]{2,1,0:T(8,128)}, f32[8,64,256]{2,1,0:T(8,128)}, u32[]{:S(2)}, u32[]{:S(2)}) collective-permute-start(f32[8,64,256]{2,1,0:T(8,128)} %shard_map.116), channel_id=1, source_target_pairs={{2,1},{0,5},{6,2},{4,6},{10,9},{8,13},{14,10},{12,14},{18,17},{16,... | collective-permute-start | bytes 1572872 | tf_op jit(solution)/shard_map/ppermute | solution.py:405
  18.6 3.0 %collective-permute-start.4 = (f32[16,256]{1,0:T(8,128)S(1)}, f32[16,256]{1,0:T(8,128)S(1)}, u32[]{:S(2)}, u32[]{:S(2)}) collective-permute-start(f32[16,256]{1,0:T(8,128)S(1)} %copy-done.22), channel_id=1, source_target_pairs={{0,4},{4,0},{8,12},{12,8},{16,20},{20,16},{24,28},{28,24},{1,5},{5... | collective-permute-start | bytes 49160 | tf_op jit(solution)/shard_map/ppermute | solution.py:431
  21.6 26.5 %copy-start.18 = (f32[256]{0:T(256)S(1)}, f32[256]{0:T(256)}, u32[]{:S(2)}) copy-start(f32[256]{0:T(256)} %param.15) | copy-start | bytes 3076
  21.6 20.5 %collective-permute-start.7 = (f32[8,64,256]{2,1,0:T(8,128)S(1)}, f32[8,64,256]{2,1,0:T(8,128)S(1)}, u32[]{:S(2)}, u32[]{:S(2)}) collective-permute-start(f32[8,64,256]{2,1,0:T(8,128)S(1)} %shard_map.118), channel_id=1, source_target_pairs={{1,1},{3,5},{5,2},{7,6},{9,9},{11,13},{13,10},{15,14},{17,17},{19,... | collective-permute-start | bytes 1572872 | tf_op jit(solution)/shard_map/ppermute | solution.py:405
  22.3 25.7 %collective-permute-start.6 = (f32[8,64,256]{2,1,0:T(8,128)S(1)}, f32[8,64,256]{2,1,0:T(8,128)S(1)}, u32[]{:S(2)}, u32[]{:S(2)}) collective-permute-start(f32[8,64,256]{2,1,0:T(8,128)S(1)} %shard_map.118), channel_id=1, source_target_pairs={{0,1},{2,5},{4,2},{6,6},{8,9},{10,13},{12,10},{14,14},{16,17},{18,... | collective-permute-start | bytes 1572872 | tf_op jit(solution)/shard_map/ppermute | solution.py:405
  25.7 35.9 %collective-permute-start.13 = (f32[8,64,256]{2,1,0:T(8,128)S(1)}, f32[8,64,256]{2,1,0:T(8,128)S(1)}, u32[]{:S(2)}, u32[]{:S(2)}) collective-permute-start(f32[8,64,256]{2,1,0:T(8,128)S(1)} %shard_map.120), channel_id=1, source_target_pairs={{3,1},{1,5},{7,2},{5,6},{11,9},{9,13},{15,10},{13,14},{19,17},{17,... | collective-permute-start | bytes 1572872 | tf_op jit(solution)/shard_map/ppermute | solution.py:405
  26.4 36.7 %collective-permute-start.12 = (f32[8,64,256]{2,1,0:T(8,128)S(1)}, f32[8,64,256]{2,1,0:T(8,128)S(1)}, u32[]{:S(2)}, u32[]{:S(2)}) collective-permute-start(f32[8,64,256]{2,1,0:T(8,128)S(1)} %shard_map.120), channel_id=1, source_target_pairs={{2,1},{0,5},{6,2},{4,6},{10,9},{8,13},{14,10},{12,14},{18,17},{16,... | collective-permute-start | bytes 1572872 | tf_op jit(solution)/shard_map/ppermute | solution.py:405
  41.4 24.8 %copy-start = (f32[8,256,256]{2,1,0:T(8,128)}, f32[8,256,256]{2,1,0:T(8,128)S(1)}, u32[]{:S(2)}) copy-start(f32[8,256,256]{2,1,0:T(8,128)S(1)} %get-tuple-element.28.rest_2_.rest_4_.rest_0_.maps) | copy-start | bytes 6291460
  41.4 24.8 %copy-start.14 = (f32[272,256]{1,0:T(8,128)}, f32[272,256]{1,0:T(8,128)S(1)}, u32[]{:S(2)}) copy-start(f32[272,256]{1,0:T(8,128)S(1)} %get-tuple-element.27.own) | copy-start | bytes 835588
  41.4 6.7 %collective-permute-start.5 = (f32[272,256]{1,0:T(8,128)S(1)}, f32[272,256]{1,0:T(8,128)S(1)}, u32[]{:S(2)}, u32[]{:S(2)}) collective-permute-start(f32[272,256]{1,0:T(8,128)S(1)} %get-tuple-element.27.own), channel_id=1, source_target_pairs={{5,1},{6,2},{13,9},{14,10},{21,17},{22,18},{29,25},{30,26}} | collective-permute-start | bytes 835592 | tf_op jit(solution)/shard_map/ppermute | solution.py:429
  49.1 16.1 %collective-permute-start.14 = (f32[272,256]{1,0:T(8,128)S(1)}, f32[272,256]{1,0:T(8,128)S(1)}, u32[]{:S(2)}, u32[]{:S(2)}) collective-permute-start(f32[272,256]{1,0:T(8,128)S(1)} %get-tuple-element.32.own), channel_id=1, source_target_pairs={{1,2},{2,1},{9,10},{10,9},{17,18},{18,17},{25,26},{26,25}} | collective-permute-start | bytes 835592 | tf_op jit(solution)/shard_map/ppermute | solution.py:429
  49.8 26.8 %collective-permute-start.9 = (f32[8,64,256]{2,1,0:T(8,128)}, f32[8,64,256]{2,1,0:T(8,128)}, u32[]{:S(2)}, u32[]{:S(2)}) collective-permute-start(f32[8,64,256]{2,1,0:T(8,128)} %shard_map.113.rest_0_), channel_id=1, source_target_pairs={{1,1},{3,5},{5,2},{7,6},{9,9},{11,13},{13,10},{15,14},{17,17},{19,... | collective-permute-start | bytes 1572872 | tf_op jit(solution)/shard_map/ppermute | solution.py:405
  51.2 25.3 %collective-permute-start.8 = (f32[8,64,256]{2,1,0:T(8,128)}, f32[8,64,256]{2,1,0:T(8,128)}, u32[]{:S(2)}, u32[]{:S(2)}) collective-permute-start(f32[8,64,256]{2,1,0:T(8,128)} %shard_map.113.rest_0_), channel_id=1, source_target_pairs={{0,1},{2,5},{4,2},{6,6},{8,9},{10,13},{12,10},{14,14},{16,17},{18,... | collective-permute-start | bytes 1572872 | tf_op jit(solution)/shard_map/ppermute | solution.py:405
  61.6 15.0 %collective-permute-start.11 = (f32[8,64,256]{2,1,0:T(8,128)}, f32[8,64,256]{2,1,0:T(8,128)}, u32[]{:S(2)}, u32[]{:S(2)}) collective-permute-start(f32[8,64,256]{2,1,0:T(8,128)} %shard_map.114.rest_1_), channel_id=1, source_target_pairs={{3,1},{1,5},{7,2},{5,6},{11,9},{9,13},{15,10},{13,14},{19,17},{17,... | collective-permute-start | bytes 1572872 | tf_op jit(solution)/shard_map/ppermute | solution.py:405
  63.0 18.4 %collective-permute-start.10 = (f32[8,64,256]{2,1,0:T(8,128)}, f32[8,64,256]{2,1,0:T(8,128)}, u32[]{:S(2)}, u32[]{:S(2)}) collective-permute-start(f32[8,64,256]{2,1,0:T(8,128)} %shard_map.114.rest_1_), channel_id=1, source_target_pairs={{2,1},{0,5},{6,2},{4,6},{10,9},{8,13},{14,10},{12,14},{18,17},{16,... | collective-permute-start | bytes 1572872 | tf_op jit(solution)/shard_map/ppermute | solution.py:405
  66.2 5.8 %collective-permute-start.15 = (f32[272,256]{1,0:T(8,128)}, f32[272,256]{1,0:T(8,128)}, u32[]{:S(2)}, u32[]{:S(2)}) collective-permute-start(f32[272,256]{1,0:T(8,128)} %get-tuple-element.36.own), channel_id=1, source_target_pairs={{1,9},{2,10},{9,1},{10,2},{17,25},{18,26},{25,17},{26,18}} | collective-permute-start | bytes 835592 | tf_op jit(solution)/shard_map/ppermute | solution.py:429
  74.2 0.9 collective-permute-start.16
  87.7 4.6 %collective-permute-start.17 = (f32[512,256]{1,0:T(8,128)S(1)}, f32[512,256]{1,0:T(8,128)S(1)}, u32[]{:S(2)}, u32[]{:S(2)}) collective-permute-start(f32[512,256]{1,0:T(8,128)S(1)} %get-tuple-element.39.own), channel_id=1, source_target_pairs={{5,1},{6,2},{13,9},{14,10},{21,17},{22,18},{29,25},{30,26}} | collective-permute-start | bytes 1572872 | tf_op jit(solution)/shard_map/ppermute | solution.py:429
  88.4 0.7 collective-permute-start.18
  93.0 2.3 %collective-permute-start.20 = (f32[512,256]{1,0:T(8,128)S(1)}, f32[512,256]{1,0:T(8,128)S(1)}, u32[]{:S(2)}, u32[]{:S(2)}) collective-permute-start(f32[512,256]{1,0:T(8,128)S(1)} %shard_map.128), channel_id=1, source_target_pairs={{1,2},{2,1},{9,10},{10,9},{17,18},{18,17},{25,26},{26,25}} | collective-permute-start | bytes 1572872 | tf_op jit(solution)/shard_map/ppermute | solution.py:429
  93.7 0.7 collective-permute-start.19
  94.6 0.8 collective-permute-start.21
  96.1 0.7 collective-permute-start.22
  98.3 1.5 collective-permute-start.23
  100.5 0.7 collective-permute-start.24
  104.5 59.2 %collective-permute-start.25 = (f32[520,256]{1,0:T(8,128)S(1)}, f32[520,256]{1,0:T(8,128)S(1)}, u32[]{:S(2)}, u32[]{:S(2)}) collective-permute-start(f32[520,256]{1,0:T(8,128)S(1)} %get-tuple-element.46), channel_id=1, source_target_pairs={{1,0},{5,2},{2,4},{6,6},{9,8},{13,10},{10,12},{14,14},{17,16},{21,... | collective-permute-start | bytes 1597448 | tf_op jit(solution)/shard_map/ppermute | solution.py:414
  105.8 58.0 %collective-permute-start.26 = (f32[520,256]{1,0:T(8,128)S(1)}, f32[520,256]{1,0:T(8,128)S(1)}, u32[]{:S(2)}, u32[]{:S(2)}) collective-permute-start(f32[520,256]{1,0:T(8,128)S(1)} %get-tuple-element.47), channel_id=1, source_target_pairs={{1,1},{5,3},{2,5},{6,7},{9,9},{13,11},{10,13},{14,15},{17,17},{21,... | collective-permute-start | bytes 1597448 | tf_op jit(solution)/shard_map/ppermute | solution.py:414
  106.5 58.9 %collective-permute-start.27 = (f32[520,256]{1,0:T(8,128)S(1)}, f32[520,256]{1,0:T(8,128)S(1)}, u32[]{:S(2)}, u32[]{:S(2)}) collective-permute-start(f32[520,256]{1,0:T(8,128)S(1)} %get-tuple-element.48), channel_id=1, source_target_pairs={{1,2},{5,0},{2,6},{6,4},{9,10},{13,8},{10,14},{14,12},{17,18},{21,... | collective-permute-start | bytes 1597448 | tf_op jit(solution)/shard_map/ppermute | solution.py:414
  107.8 57.6 %collective-permute-start.28 = (f32[520,256]{1,0:T(8,128)S(1)}, f32[520,256]{1,0:T(8,128)S(1)}, u32[]{:S(2)}, u32[]{:S(2)}) collective-permute-start(f32[520,256]{1,0:T(8,128)S(1)} %get-tuple-element.49), channel_id=1, source_target_pairs={{1,3},{5,1},{2,7},{6,5},{9,11},{13,9},{10,15},{14,13},{17,19},{21,... | collective-permute-start | bytes 1597448 | tf_op jit(solution)/shard_map/ppermute | solution.py:414
  (22 other events, 92.4 us)

commit v5 on v4

--- a/solution.py
+++ b/solution.py
@@ -245,16 +245,42 @@
         behind[...] = after[...]
 
 
-def smooth_reach(where, other, after, reached):
+def smooth_join_split(where, own, other, chain, tail):
+    width = own.shape[1]
+
+    def follow(early, latter):
+        gain = halves(early[:width])
+        chain[...] = product(gain, halves(latter[:width]), ((1,), (0,)))
+        tail[...] = carry(gain, early[width:], latter[width:])
+
+    @pl.when(where[0] == 0)
+    def _():
+        follow(own, other)
+
+    @pl.when(where[0] != 0)
+    def _():
+        follow(other, own)
+
+
+def smooth_reach(where, t1, t2, t3, c2, c13, after, reached, current):
     width = after.shape[1]
-
-    @pl.when(where[0] == 0)
-    def _():
-        reached[...] = carry(halves(after[:width]), after[width:], other[...])
-
-    @pl.when(where[0] != 0)
-    def _():
-        reached[...] = after[width:]
+    odd = where[0] != 0
+
+    def step(chain, tail):
+        current[...] = carry(halves(chain[...]), tail[...], current[...])
+
+    @pl.when(odd)
+    def _():
+        current[...] = t2[...]
+        step(c13, t3)
+
+    @pl.when(jnp.logical_not(odd))
+    def _():
+        current[...] = t3[...]
+        step(c2, t2)
+        step(c13, t1)
+
+    reached[...] = carry(halves(after[:width]), after[width:], current[...])
 
 
 def smooth_last(where, own, other, next_total, maps, covs, offsets, p0, p1, p2, p3, start):
@@ -495,20 +521,43 @@
     next_delta = swap(delta, 0, (1,))
     (delta,) = call(smooth_join_delta, [(PAD, width)])([0], first, delta, next_delta)
     behind = None
-    for level in range(1, len(levels) - 1):
+    for level in range(1, len(levels) - 2):
         arrived = swap(total, level, (0,))
         if behind is None:
             arrived = jnp.concatenate([arrived, swap(delta, level, (0,))], axis=0)
             total = jnp.concatenate([total, delta], axis=0)
         late = levels[level][1]
-        (total,) = call(smooth_join, [packed_smooth])([late], total, arrived)
+        if level == len(levels) - 3:
+            chain, tail = call(smooth_join_split, [(width, width), packed_filter])(
+                [late], total, arrived
+            )
+        else:
+            (total,) = call(smooth_join, [packed_smooth])([late], total, arrived)
         if behind is None:
             behind = jnp.where(late == 0, arrived, jnp.eye(*packed_smooth, dtype=jnp.float32))
         else:
             (behind,) = call(smooth_behind, [packed_smooth])([late], arrived, behind)
     next_total = jnp.concatenate([next_cov, next_delta], axis=0)
-    arrived = swap(total[width:], len(levels) - 1, (0,))
-    (reached,) = call(smooth_reach, [packed_filter])([levels[-1][1]], arrived, behind)
+    quarter = tm_count // 4
+
+    def from_later(array, hops):
+        pairs = [
+            (place(t, z), place(t - (source - target) * quarter, z))
+            for t in range(0, tm_count, 2)
+            for z in (1, 2)
+            for source, target in hops
+            if t // quarter == source
+        ]
+        return lax.ppermute(array, BOTH, pairs)
+
+    tail3 = from_later(tail, ((3, 0), (2, 1)))
+    tail2 = from_later(tail, ((3, 1), (2, 0)))
+    chain2 = from_later(chain, ((2, 0),))
+    chain13 = from_later(chain, ((2, 1), (1, 0)))
+    tail1 = from_later(tail, ((3, 2), (1, 0)))
+    (reached,) = call(smooth_reach, [packed_filter], [packed_filter])(
+        [(tm // quarter) % 2], tail1, tail2, tail3, chain2, chain13, behind
+    )
     piece = (steps * row_count + steps, width)
     pieces = call(smooth_last, [piece] * 4, [packed_filter])(
         [half], reached, swap(reached, 0, (0,)), next_total, maps, covs, offsets

time: 169 us -> 168 us (level)
  waiting for transfers between devices: 70.8 us -> 63.9 us
  starting transfers between devices: 55 us -> 60 us
  Pallas kernels: 33.6 us -> 35.4 us
    ppermute x4, waiting for transfers between devices: 56.9 us -> 50.1 us  [from_workers(): return lax.ppermute(array, BOTH, route)]
    ppermute x0 -> x5, starting transfers between devices: none -> 6.14 us  [from_later(): return lax.ppermute(array, BOTH, pairs)]
    pallas_call x23 -> x21, Pallas kernels: 33.6 us -> 35.4 us  [run(): pl.pallas_call(body, out_shape=[jax.ShapeDtypeStruct(shape, jnp.float32)...]
    ppermute x12 -> x10, starting transfers between devices: 8.96 us -> 7.61 us  [swap(): return lax.ppermute(array, BOTH, route)]
    unnamed x52 -> x48, local copies, waits for them, and re-layouts: 3.87 us -> 3.86 us
  transfers between devices with their start and end apart: 29 -> 32, of which waited for: 6 -> 6; matrix products, arithmetic and copies ran while one was open for 1% -> 1% of each run, Pallas kernels for 11% -> 11%
where the time goes in v5:
time: 168 us; the launch traced here: 166 us
  waiting for transfers between devices  63.9 us (38%)
  starting transfers between devices  60 us (36%)
  Pallas kernels  35.4 us (21%)
  local copies, waits for them, and re-layouts  4.59 us (3%)
    ppermute x4, waiting for transfers between devices, from_workers(): return lax.ppermute(array, BOTH, route)  50.1 us
    ppermute x12, starting transfers between devices, to_workers(): return lax.ppermute(array, BOTH, pairs)  42.2 us
    pallas_call x21, Pallas kernels, run(): pl.pallas_call(body, out_shape=[jax.ShapeDtypeStruct(shape, jnp.float32)...  35.4 us
    ppermute x12, waiting for transfers between devices, to_workers(): return lax.ppermute(array, BOTH, pairs)  13.7 us
    ppermute x10, starting transfers between devices, swap(): return lax.ppermute(array, BOTH, route)  7.61 us
    ppermute x5, starting transfers between devices, from_later(): return lax.ppermute(array, BOTH, pairs)  6.14 us
    ppermute x4, starting transfers between devices, from_workers(): return lax.ppermute(array, BOTH, route)  3.97 us
    unnamed x48, local copies, waits for them, and re-layouts  3.86 us
  transfers between devices with their start and end apart: 32, of which 6 were waited for; matrix products, arithmetic and copies ran while one was open for 1% of the time, Pallas kernels for 11%

profile of v5, /device:TPU:0, one launch (start us, length us, event | category | flops | bytes accessed | tf_op | source)
XLA Modules:
  0.0 166.2 jit_solution(3946166110734696663)
XLA Ops:
  2.7 1.5 collective-permute-start.1
  4.2 9.6 %collective-permute-start = (f32[8,64,256]{2,1,0:T(8,128)}, f32[8,64,256]{2,1,0:T(8,128)}, u32[]{:S(2)}, u32[]{:S(2)}) collective-permute-start(f32[8,64,256]{2,1,0:T(8,128)} %shard_map.115), channel_id=1, source_target_pairs={{0,1},{2,5},{4,2},{6,6},{8,9},{10,13},{12,10},{14,14},{16,17},{18,... | collective-permute-start | bytes 1572872 | tf_op jit(solution)/shard_map/ppermute | solution.py:431
  14.6 1.5 collective-permute-start.3
  16.1 2.6 %collective-permute-start.2 = (f32[8,64,256]{2,1,0:T(8,128)}, f32[8,64,256]{2,1,0:T(8,128)}, u32[]{:S(2)}, u32[]{:S(2)}) collective-permute-start(f32[8,64,256]{2,1,0:T(8,128)} %shard_map.116), channel_id=1, source_target_pairs={{2,1},{0,5},{6,2},{4,6},{10,9},{8,13},{14,10},{12,14},{18,17},{16,... | collective-permute-start | bytes 1572872 | tf_op jit(solution)/shard_map/ppermute | solution.py:431
  22.4 1.3 collective-permute-start.6
  26.3 9.0 %collective-permute-start.12 = (f32[8,64,256]{2,1,0:T(8,128)S(1)}, f32[8,64,256]{2,1,0:T(8,128)S(1)}, u32[]{:S(2)}, u32[]{:S(2)}) collective-permute-start(f32[8,64,256]{2,1,0:T(8,128)S(1)} %shard_map.120), channel_id=1, source_target_pairs={{2,1},{0,5},{6,2},{4,6},{10,9},{8,13},{14,10},{12,14},{18,17},{16,... | collective-permute-start | bytes 1572872 | tf_op jit(solution)/shard_map/ppermute | solution.py:431
  35.4 1.5 collective-permute-done.2.k2
  36.9 4.5 %shard_map.117 = (f32[272,256]{1,0:T(8,128)S(1)}, f32[8,256,256]{2,1,0:T(8,128)S(1)}, f32[8,256]{1,0:T(8,128)S(1)}) custom-call(s32[1]{0:T(128)} %bitcast.1.where, f32[8,64,256]{2,1,0:T(8,128)} %collective-permute-done.k0, f32[8,64,256]{2,1,0:T(8,128)} %collective-permute-done.1.k1, f32[8,64,256]{2,1,0:T(8,128)} %collective-permute-done.2.k2, ...), custom_call_target="tpu_custom_call" | custom-call | tf_op jit(solution)/shard_map/pallas_call | solution.py:378
  42.1 6.0 %collective-permute-done.6.rest_0_.f0 = f32[8,64,256]{2,1,0:T(8,128)S(1)} collective-permute-done((f32[8,64,256]{2,1,0:T(8,128)S(1)}, f32[8,64,256]{2,1,0:T(8,128)S(1)}, u32[]{:S(2)}, u32[]{:S(2)}) %collective-permute-start.6) | collective-permute-done | bytes 524320 | tf_op jit(solution)/shard_map/ppermute | solution.py:431
  49.7 1.5 collective-permute-start.9
  51.2 10.3 %collective-permute-start.8 = (f32[8,64,256]{2,1,0:T(8,128)}, f32[8,64,256]{2,1,0:T(8,128)}, u32[]{:S(2)}, u32[]{:S(2)}) collective-permute-start(f32[8,64,256]{2,1,0:T(8,128)} %shard_map.113.rest_0_), channel_id=1, source_target_pairs={{0,1},{2,5},{4,2},{6,6},{8,9},{10,13},{12,10},{14,14},{16,17},{18,... | collective-permute-start | bytes 1572872 | tf_op jit(solution)/shard_map/ppermute | solution.py:431
  61.5 1.5 collective-permute-start.11
  63.0 2.1 %collective-permute-start.10 = (f32[8,64,256]{2,1,0:T(8,128)}, f32[8,64,256]{2,1,0:T(8,128)}, u32[]{:S(2)}, u32[]{:S(2)}) collective-permute-start(f32[8,64,256]{2,1,0:T(8,128)} %shard_map.114.rest_1_), channel_id=1, source_target_pairs={{2,1},{0,5},{6,2},{4,6},{10,9},{8,13},{14,10},{12,14},{18,17},{16,... | collective-permute-start | bytes 1572872 | tf_op jit(solution)/shard_map/ppermute | solution.py:431
  66.2 1.4 collective-permute-start.15
  69.8 2.1 %shard_map.122 = (f32[8,256,256]{2,1,0:T(8,128)S(1)}, f32[8,256,256]{2,1,0:T(8,128)S(1)}) custom-call(s32[1]{0:T(128)} %bitcast.1.where, f32[8,64,256]{2,1,0:T(8,128)S(1)} %collective-permute-done.6.rest_0_.f0, f32[8,64,256]{2,1,0:T(8,128)S(1)} %collective-permute-done.7.rest_1_.f1, f32[8,64,256]{2,1,0:T(8,128)S(1)} %copy-done.11, ...), custom_call_target="tpu_custom_call" | custom-call | tf_op jit(solution)/shard_map/pallas_call | solution.py:378
  72.0 2.1 %shard_map.123 = (f32[272,256]{1,0:T(8,128)}, f32[16,256]{1,0:T(8,128)S(1)}) custom-call(s32[1]{0:T(128)} %bitcast.2.where, f32[272,256]{1,0:T(8,128)} %get-tuple-element.38.own, f32[272,256]{1,0:T(8,128)} %collective-permute-done.15.other.rest_0_, f32[1,256]{1,0:T(1,128)S(1)} %bitcast.24, f32[8,256,256]{2,1,0:T(8,128)S(1)} %copy-done.1, ...), custom_call_target="tpu_custom_call" | custom-call | tf_op jit(solution)/shard_map/pallas_call | solution.py:378
  75.1 1.4 shard_map.124
  76.5 4.9 %collective-permute-done.10.g2 = f32[8,64,256]{2,1,0:T(8,128)} collective-permute-done((f32[8,64,256]{2,1,0:T(8,128)}, f32[8,64,256]{2,1,0:T(8,128)}, u32[]{:S(2)}, u32[]{:S(2)}) %collective-permute-start.10) | collective-permute-done | bytes 524320 | tf_op jit(solution)/shard_map/ppermute | solution.py:431
  81.5 6.2 %shard_map.125 = (f32[512,256]{1,0:T(8,128)S(1)}, f32[8,256,256]{2,1,0:T(8,128)S(1)}, f32[8,256,256]{2,1,0:T(8,128)S(1)}) custom-call(s32[2]{0:T(128)S(1)} %pad_add_fusion.where, f32[8,64,256]{2,1,0:T(8,128)} %collective-permute-done.8.g0, f32[8,64,256]{2,1,0:T(8,128)} %collective-permute-done.9.g1, ...), custom_call_target="tpu_custom_call", output_to_operand_aliasing={{1}: (6, {}), {2}: (5, {})} | custom-call | tf_op jit(solution)/shard_map/pallas_call | solution.py:378
  89.5 2.8 %shard_map.127 = (f32[8,256]{1,0:T(8,128)S(1)}, f32[16,256]{1,0:T(8,128)S(1)}) custom-call(s32[2]{0:T(128)S(1)} %pad_add_fusion.where, f32[8,64,256]{2,1,0:T(8,128)} %collective-permute-done.8.g0, f32[8,64,256]{2,1,0:T(8,128)} %collective-permute-done.9.g1, f32[8,64,256]{2,1,0:T(8,128)} %collective-permute-done.10.g2, ...), custom_call_target="tpu_custom_call" | custom-call | tf_op jit(solution)/shard_map/pallas_call | solution.py:378
  95.3 1.6 shard_map.130
  97.6 1.4 collective-permute-start.23
  99.0 1.4 collective-permute-start.22
  100.3 1.4 collective-permute-start.26
  101.7 1.4 collective-permute-start.25
  103.1 3.2 %shard_map.131.own = f32[272,256]{1,0:T(8,128)S(1)} custom-call(s32[1]{0:T(128)} %bitcast.2.where, f32[272,256]{1,0:T(8,128)} %collective-permute-done.22.t1, f32[272,256]{1,0:T(8,128)} %collective-permute-done.23.t2, f32[272,256]{1,0:T(8,128)S(1)} %collective-permute-done.24.t3, f32[256,256]{1,0:T(8,128)} %collective-permute-done.25.c2, ...), custom_call_target="tpu_custom_call" | custom-call | tf_op jit(solution)/shard_map/pallas_call | solution.py:378
  107.1 3.2 %shard_map.132 = (f32[520,256]{1,0:T(8,128)S(1)}, f32[520,256]{1,0:T(8,128)S(1)}, f32[520,256]{1,0:T(8,128)S(1)}, f32[520,256]{1,0:T(8,128)S(1)}) custom-call(s32[1]{0:T(128)} %bitcast.1.where, f32[272,256]{1,0:T(8,128)S(1)} %shard_map.131.own, f32[272,256]{1,0:T(8,128)S(1)} %collective-permute-done.27.other, f32[528,256]{1,0:T(8,128)S(1)} %pad_maximum_fusion.1.next_total, ...), custom_call_target="tpu_custom_call" | custom-call | tf_op jit(solution)/shard_map/pallas_call | solution.py:378
  110.2 1.3 collective-permute-start.28
  112.2 1.3 collective-permute-start.30
  114.2 48.3 %collective-permute-done.28.a0 = f32[520,256]{1,0:T(8,128)S(1)} collective-permute-done((f32[520,256]{1,0:T(8,128)S(1)}, f32[520,256]{1,0:T(8,128)S(1)}, u32[]{:S(2)}, u32[]{:S(2)}) %collective-permute-start.28) | collective-permute-done | bytes 532512 | tf_op jit(solution)/shard_map/ppermute | solution.py:440
  162.6 1.8 %collective-permute-done.30.a2 = f32[520,256]{1,0:T(8,128)S(1)} collective-permute-done((f32[520,256]{1,0:T(8,128)S(1)}, f32[520,256]{1,0:T(8,128)S(1)}, u32[]{:S(2)}, u32[]{:S(2)}) %collective-permute-start.30) | collective-permute-done | bytes 532512 | tf_op jit(solution)/shard_map/ppermute | solution.py:440
  164.4 1.6 shard_map.133
  (122 shorter events, 23.4 us)
Async XLA Ops:
  2.7 19.7 %collective-permute-start.1 = (f32[8,64,256]{2,1,0:T(8,128)}, f32[8,64,256]{2,1,0:T(8,128)}, u32[]{:S(2)}, u32[]{:S(2)}) collective-permute-start(f32[8,64,256]{2,1,0:T(8,128)} %shard_map.115), channel_id=1, source_target_pairs={{1,1},{3,5},{5,2},{7,6},{9,9},{11,13},{13,10},{15,14},{17,17},{19,... | collective-permute-start | bytes 1572872 | tf_op jit(solution)/shard_map/ppermute | solution.py:431
  4.2 21.5 %collective-permute-start = (f32[8,64,256]{2,1,0:T(8,128)}, f32[8,64,256]{2,1,0:T(8,128)}, u32[]{:S(2)}, u32[]{:S(2)}) collective-permute-start(f32[8,64,256]{2,1,0:T(8,128)} %shard_map.115), channel_id=1, source_target_pairs={{0,1},{2,5},{4,2},{6,6},{8,9},{10,13},{12,10},{14,14},{16,17},{18,... | collective-permute-start | bytes 1572872 | tf_op jit(solution)/shard_map/ppermute | solution.py:431
  14.6 11.7 %collective-permute-start.3 = (f32[8,64,256]{2,1,0:T(8,128)}, f32[8,64,256]{2,1,0:T(8,128)}, u32[]{:S(2)}, u32[]{:S(2)}) collective-permute-start(f32[8,64,256]{2,1,0:T(8,128)} %shard_map.116), channel_id=1, source_target_pairs={{3,1},{1,5},{7,2},{5,6},{11,9},{9,13},{15,10},{13,14},{19,17},{17,... | collective-permute-start | bytes 1572872 | tf_op jit(solution)/shard_map/ppermute | solution.py:431
  16.1 20.8 %collective-permute-start.2 = (f32[8,64,256]{2,1,0:T(8,128)}, f32[8,64,256]{2,1,0:T(8,128)}, u32[]{:S(2)}, u32[]{:S(2)}) collective-permute-start(f32[8,64,256]{2,1,0:T(8,128)} %shard_map.116), channel_id=1, source_target_pairs={{2,1},{0,5},{6,2},{4,6},{10,9},{8,13},{14,10},{12,14},{18,17},{16,... | collective-permute-start | bytes 1572872 | tf_op jit(solution)/shard_map/ppermute | solution.py:431
  18.7 3.0 %collective-permute-start.4 = (f32[16,256]{1,0:T(8,128)S(1)}, f32[16,256]{1,0:T(8,128)S(1)}, u32[]{:S(2)}, u32[]{:S(2)}) collective-permute-start(f32[16,256]{1,0:T(8,128)S(1)} %copy-done.20), channel_id=1, source_target_pairs={{0,4},{4,0},{8,12},{12,8},{16,20},{20,16},{24,28},{28,24},{1,5},{5... | collective-permute-start | bytes 49160 | tf_op jit(solution)/shard_map/ppermute | solution.py:457
  21.7 20.3 %collective-permute-start.7 = (f32[8,64,256]{2,1,0:T(8,128)S(1)}, f32[8,64,256]{2,1,0:T(8,128)S(1)}, u32[]{:S(2)}, u32[]{:S(2)}) collective-permute-start(f32[8,64,256]{2,1,0:T(8,128)S(1)} %shard_map.118), channel_id=1, source_target_pairs={{1,1},{3,5},{5,2},{7,6},{9,9},{11,13},{13,10},{15,14},{17,17},{19,... | collective-permute-start | bytes 1572872 | tf_op jit(solution)/shard_map/ppermute | solution.py:431
  22.4 25.6 %collective-permute-start.6 = (f32[8,64,256]{2,1,0:T(8,128)S(1)}, f32[8,64,256]{2,1,0:T(8,128)S(1)}, u32[]{:S(2)}, u32[]{:S(2)}) collective-permute-start(f32[8,64,256]{2,1,0:T(8,128)S(1)} %shard_map.118), channel_id=1, source_target_pairs={{0,1},{2,5},{4,2},{6,6},{8,9},{10,13},{12,10},{14,14},{16,17},{18,... | collective-permute-start | bytes 1572872 | tf_op jit(solution)/shard_map/ppermute | solution.py:431
  25.6 35.9 %collective-permute-start.13 = (f32[8,64,256]{2,1,0:T(8,128)S(1)}, f32[8,64,256]{2,1,0:T(8,128)S(1)}, u32[]{:S(2)}, u32[]{:S(2)}) collective-permute-start(f32[8,64,256]{2,1,0:T(8,128)S(1)} %shard_map.120), channel_id=1, source_target_pairs={{3,1},{1,5},{7,2},{5,6},{11,9},{9,13},{15,10},{13,14},{19,17},{17,... | collective-permute-start | bytes 1572872 | tf_op jit(solution)/shard_map/ppermute | solution.py:431
  26.3 36.7 %collective-permute-start.12 = (f32[8,64,256]{2,1,0:T(8,128)S(1)}, f32[8,64,256]{2,1,0:T(8,128)S(1)}, u32[]{:S(2)}, u32[]{:S(2)}) collective-permute-start(f32[8,64,256]{2,1,0:T(8,128)S(1)} %shard_map.120), channel_id=1, source_target_pairs={{2,1},{0,5},{6,2},{4,6},{10,9},{8,13},{14,10},{12,14},{18,17},{16,... | collective-permute-start | bytes 1572872 | tf_op jit(solution)/shard_map/ppermute | solution.py:431
  41.4 6.7 %collective-permute-start.5 = (f32[272,256]{1,0:T(8,128)S(1)}, f32[272,256]{1,0:T(8,128)S(1)}, u32[]{:S(2)}, u32[]{:S(2)}) collective-permute-start(f32[272,256]{1,0:T(8,128)S(1)} %get-tuple-element.29.own), channel_id=1, source_target_pairs={{5,1},{6,2},{13,9},{14,10},{21,17},{22,18},{29,25},{30,26}} | collective-permute-start | bytes 835592 | tf_op jit(solution)/shard_map/ppermute | solution.py:455
  49.1 16.0 %collective-permute-start.14 = (f32[272,256]{1,0:T(8,128)S(1)}, f32[272,256]{1,0:T(8,128)S(1)}, u32[]{:S(2)}, u32[]{:S(2)}) collective-permute-start(f32[272,256]{1,0:T(8,128)S(1)} %get-tuple-element.34.own), channel_id=1, source_target_pairs={{1,2},{2,1},{9,10},{10,9},{17,18},{18,17},{25,26},{26,25}} | collective-permute-start | bytes 835592 | tf_op jit(solution)/shard_map/ppermute | solution.py:455
  49.7 26.7 %collective-permute-start.9 = (f32[8,64,256]{2,1,0:T(8,128)}, f32[8,64,256]{2,1,0:T(8,128)}, u32[]{:S(2)}, u32[]{:S(2)}) collective-permute-start(f32[8,64,256]{2,1,0:T(8,128)} %shard_map.113.rest_0_), channel_id=1, source_target_pairs={{1,1},{3,5},{5,2},{7,6},{9,9},{11,13},{13,10},{15,14},{17,17},{19,... | collective-permute-start | bytes 1572872 | tf_op jit(solution)/shard_map/ppermute | solution.py:431
  51.2 25.3 %collective-permute-start.8 = (f32[8,64,256]{2,1,0:T(8,128)}, f32[8,64,256]{2,1,0:T(8,128)}, u32[]{:S(2)}, u32[]{:S(2)}) collective-permute-start(f32[8,64,256]{2,1,0:T(8,128)} %shard_map.113.rest_0_), channel_id=1, source_target_pairs={{0,1},{2,5},{4,2},{6,6},{8,9},{10,13},{12,10},{14,14},{16,17},{18,... | collective-permute-start | bytes 1572872 | tf_op jit(solution)/shard_map/ppermute | solution.py:431
  61.5 15.0 %collective-permute-start.11 = (f32[8,64,256]{2,1,0:T(8,128)}, f32[8,64,256]{2,1,0:T(8,128)}, u32[]{:S(2)}, u32[]{:S(2)}) collective-permute-start(f32[8,64,256]{2,1,0:T(8,128)} %shard_map.114.rest_1_), channel_id=1, source_target_pairs={{3,1},{1,5},{7,2},{5,6},{11,9},{9,13},{15,10},{13,14},{19,17},{17,... | collective-permute-start | bytes 1572872 | tf_op jit(solution)/shard_map/ppermute | solution.py:431
  63.0 18.4 %collective-permute-start.10 = (f32[8,64,256]{2,1,0:T(8,128)}, f32[8,64,256]{2,1,0:T(8,128)}, u32[]{:S(2)}, u32[]{:S(2)}) collective-permute-start(f32[8,64,256]{2,1,0:T(8,128)} %shard_map.114.rest_1_), channel_id=1, source_target_pairs={{2,1},{0,5},{6,2},{4,6},{10,9},{8,13},{14,10},{12,14},{18,17},{16,... | collective-permute-start | bytes 1572872 | tf_op jit(solution)/shard_map/ppermute | solution.py:431
  66.2 5.8 %collective-permute-start.15 = (f32[272,256]{1,0:T(8,128)}, f32[272,256]{1,0:T(8,128)}, u32[]{:S(2)}, u32[]{:S(2)}) collective-permute-start(f32[272,256]{1,0:T(8,128)} %get-tuple-element.38.own), channel_id=1, source_target_pairs={{1,9},{2,10},{9,1},{10,2},{17,25},{18,26},{25,17},{26,18}} | collective-permute-start | bytes 835592 | tf_op jit(solution)/shard_map/ppermute | solution.py:455
  74.1 0.9 collective-permute-start.16
  87.6 4.6 %collective-permute-start.17 = (f32[512,256]{1,0:T(8,128)S(1)}, f32[512,256]{1,0:T(8,128)S(1)}, u32[]{:S(2)}, u32[]{:S(2)}) collective-permute-start(f32[512,256]{1,0:T(8,128)S(1)} %get-tuple-element.41.own), channel_id=1, source_target_pairs={{5,1},{6,2},{13,9},{14,10},{21,17},{22,18},{29,25},{30,26}} | collective-permute-start | bytes 1572872 | tf_op jit(solution)/shard_map/ppermute | solution.py:455
  88.4 0.7 collective-permute-start.18
  93.0 2.3 %collective-permute-start.20 = (f32[512,256]{1,0:T(8,128)S(1)}, f32[512,256]{1,0:T(8,128)S(1)}, u32[]{:S(2)}, u32[]{:S(2)}) collective-permute-start(f32[512,256]{1,0:T(8,128)S(1)} %shard_map.128), channel_id=1, source_target_pairs={{1,2},{2,1},{9,10},{10,9},{17,18},{18,17},{25,26},{26,25}} | collective-permute-start | bytes 1572872 | tf_op jit(solution)/shard_map/ppermute | solution.py:455
  93.7 0.7 collective-permute-start.19
  94.5 0.8 collective-permute-start.21
  96.9 6.2 %collective-permute-start.24 = (f32[272,256]{1,0:T(8,128)}, f32[272,256]{1,0:T(8,128)S(1)}, u32[]{:S(2)}, u32[]{:S(2)}) collective-permute-start(f32[272,256]{1,0:T(8,128)} %get-tuple-element.46), channel_id=1, source_target_pairs={{17,9},{18,10},{25,1},{26,2}} | collective-permute-start | bytes 835592 | tf_op jit(solution)/shard_map/ppermute | solution.py:551
  97.6 5.6 %collective-permute-start.23 = (f32[272,256]{1,0:T(8,128)}, f32[272,256]{1,0:T(8,128)}, u32[]{:S(2)}, u32[]{:S(2)}) collective-permute-start(f32[272,256]{1,0:T(8,128)} %get-tuple-element.46), channel_id=1, source_target_pairs={{17,1},{18,2},{25,9},{26,10}} | collective-permute-start | bytes 835592 | tf_op jit(solution)/shard_map/ppermute | solution.py:551
  99.0 4.2 %collective-permute-start.22 = (f32[272,256]{1,0:T(8,128)}, f32[272,256]{1,0:T(8,128)}, u32[]{:S(2)}, u32[]{:S(2)}) collective-permute-start(f32[272,256]{1,0:T(8,128)} %get-tuple-element.46), channel_id=1, source_target_pairs={{9,1},{10,2},{25,17},{26,18}} | collective-permute-start | bytes 835592 | tf_op jit(solution)/shard_map/ppermute | solution.py:551
  100.3 2.8 %collective-permute-start.26 = (f32[256,256]{1,0:T(8,128)}, f32[256,256]{1,0:T(8,128)}, u32[]{:S(2)}, u32[]{:S(2)}) collective-permute-start(f32[256,256]{1,0:T(8,128)} %get-tuple-element.47), channel_id=1, source_target_pairs={{9,1},{10,2},{17,9},{18,10}} | collective-permute-start | bytes 786440 | tf_op jit(solution)/shard_map/ppermute | solution.py:551
  101.7 1.4 collective-permute-start.25
  106.3 0.7 collective-permute-start.27
  110.2 52.3 %collective-permute-start.28 = (f32[520,256]{1,0:T(8,128)S(1)}, f32[520,256]{1,0:T(8,128)S(1)}, u32[]{:S(2)}, u32[]{:S(2)}) collective-permute-start(f32[520,256]{1,0:T(8,128)S(1)} %get-tuple-element.50), channel_id=1, source_target_pairs={{1,0},{5,2},{2,4},{6,6},{9,8},{13,10},{10,12},{14,14},{17,16},{21,... | collective-permute-start | bytes 1597448 | tf_op jit(solution)/shard_map/ppermute | solution.py:440
  111.5 51.0 %collective-permute-start.29 = (f32[520,256]{1,0:T(8,128)S(1)}, f32[520,256]{1,0:T(8,128)S(1)}, u32[]{:S(2)}, u32[]{:S(2)}) collective-permute-start(f32[520,256]{1,0:T(8,128)S(1)} %get-tuple-element.51), channel_id=1, source_target_pairs={{1,1},{5,3},{2,5},{6,7},{9,9},{13,11},{10,13},{14,15},{17,17},{21,... | collective-permute-start | bytes 1597448 | tf_op jit(solution)/shard_map/ppermute | solution.py:440
  112.2 52.1 %collective-permute-start.30 = (f32[520,256]{1,0:T(8,128)S(1)}, f32[520,256]{1,0:T(8,128)S(1)}, u32[]{:S(2)}, u32[]{:S(2)}) collective-permute-start(f32[520,256]{1,0:T(8,128)S(1)} %get-tuple-element.52), channel_id=1, source_target_pairs={{1,2},{5,0},{2,6},{6,4},{9,10},{13,8},{10,14},{14,12},{17,18},{21,... | collective-permute-start | bytes 1597448 | tf_op jit(solution)/shard_map/ppermute | solution.py:440
  113.5 50.8 %collective-permute-start.31 = (f32[520,256]{1,0:T(8,128)S(1)}, f32[520,256]{1,0:T(8,128)S(1)}, u32[]{:S(2)}, u32[]{:S(2)}) collective-permute-start(f32[520,256]{1,0:T(8,128)S(1)} %get-tuple-element.53), channel_id=1, source_target_pairs={{1,3},{5,1},{2,7},{6,5},{9,11},{13,9},{10,15},{14,13},{17,19},{21,... | collective-permute-start | bytes 1597448 | tf_op jit(solution)/shard_map/ppermute | solution.py:440
  (23 other events, 166.0 us)

commit v6 on v5

--- a/solution.py
+++ b/solution.py
@@ -88,8 +88,8 @@
     return moved[:width], moved[width:] + late_shift
 
 
-def filter_join(where, own, other, initial, *rest):
-    total, state = rest[-2:]
+def filter_join(where, own, other, *rest):
+    total = rest[-1]
     width = own.shape[1]
 
     def follow(early, latter):
@@ -105,7 +105,22 @@
     def _():
         follow(other, own)
 
-    state[...] = mm(rows_of(initial[...]), total[:width]) + total[width:]
+
+def filter_ahead(where, own, other, initial, *rest):
+    state = rest[-1]
+    width = own.shape[1]
+
+    def follow(early, latter):
+        moved = mm(rows_of(initial[...]), early[:width]) + early[width:]
+        state[...] = mm(moved, latter[:width]) + latter[width:]
+
+    @pl.when(where[0] == 0)
+    def _():
+        follow(own, other)
+
+    @pl.when(where[0] != 0)
+    def _():
+        follow(other, own)
 
 
 def filter_reach(where, state, initial, own, *rest):
@@ -479,16 +494,19 @@
     )
     total, arrived, others = chunk, swap(chunk, 0, (1,)), []
     for level in range(len(levels) - 1):
-        after = (cov_parts[:2], cov_parts)[level] if level < 2 else []
+        after = (cov_parts[:1], cov_parts)[level] if level < 2 else []
         after = after + [maps]
         if level == len(levels) - 2:
             after = after + [pred]
-        total, state = call(
-            filter_join, [packed_filter, (PAD, width)], far=range(-len(after), 0)
-        )([levels[level][1] if level else 0], total, arrived, initial, *after)
+        operands = ([levels[level][1] if level else 0], total, arrived)
+        far = range(-len(after), 0)
+        if level == len(levels) - 2:
+            (state,) = call(filter_ahead, [(PAD, width)], far=far)(*operands, initial, *after)
+        else:
+            (total,) = call(filter_join, [packed_filter], far=far)(*operands, *after)
         if level == 1:
             filt, pred = call(predict, [stack] * 2, far=[-1])(
-                [half], *cov_parts, trans_map, noise, state
+                [half], *cov_parts, trans_map, noise, total
             )
         if level:
             others.insert(0, (levels[level][1], arrived))

time: 168 us -> 167 us (level)
  Pallas kernels: 35.4 us -> 33.1 us
    pallas_call x21, Pallas kernels: 35.4 us -> 33.1 us  [run(): pl.pallas_call(body, out_shape=[jax.ShapeDtypeStruct(shape, jnp.float32)...]
  transfers between devices with their start and end apart: 32 -> 32, of which waited for: 6 -> 6; matrix products, arithmetic and copies ran while one was open for 1% -> 1% of each run, Pallas kernels for 11% -> 10%
where the time goes in v6:
time: 167 us; the launch traced here: 165 us
  waiting for transfers between devices  63.8 us (38%)
  starting transfers between devices  60.1 us (36%)
  Pallas kernels  33.1 us (20%)
  local copies, waits for them, and re-layouts  5.98 us (4%)
    ppermute x4, waiting for transfers between devices, from_workers(): return lax.ppermute(array, BOTH, route)  49.9 us
    ppermute x12, starting transfers between devices, to_workers(): return lax.ppermute(array, BOTH, pairs)  42.2 us
    pallas_call x21, Pallas kernels, run(): pl.pallas_call(body, out_shape=[jax.ShapeDtypeStruct(shape, jnp.float32)...  33.1 us
    ppermute x12, waiting for transfers between devices, to_workers(): return lax.ppermute(array, BOTH, pairs)  13.8 us
    ppermute x10, starting transfers between devices, swap(): return lax.ppermute(array, BOTH, route)  7.77 us
    ppermute x5, starting transfers between devices, from_later(): return lax.ppermute(array, BOTH, pairs)  6.15 us
    unnamed x48, local copies, waits for them, and re-layouts  5.24 us
    ppermute x4, starting transfers between devices, from_workers(): return lax.ppermute(array, BOTH, route)  3.97 us
  transfers between devices with their start and end apart: 32, of which 6 were waited for; matrix products, arithmetic and copies ran while one was open for 1% of the time, Pallas kernels for 10%

profile of v6, /device:TPU:0, one launch (start us, length us, event | category | flops | bytes accessed | tf_op | source)
XLA Modules:
  0.0 165.3 jit_solution(67703979597073394)
XLA Ops:
  2.7 1.5 collective-permute-start.1
  4.2 9.6 %collective-permute-start = (f32[8,64,256]{2,1,0:T(8,128)}, f32[8,64,256]{2,1,0:T(8,128)}, u32[]{:S(2)}, u32[]{:S(2)}) collective-permute-start(f32[8,64,256]{2,1,0:T(8,128)} %shard_map.115), channel_id=1, source_target_pairs={{0,1},{2,5},{4,2},{6,6},{8,9},{10,13},{12,10},{14,14},{16,17},{18,... | collective-permute-start | bytes 1572872 | tf_op jit(solution)/shard_map/ppermute | solution.py:446
  14.7 1.5 collective-permute-start.3
  16.1 2.5 %collective-permute-start.2 = (f32[8,64,256]{2,1,0:T(8,128)}, f32[8,64,256]{2,1,0:T(8,128)}, u32[]{:S(2)}, u32[]{:S(2)}) collective-permute-start(f32[8,64,256]{2,1,0:T(8,128)} %shard_map.116), channel_id=1, source_target_pairs={{2,1},{0,5},{6,2},{4,6},{10,9},{8,13},{14,10},{12,14},{18,17},{16,... | collective-permute-start | bytes 1572872 | tf_op jit(solution)/shard_map/ppermute | solution.py:446
  21.6 1.3 collective-permute-start.6
  24.3 1.4 collective-permute-done.k0
  26.4 9.0 %collective-permute-start.12 = (f32[8,64,256]{2,1,0:T(8,128)S(1)}, f32[8,64,256]{2,1,0:T(8,128)S(1)}, u32[]{:S(2)}, u32[]{:S(2)}) collective-permute-start(f32[8,64,256]{2,1,0:T(8,128)S(1)} %shard_map.120), channel_id=1, source_target_pairs={{2,1},{0,5},{6,2},{4,6},{10,9},{8,13},{14,10},{12,14},{18,17},{16,... | collective-permute-start | bytes 1572872 | tf_op jit(solution)/shard_map/ppermute | solution.py:446
  35.4 1.5 collective-permute-done.2.k2
  36.9 4.4 %shard_map.117 = (f32[272,256]{1,0:T(8,128)S(1)}, f32[8,256,256]{2,1,0:T(8,128)S(1)}, f32[8,256]{1,0:T(8,128)S(1)}) custom-call(s32[1]{0:T(128)} %bitcast.1.where, f32[8,64,256]{2,1,0:T(8,128)} %collective-permute-done.k0, f32[8,64,256]{2,1,0:T(8,128)} %collective-permute-done.1.k1, f32[8,64,256]{2,1,0:T(8,128)} %collective-permute-done.2.k2, ...), custom_call_target="tpu_custom_call" | custom-call | tf_op jit(solution)/shard_map/pallas_call | solution.py:393
  42.1 6.0 %collective-permute-done.6.rest_0_.f0 = f32[8,64,256]{2,1,0:T(8,128)S(1)} collective-permute-done((f32[8,64,256]{2,1,0:T(8,128)S(1)}, f32[8,64,256]{2,1,0:T(8,128)S(1)}, u32[]{:S(2)}, u32[]{:S(2)}) %collective-permute-start.6) | collective-permute-done | bytes 524320 | tf_op jit(solution)/shard_map/ppermute | solution.py:446
  49.0 1.5 collective-permute-start.8
  50.5 10.3 %collective-permute-start.7 = (f32[8,64,256]{2,1,0:T(8,128)}, f32[8,64,256]{2,1,0:T(8,128)}, u32[]{:S(2)}, u32[]{:S(2)}) collective-permute-start(f32[8,64,256]{2,1,0:T(8,128)} %shard_map.113.rest_0_), channel_id=1, source_target_pairs={{0,1},{2,5},{4,2},{6,6},{8,9},{10,13},{12,10},{14,14},{16,17},{18,... | collective-permute-start | bytes 1572872 | tf_op jit(solution)/shard_map/ppermute | solution.py:446
  60.9 1.5 collective-permute-start.10
  62.3 2.1 %collective-permute-start.9 = (f32[8,64,256]{2,1,0:T(8,128)}, f32[8,64,256]{2,1,0:T(8,128)}, u32[]{:S(2)}, u32[]{:S(2)}) collective-permute-start(f32[8,64,256]{2,1,0:T(8,128)} %shard_map.114.rest_1_), channel_id=1, source_target_pairs={{2,1},{0,5},{6,2},{4,6},{10,9},{8,13},{14,10},{12,14},{18,17},{16,... | collective-permute-start | bytes 1572872 | tf_op jit(solution)/shard_map/ppermute | solution.py:446
  65.1 1.5 collective-permute-start.15
  70.0 2.1 %shard_map.122 = (f32[8,256,256]{2,1,0:T(8,128)S(1)}, f32[8,256,256]{2,1,0:T(8,128)S(1)}) custom-call(s32[1]{0:T(128)} %bitcast.1.where, f32[8,64,256]{2,1,0:T(8,128)S(1)} %collective-permute-done.6.rest_0_.f0, f32[8,64,256]{2,1,0:T(8,128)S(1)} %copy-done.9, f32[8,64,256]{2,1,0:T(8,128)S(1)} %copy-done.13, f32[8,64,256]{2,1,0:T(8,128)S(1)} %copy-done.11, ...), custom_call_target="tpu_custom_call" | custom-call | tf_op jit(solution)/shard_map/pallas_call | solution.py:393
  72.2 1.3 shard_map.123
  74.4 1.4 shard_map.124
  75.9 4.9 %collective-permute-done.9.g2 = f32[8,64,256]{2,1,0:T(8,128)} collective-permute-done((f32[8,64,256]{2,1,0:T(8,128)}, f32[8,64,256]{2,1,0:T(8,128)}, u32[]{:S(2)}, u32[]{:S(2)}) %collective-permute-start.9) | collective-permute-done | bytes 524320 | tf_op jit(solution)/shard_map/ppermute | solution.py:446
  80.8 6.2 %shard_map.125 = (f32[512,256]{1,0:T(8,128)S(1)}, f32[8,256,256]{2,1,0:T(8,128)S(1)}, f32[8,256,256]{2,1,0:T(8,128)S(1)}) custom-call(s32[2]{0:T(128)S(1)} %pad_add_fusion.where, f32[8,64,256]{2,1,0:T(8,128)} %collective-permute-done.7.g0, f32[8,64,256]{2,1,0:T(8,128)} %collective-permute-done.8.g1, ...), custom_call_target="tpu_custom_call", output_to_operand_aliasing={{1}: (6, {}), {2}: (5, {})} | custom-call | tf_op jit(solution)/shard_map/pallas_call | solution.py:393
  88.8 2.8 %shard_map.127 = (f32[8,256]{1,0:T(8,128)S(1)}, f32[16,256]{1,0:T(8,128)S(1)}) custom-call(s32[2]{0:T(128)S(1)} %pad_add_fusion.where, f32[8,64,256]{2,1,0:T(8,128)} %collective-permute-done.7.g0, f32[8,64,256]{2,1,0:T(8,128)} %collective-permute-done.8.g1, f32[8,64,256]{2,1,0:T(8,128)} %collective-permute-done.9.g2, ...), custom_call_target="tpu_custom_call" | custom-call | tf_op jit(solution)/shard_map/pallas_call | solution.py:393
  94.7 1.6 shard_map.130
  96.9 1.4 collective-permute-start.23
  98.3 1.4 collective-permute-start.22
  99.7 1.4 collective-permute-start.26
  101.0 1.3 collective-permute-start.25
  102.5 3.2 %shard_map.131.own = f32[272,256]{1,0:T(8,128)S(1)} custom-call(s32[1]{0:T(128)} %bitcast.2.where, f32[272,256]{1,0:T(8,128)} %collective-permute-done.22.t1, f32[272,256]{1,0:T(8,128)} %collective-permute-done.23.t2, f32[272,256]{1,0:T(8,128)S(1)} %collective-permute-done.24.t3, f32[256,256]{1,0:T(8,128)} %collective-permute-done.25.c2, ...), custom_call_target="tpu_custom_call" | custom-call | tf_op jit(solution)/shard_map/pallas_call | solution.py:393
  106.4 3.2 %shard_map.132 = (f32[520,256]{1,0:T(8,128)S(1)}, f32[520,256]{1,0:T(8,128)S(1)}, f32[520,256]{1,0:T(8,128)S(1)}, f32[520,256]{1,0:T(8,128)S(1)}) custom-call(s32[1]{0:T(128)} %bitcast.1.where, f32[272,256]{1,0:T(8,128)S(1)} %shard_map.131.own, f32[272,256]{1,0:T(8,128)S(1)} %collective-permute-done.27.other, f32[528,256]{1,0:T(8,128)S(1)} %pad_maximum_fusion.1.next_total, ...), custom_call_target="tpu_custom_call" | custom-call | tf_op jit(solution)/shard_map/pallas_call | solution.py:393
  109.6 1.3 collective-permute-start.28
  113.6 48.1 %collective-permute-done.28.a0 = f32[520,256]{1,0:T(8,128)S(1)} collective-permute-done((f32[520,256]{1,0:T(8,128)S(1)}, f32[520,256]{1,0:T(8,128)S(1)}, u32[]{:S(2)}, u32[]{:S(2)}) %collective-permute-start.28) | collective-permute-done | bytes 532512 | tf_op jit(solution)/shard_map/ppermute | solution.py:455
  161.6 1.8 %collective-permute-done.30.a2 = f32[520,256]{1,0:T(8,128)S(1)} collective-permute-done((f32[520,256]{1,0:T(8,128)S(1)}, f32[520,256]{1,0:T(8,128)S(1)}, u32[]{:S(2)}, u32[]{:S(2)}) %collective-permute-start.30) | collective-permute-done | bytes 532512 | tf_op jit(solution)/shard_map/ppermute | solution.py:455
  163.5 1.6 shard_map.133
  (122 shorter events, 23.3 us)
Async XLA Ops:
  2.7 20.8 %collective-permute-start.1 = (f32[8,64,256]{2,1,0:T(8,128)}, f32[8,64,256]{2,1,0:T(8,128)}, u32[]{:S(2)}, u32[]{:S(2)}) collective-permute-start(f32[8,64,256]{2,1,0:T(8,128)} %shard_map.115), channel_id=1, source_target_pairs={{1,1},{3,5},{5,2},{7,6},{9,9},{11,13},{13,10},{15,14},{17,17},{19,... | collective-permute-start | bytes 1572872 | tf_op jit(solution)/shard_map/ppermute | solution.py:446
  4.2 21.5 %collective-permute-start = (f32[8,64,256]{2,1,0:T(8,128)}, f32[8,64,256]{2,1,0:T(8,128)}, u32[]{:S(2)}, u32[]{:S(2)}) collective-permute-start(f32[8,64,256]{2,1,0:T(8,128)} %shard_map.115), channel_id=1, source_target_pairs={{0,1},{2,5},{4,2},{6,6},{8,9},{10,13},{12,10},{14,14},{16,17},{18,... | collective-permute-start | bytes 1572872 | tf_op jit(solution)/shard_map/ppermute | solution.py:446
  14.7 11.7 %collective-permute-start.3 = (f32[8,64,256]{2,1,0:T(8,128)}, f32[8,64,256]{2,1,0:T(8,128)}, u32[]{:S(2)}, u32[]{:S(2)}) collective-permute-start(f32[8,64,256]{2,1,0:T(8,128)} %shard_map.116), channel_id=1, source_target_pairs={{3,1},{1,5},{7,2},{5,6},{11,9},{9,13},{15,10},{13,14},{19,17},{17,... | collective-permute-start | bytes 1572872 | tf_op jit(solution)/shard_map/ppermute | solution.py:446
  16.1 20.8 %collective-permute-start.2 = (f32[8,64,256]{2,1,0:T(8,128)}, f32[8,64,256]{2,1,0:T(8,128)}, u32[]{:S(2)}, u32[]{:S(2)}) collective-permute-start(f32[8,64,256]{2,1,0:T(8,128)} %shard_map.116), channel_id=1, source_target_pairs={{2,1},{0,5},{6,2},{4,6},{10,9},{8,13},{14,10},{12,14},{18,17},{16,... | collective-permute-start | bytes 1572872 | tf_op jit(solution)/shard_map/ppermute | solution.py:446
  18.6 3.0 %collective-permute-start.4 = (f32[16,256]{1,0:T(8,128)S(1)}, f32[16,256]{1,0:T(8,128)S(1)}, u32[]{:S(2)}, u32[]{:S(2)}) collective-permute-start(f32[16,256]{1,0:T(8,128)S(1)} %copy-done.20), channel_id=1, source_target_pairs={{0,4},{4,0},{8,12},{12,8},{16,20},{20,16},{24,28},{28,24},{1,5},{5... | collective-permute-start | bytes 49160 | tf_op jit(solution)/shard_map/ppermute | solution.py:472
  21.6 26.4 %collective-permute-start.6 = (f32[8,64,256]{2,1,0:T(8,128)S(1)}, f32[8,64,256]{2,1,0:T(8,128)S(1)}, u32[]{:S(2)}, u32[]{:S(2)}) collective-permute-start(f32[8,64,256]{2,1,0:T(8,128)S(1)} %shard_map.118), channel_id=1, source_target_pairs={{0,1},{2,5},{4,2},{6,6},{8,9},{10,13},{12,10},{14,14},{16,17},{18,... | collective-permute-start | bytes 1572872 | tf_op jit(solution)/shard_map/ppermute | solution.py:446
  23.6 27.0 %collective-permute-start.11 = (f32[8,64,256]{2,1,0:T(8,128)S(1)}, f32[8,64,256]{2,1,0:T(8,128)S(1)}, u32[]{:S(2)}, u32[]{:S(2)}) collective-permute-start(f32[8,64,256]{2,1,0:T(8,128)S(1)} %shard_map.118), channel_id=1, source_target_pairs={{1,1},{3,5},{5,2},{7,6},{9,9},{11,13},{13,10},{15,14},{17,17},{19,... | collective-permute-start | bytes 1572872 | tf_op jit(solution)/shard_map/ppermute | solution.py:446
  25.7 35.2 %collective-permute-start.13 = (f32[8,64,256]{2,1,0:T(8,128)S(1)}, f32[8,64,256]{2,1,0:T(8,128)S(1)}, u32[]{:S(2)}, u32[]{:S(2)}) collective-permute-start(f32[8,64,256]{2,1,0:T(8,128)S(1)} %shard_map.120), channel_id=1, source_target_pairs={{3,1},{1,5},{7,2},{5,6},{11,9},{9,13},{15,10},{13,14},{19,17},{17,... | collective-permute-start | bytes 1572872 | tf_op jit(solution)/shard_map/ppermute | solution.py:446
  26.4 35.9 %collective-permute-start.12 = (f32[8,64,256]{2,1,0:T(8,128)S(1)}, f32[8,64,256]{2,1,0:T(8,128)S(1)}, u32[]{:S(2)}, u32[]{:S(2)}) collective-permute-start(f32[8,64,256]{2,1,0:T(8,128)S(1)} %shard_map.120), channel_id=1, source_target_pairs={{2,1},{0,5},{6,2},{4,6},{10,9},{8,13},{14,10},{12,14},{18,17},{16,... | collective-permute-start | bytes 1572872 | tf_op jit(solution)/shard_map/ppermute | solution.py:446
  41.4 6.7 %collective-permute-start.5 = (f32[272,256]{1,0:T(8,128)S(1)}, f32[272,256]{1,0:T(8,128)S(1)}, u32[]{:S(2)}, u32[]{:S(2)}) collective-permute-start(f32[272,256]{1,0:T(8,128)S(1)} %get-tuple-element.25.own), channel_id=1, source_target_pairs={{5,1},{6,2},{13,9},{14,10},{21,17},{22,18},{29,25},{30,26}} | collective-permute-start | bytes 835592 | tf_op jit(solution)/shard_map/ppermute | solution.py:470
  48.3 16.1 %collective-permute-start.14 = (f32[272,256]{1,0:T(8,128)S(1)}, f32[272,256]{1,0:T(8,128)S(1)}, u32[]{:S(2)}, u32[]{:S(2)}) collective-permute-start(f32[272,256]{1,0:T(8,128)S(1)} %shard_map.119.own), channel_id=1, source_target_pairs={{1,2},{2,1},{9,10},{10,9},{17,18},{18,17},{25,26},{26,25}} | collective-permute-start | bytes 835592 | tf_op jit(solution)/shard_map/ppermute | solution.py:470
  49.0 26.8 %collective-permute-start.8 = (f32[8,64,256]{2,1,0:T(8,128)}, f32[8,64,256]{2,1,0:T(8,128)}, u32[]{:S(2)}, u32[]{:S(2)}) collective-permute-start(f32[8,64,256]{2,1,0:T(8,128)} %shard_map.113.rest_0_), channel_id=1, source_target_pairs={{1,1},{3,5},{5,2},{7,6},{9,9},{11,13},{13,10},{15,14},{17,17},{19,... | collective-permute-start | bytes 1572872 | tf_op jit(solution)/shard_map/ppermute | solution.py:446
  50.5 25.3 %collective-permute-start.7 = (f32[8,64,256]{2,1,0:T(8,128)}, f32[8,64,256]{2,1,0:T(8,128)}, u32[]{:S(2)}, u32[]{:S(2)}) collective-permute-start(f32[8,64,256]{2,1,0:T(8,128)} %shard_map.113.rest_0_), channel_id=1, source_target_pairs={{0,1},{2,5},{4,2},{6,6},{8,9},{10,13},{12,10},{14,14},{16,17},{18,... | collective-permute-start | bytes 1572872 | tf_op jit(solution)/shard_map/ppermute | solution.py:446
  60.9 15.0 %collective-permute-start.10 = (f32[8,64,256]{2,1,0:T(8,128)}, f32[8,64,256]{2,1,0:T(8,128)}, u32[]{:S(2)}, u32[]{:S(2)}) collective-permute-start(f32[8,64,256]{2,1,0:T(8,128)} %shard_map.114.rest_1_), channel_id=1, source_target_pairs={{3,1},{1,5},{7,2},{5,6},{11,9},{9,13},{15,10},{13,14},{19,17},{17,... | collective-permute-start | bytes 1572872 | tf_op jit(solution)/shard_map/ppermute | solution.py:446
  62.3 18.4 %collective-permute-start.9 = (f32[8,64,256]{2,1,0:T(8,128)}, f32[8,64,256]{2,1,0:T(8,128)}, u32[]{:S(2)}, u32[]{:S(2)}) collective-permute-start(f32[8,64,256]{2,1,0:T(8,128)} %shard_map.114.rest_1_), channel_id=1, source_target_pairs={{2,1},{0,5},{6,2},{4,6},{10,9},{8,13},{14,10},{12,14},{18,17},{16,... | collective-permute-start | bytes 1572872 | tf_op jit(solution)/shard_map/ppermute | solution.py:446
  65.1 7.0 %collective-permute-start.15 = (f32[272,256]{1,0:T(8,128)S(1)}, f32[272,256]{1,0:T(8,128)}, u32[]{:S(2)}, u32[]{:S(2)}) collective-permute-start(f32[272,256]{1,0:T(8,128)S(1)} %shard_map.121.after.own), channel_id=1, source_target_pairs={{1,9},{2,10},{9,1},{10,2},{17,25},{18,26},{25,17},{26,18}} | collective-permute-start | bytes 835592 | tf_op jit(solution)/shard_map/ppermute | solution.py:470
  73.5 0.9 collective-permute-start.16
  87.0 4.6 %collective-permute-start.17 = (f32[512,256]{1,0:T(8,128)S(1)}, f32[512,256]{1,0:T(8,128)S(1)}, u32[]{:S(2)}, u32[]{:S(2)}) collective-permute-start(f32[512,256]{1,0:T(8,128)S(1)} %get-tuple-element.33.own), channel_id=1, source_target_pairs={{5,1},{6,2},{13,9},{14,10},{21,17},{22,18},{29,25},{30,26}} | collective-permute-start | bytes 1572872 | tf_op jit(solution)/shard_map/ppermute | solution.py:470
  87.7 0.7 collective-permute-start.18
  92.3 2.3 %collective-permute-start.20 = (f32[512,256]{1,0:T(8,128)S(1)}, f32[512,256]{1,0:T(8,128)S(1)}, u32[]{:S(2)}, u32[]{:S(2)}) collective-permute-start(f32[512,256]{1,0:T(8,128)S(1)} %shard_map.128), channel_id=1, source_target_pairs={{1,2},{2,1},{9,10},{10,9},{17,18},{18,17},{25,26},{26,25}} | collective-permute-start | bytes 1572872 | tf_op jit(solution)/shard_map/ppermute | solution.py:470
  93.0 0.7 collective-permute-start.19
  93.9 0.8 collective-permute-start.21
  96.2 6.2 %collective-permute-start.24 = (f32[272,256]{1,0:T(8,128)}, f32[272,256]{1,0:T(8,128)S(1)}, u32[]{:S(2)}, u32[]{:S(2)}) collective-permute-start(f32[272,256]{1,0:T(8,128)} %get-tuple-element.38), channel_id=1, source_target_pairs={{17,9},{18,10},{25,1},{26,2}} | collective-permute-start | bytes 835592 | tf_op jit(solution)/shard_map/ppermute | solution.py:569
  96.9 5.6 %collective-permute-start.23 = (f32[272,256]{1,0:T(8,128)}, f32[272,256]{1,0:T(8,128)}, u32[]{:S(2)}, u32[]{:S(2)}) collective-permute-start(f32[272,256]{1,0:T(8,128)} %get-tuple-element.38), channel_id=1, source_target_pairs={{17,1},{18,2},{25,9},{26,10}} | collective-permute-start | bytes 835592 | tf_op jit(solution)/shard_map/ppermute | solution.py:569
  98.3 4.2 %collective-permute-start.22 = (f32[272,256]{1,0:T(8,128)}, f32[272,256]{1,0:T(8,128)}, u32[]{:S(2)}, u32[]{:S(2)}) collective-permute-start(f32[272,256]{1,0:T(8,128)} %get-tuple-element.38), channel_id=1, source_target_pairs={{9,1},{10,2},{25,17},{26,18}} | collective-permute-start | bytes 835592 | tf_op jit(solution)/shard_map/ppermute | solution.py:569
  99.7 2.8 %collective-permute-start.26 = (f32[256,256]{1,0:T(8,128)}, f32[256,256]{1,0:T(8,128)}, u32[]{:S(2)}, u32[]{:S(2)}) collective-permute-start(f32[256,256]{1,0:T(8,128)} %get-tuple-element.39), channel_id=1, source_target_pairs={{9,1},{10,2},{17,9},{18,10}} | collective-permute-start | bytes 786440 | tf_op jit(solution)/shard_map/ppermute | solution.py:569
  101.0 1.4 collective-permute-start.25
  105.6 0.7 collective-permute-start.27
  109.6 52.1 %collective-permute-start.28 = (f32[520,256]{1,0:T(8,128)S(1)}, f32[520,256]{1,0:T(8,128)S(1)}, u32[]{:S(2)}, u32[]{:S(2)}) collective-permute-start(f32[520,256]{1,0:T(8,128)S(1)} %get-tuple-element.42), channel_id=1, source_target_pairs={{1,0},{5,2},{2,4},{6,6},{9,8},{13,10},{10,12},{14,14},{17,16},{21,... | collective-permute-start | bytes 1597448 | tf_op jit(solution)/shard_map/ppermute | solution.py:455
  110.9 50.8 %collective-permute-start.29 = (f32[520,256]{1,0:T(8,128)S(1)}, f32[520,256]{1,0:T(8,128)S(1)}, u32[]{:S(2)}, u32[]{:S(2)}) collective-permute-start(f32[520,256]{1,0:T(8,128)S(1)} %get-tuple-element.43), channel_id=1, source_target_pairs={{1,1},{5,3},{2,5},{6,7},{9,9},{13,11},{10,13},{14,15},{17,17},{21,... | collective-permute-start | bytes 1597448 | tf_op jit(solution)/shard_map/ppermute | solution.py:455
  111.6 51.9 %collective-permute-start.30 = (f32[520,256]{1,0:T(8,128)S(1)}, f32[520,256]{1,0:T(8,128)S(1)}, u32[]{:S(2)}, u32[]{:S(2)}) collective-permute-start(f32[520,256]{1,0:T(8,128)S(1)} %get-tuple-element.44), channel_id=1, source_target_pairs={{1,2},{5,0},{2,6},{6,4},{9,10},{13,8},{10,14},{14,12},{17,18},{21,... | collective-permute-start | bytes 1597448 | tf_op jit(solution)/shard_map/ppermute | solution.py:455
  112.9 50.6 %collective-permute-start.31 = (f32[520,256]{1,0:T(8,128)S(1)}, f32[520,256]{1,0:T(8,128)S(1)}, u32[]{:S(2)}, u32[]{:S(2)}) collective-permute-start(f32[520,256]{1,0:T(8,128)S(1)} %get-tuple-element.45), channel_id=1, source_target_pairs={{1,3},{5,1},{2,7},{6,5},{9,11},{13,9},{10,15},{14,13},{17,19},{21,... | collective-permute-start | bytes 1597448 | tf_op jit(solution)/shard_map/ppermute | solution.py:455
  (23 other events, 130.7 us)

commit v7 on v6

--- a/solution.py
+++ b/solution.py
@@ -11,7 +11,7 @@
 highest = lax.Precision.HIGHEST
 BOTH = ("tm", "blk")
 PAD = 16
-CUTS = 4
+CUTS = 8
 SPARE = 4 * 1024 * 1024
 
 

time: 167 us -> 167 us (level)
  no operation moved by 1% of the time
where the time goes in v7:
time: 167 us; the launch traced here: 165 us
  waiting for transfers between devices  63.8 us (38%)
  starting transfers between devices  60.1 us (36%)
  Pallas kernels  33.1 us (20%)
  local copies, waits for them, and re-layouts  5.98 us (4%)
    ppermute x4, waiting for transfers between devices, from_workers(): return lax.ppermute(array, BOTH, route)  49.9 us
    ppermute x12, starting transfers between devices, to_workers(): return lax.ppermute(array, BOTH, pairs)  42.2 us
    pallas_call x21, Pallas kernels, run(): pl.pallas_call(body, out_shape=[jax.ShapeDtypeStruct(shape, jnp.float32)...  33.1 us
    ppermute x12, waiting for transfers between devices, to_workers(): return lax.ppermute(array, BOTH, pairs)  13.8 us
    ppermute x10, starting transfers between devices, swap(): return lax.ppermute(array, BOTH, route)  7.77 us
    ppermute x5, starting transfers between devices, from_later(): return lax.ppermute(array, BOTH, pairs)  6.15 us
    unnamed x48, local copies, waits for them, and re-layouts  5.24 us
    ppermute x4, starting transfers between devices, from_workers(): return lax.ppermute(array, BOTH, route)  3.97 us
  transfers between devices with their start and end apart: 32, of which 6 were waited for; matrix products, arithmetic and copies ran while one was open for 1% of the time, Pallas kernels for 10%

profile of v7, /device:TPU:0, one launch (start us, length us, event | category | flops | bytes accessed | tf_op | source)
XLA Modules:
  0.0 165.3 jit_solution(11325776179661445373)
XLA Ops:
  2.7 1.5 collective-permute-start.1
  4.2 9.6 %collective-permute-start = (f32[8,64,256]{2,1,0:T(8,128)}, f32[8,64,256]{2,1,0:T(8,128)}, u32[]{:S(2)}, u32[]{:S(2)}) collective-permute-start(f32[8,64,256]{2,1,0:T(8,128)} %shard_map.115), channel_id=1, source_target_pairs={{0,1},{2,5},{4,2},{6,6},{8,9},{10,13},{12,10},{14,14},{16,17},{18,... | collective-permute-start | bytes 1572872 | tf_op jit(solution)/shard_map/ppermute | solution.py:446
  14.7 1.5 collective-permute-start.3
  16.1 2.5 %collective-permute-start.2 = (f32[8,64,256]{2,1,0:T(8,128)}, f32[8,64,256]{2,1,0:T(8,128)}, u32[]{:S(2)}, u32[]{:S(2)}) collective-permute-start(f32[8,64,256]{2,1,0:T(8,128)} %shard_map.116), channel_id=1, source_target_pairs={{2,1},{0,5},{6,2},{4,6},{10,9},{8,13},{14,10},{12,14},{18,17},{16,... | collective-permute-start | bytes 1572872 | tf_op jit(solution)/shard_map/ppermute | solution.py:446
  21.6 1.3 collective-permute-start.6
  24.3 1.4 collective-permute-done.k0
  26.4 9.0 %collective-permute-start.12 = (f32[8,64,256]{2,1,0:T(8,128)S(1)}, f32[8,64,256]{2,1,0:T(8,128)S(1)}, u32[]{:S(2)}, u32[]{:S(2)}) collective-permute-start(f32[8,64,256]{2,1,0:T(8,128)S(1)} %shard_map.120), channel_id=1, source_target_pairs={{2,1},{0,5},{6,2},{4,6},{10,9},{8,13},{14,10},{12,14},{18,17},{16,... | collective-permute-start | bytes 1572872 | tf_op jit(solution)/shard_map/ppermute | solution.py:446
  35.4 1.5 collective-permute-done.2.k2
  36.9 4.4 %shard_map.117 = (f32[272,256]{1,0:T(8,128)S(1)}, f32[8,256,256]{2,1,0:T(8,128)S(1)}, f32[8,256]{1,0:T(8,128)S(1)}) custom-call(s32[1]{0:T(128)} %bitcast.1.where, f32[8,64,256]{2,1,0:T(8,128)} %collective-permute-done.k0, f32[8,64,256]{2,1,0:T(8,128)} %collective-permute-done.1.k1, f32[8,64,256]{2,1,0:T(8,128)} %collective-permute-done.2.k2, ...), custom_call_target="tpu_custom_call" | custom-call | tf_op jit(solution)/shard_map/pallas_call | solution.py:393
  42.1 6.0 %collective-permute-done.6.rest_0_.f0 = f32[8,64,256]{2,1,0:T(8,128)S(1)} collective-permute-done((f32[8,64,256]{2,1,0:T(8,128)S(1)}, f32[8,64,256]{2,1,0:T(8,128)S(1)}, u32[]{:S(2)}, u32[]{:S(2)}) %collective-permute-start.6) | collective-permute-done | bytes 524320 | tf_op jit(solution)/shard_map/ppermute | solution.py:446
  49.0 1.5 collective-permute-start.8
  50.5 10.3 %collective-permute-start.7 = (f32[8,64,256]{2,1,0:T(8,128)}, f32[8,64,256]{2,1,0:T(8,128)}, u32[]{:S(2)}, u32[]{:S(2)}) collective-permute-start(f32[8,64,256]{2,1,0:T(8,128)} %shard_map.113.rest_0_), channel_id=1, source_target_pairs={{0,1},{2,5},{4,2},{6,6},{8,9},{10,13},{12,10},{14,14},{16,17},{18,... | collective-permute-start | bytes 1572872 | tf_op jit(solution)/shard_map/ppermute | solution.py:446
  60.9 1.5 collective-permute-start.10
  62.3 2.1 %collective-permute-start.9 = (f32[8,64,256]{2,1,0:T(8,128)}, f32[8,64,256]{2,1,0:T(8,128)}, u32[]{:S(2)}, u32[]{:S(2)}) collective-permute-start(f32[8,64,256]{2,1,0:T(8,128)} %shard_map.114.rest_1_), channel_id=1, source_target_pairs={{2,1},{0,5},{6,2},{4,6},{10,9},{8,13},{14,10},{12,14},{18,17},{16,... | collective-permute-start | bytes 1572872 | tf_op jit(solution)/shard_map/ppermute | solution.py:446
  65.1 1.5 collective-permute-start.15
  70.0 2.1 %shard_map.122 = (f32[8,256,256]{2,1,0:T(8,128)S(1)}, f32[8,256,256]{2,1,0:T(8,128)S(1)}) custom-call(s32[1]{0:T(128)} %bitcast.1.where, f32[8,64,256]{2,1,0:T(8,128)S(1)} %collective-permute-done.6.rest_0_.f0, f32[8,64,256]{2,1,0:T(8,128)S(1)} %copy-done.9, f32[8,64,256]{2,1,0:T(8,128)S(1)} %copy-done.13, f32[8,64,256]{2,1,0:T(8,128)S(1)} %copy-done.11, ...), custom_call_target="tpu_custom_call" | custom-call | tf_op jit(solution)/shard_map/pallas_call | solution.py:393
  72.2 1.3 shard_map.123
  74.4 1.4 shard_map.124
  75.9 4.9 %collective-permute-done.9.g2 = f32[8,64,256]{2,1,0:T(8,128)} collective-permute-done((f32[8,64,256]{2,1,0:T(8,128)}, f32[8,64,256]{2,1,0:T(8,128)}, u32[]{:S(2)}, u32[]{:S(2)}) %collective-permute-start.9) | collective-permute-done | bytes 524320 | tf_op jit(solution)/shard_map/ppermute | solution.py:446
  80.8 6.2 %shard_map.125 = (f32[512,256]{1,0:T(8,128)S(1)}, f32[8,256,256]{2,1,0:T(8,128)S(1)}, f32[8,256,256]{2,1,0:T(8,128)S(1)}) custom-call(s32[2]{0:T(128)S(1)} %pad_add_fusion.where, f32[8,64,256]{2,1,0:T(8,128)} %collective-permute-done.7.g0, f32[8,64,256]{2,1,0:T(8,128)} %collective-permute-done.8.g1, ...), custom_call_target="tpu_custom_call", output_to_operand_aliasing={{1}: (6, {}), {2}: (5, {})} | custom-call | tf_op jit(solution)/shard_map/pallas_call | solution.py:393
  88.8 2.8 %shard_map.127 = (f32[8,256]{1,0:T(8,128)S(1)}, f32[16,256]{1,0:T(8,128)S(1)}) custom-call(s32[2]{0:T(128)S(1)} %pad_add_fusion.where, f32[8,64,256]{2,1,0:T(8,128)} %collective-permute-done.7.g0, f32[8,64,256]{2,1,0:T(8,128)} %collective-permute-done.8.g1, f32[8,64,256]{2,1,0:T(8,128)} %collective-permute-done.9.g2, ...), custom_call_target="tpu_custom_call" | custom-call | tf_op jit(solution)/shard_map/pallas_call | solution.py:393
  94.7 1.6 shard_map.130
  96.9 1.4 collective-permute-start.23
  98.3 1.4 collective-permute-start.22
  99.7 1.4 collective-permute-start.26
  101.0 1.3 collective-permute-start.25
  102.5 3.2 %shard_map.131.own = f32[272,256]{1,0:T(8,128)S(1)} custom-call(s32[1]{0:T(128)} %bitcast.2.where, f32[272,256]{1,0:T(8,128)} %collective-permute-done.22.t1, f32[272,256]{1,0:T(8,128)} %collective-permute-done.23.t2, f32[272,256]{1,0:T(8,128)S(1)} %collective-permute-done.24.t3, f32[256,256]{1,0:T(8,128)} %collective-permute-done.25.c2, ...), custom_call_target="tpu_custom_call" | custom-call | tf_op jit(solution)/shard_map/pallas_call | solution.py:393
  106.4 3.2 %shard_map.132 = (f32[520,256]{1,0:T(8,128)S(1)}, f32[520,256]{1,0:T(8,128)S(1)}, f32[520,256]{1,0:T(8,128)S(1)}, f32[520,256]{1,0:T(8,128)S(1)}) custom-call(s32[1]{0:T(128)} %bitcast.1.where, f32[272,256]{1,0:T(8,128)S(1)} %shard_map.131.own, f32[272,256]{1,0:T(8,128)S(1)} %collective-permute-done.27.other, f32[528,256]{1,0:T(8,128)S(1)} %pad_maximum_fusion.1.next_total, ...), custom_call_target="tpu_custom_call" | custom-call | tf_op jit(solution)/shard_map/pallas_call | solution.py:393
  109.6 1.3 collective-permute-start.28
  113.6 48.1 %collective-permute-done.28.a0 = f32[520,256]{1,0:T(8,128)S(1)} collective-permute-done((f32[520,256]{1,0:T(8,128)S(1)}, f32[520,256]{1,0:T(8,128)S(1)}, u32[]{:S(2)}, u32[]{:S(2)}) %collective-permute-start.28) | collective-permute-done | bytes 532512 | tf_op jit(solution)/shard_map/ppermute | solution.py:455
  161.6 1.8 %collective-permute-done.30.a2 = f32[520,256]{1,0:T(8,128)S(1)} collective-permute-done((f32[520,256]{1,0:T(8,128)S(1)}, f32[520,256]{1,0:T(8,128)S(1)}, u32[]{:S(2)}, u32[]{:S(2)}) %collective-permute-start.30) | collective-permute-done | bytes 532512 | tf_op jit(solution)/shard_map/ppermute | solution.py:455
  163.5 1.7 %shard_map.133 = (f32[16,64]{1,0:T(8,128)}, f32[1024,256]{1,0:T(8,128)}) custom-call(s32[1]{0:T(128)} %bitcast.where, f32[520,256]{1,0:T(8,128)S(1)} %collective-permute-done.28.a0, f32[520,256]{1,0:T(8,128)S(1)} %collective-permute-done.29.a1, f32[520,256]{1,0:T(8,128)S(1)} %collective-permute-done.30.a2, f32[520,256]{1,0:T(8,128)S(1)} %collective-permute-done.31.a3), custom_call_target="tpu_custom_call" | custom-call | tf_op jit(solution)/shard_map/pallas_call | solution.py:393
  (122 shorter events, 23.3 us)
Async XLA Ops:
  2.7 20.8 %collective-permute-start.1 = (f32[8,64,256]{2,1,0:T(8,128)}, f32[8,64,256]{2,1,0:T(8,128)}, u32[]{:S(2)}, u32[]{:S(2)}) collective-permute-start(f32[8,64,256]{2,1,0:T(8,128)} %shard_map.115), channel_id=1, source_target_pairs={{1,1},{3,5},{5,2},{7,6},{9,9},{11,13},{13,10},{15,14},{17,17},{19,... | collective-permute-start | bytes 1572872 | tf_op jit(solution)/shard_map/ppermute | solution.py:446
  4.2 21.5 %collective-permute-start = (f32[8,64,256]{2,1,0:T(8,128)}, f32[8,64,256]{2,1,0:T(8,128)}, u32[]{:S(2)}, u32[]{:S(2)}) collective-permute-start(f32[8,64,256]{2,1,0:T(8,128)} %shard_map.115), channel_id=1, source_target_pairs={{0,1},{2,5},{4,2},{6,6},{8,9},{10,13},{12,10},{14,14},{16,17},{18,... | collective-permute-start | bytes 1572872 | tf_op jit(solution)/shard_map/ppermute | solution.py:446
  14.7 11.7 %collective-permute-start.3 = (f32[8,64,256]{2,1,0:T(8,128)}, f32[8,64,256]{2,1,0:T(8,128)}, u32[]{:S(2)}, u32[]{:S(2)}) collective-permute-start(f32[8,64,256]{2,1,0:T(8,128)} %shard_map.116), channel_id=1, source_target_pairs={{3,1},{1,5},{7,2},{5,6},{11,9},{9,13},{15,10},{13,14},{19,17},{17,... | collective-permute-start | bytes 1572872 | tf_op jit(solution)/shard_map/ppermute | solution.py:446
  16.1 20.8 %collective-permute-start.2 = (f32[8,64,256]{2,1,0:T(8,128)}, f32[8,64,256]{2,1,0:T(8,128)}, u32[]{:S(2)}, u32[]{:S(2)}) collective-permute-start(f32[8,64,256]{2,1,0:T(8,128)} %shard_map.116), channel_id=1, source_target_pairs={{2,1},{0,5},{6,2},{4,6},{10,9},{8,13},{14,10},{12,14},{18,17},{16,... | collective-permute-start | bytes 1572872 | tf_op jit(solution)/shard_map/ppermute | solution.py:446
  18.6 3.0 %collective-permute-start.4 = (f32[16,256]{1,0:T(8,128)S(1)}, f32[16,256]{1,0:T(8,128)S(1)}, u32[]{:S(2)}, u32[]{:S(2)}) collective-permute-start(f32[16,256]{1,0:T(8,128)S(1)} %copy-done.20), channel_id=1, source_target_pairs={{0,4},{4,0},{8,12},{12,8},{16,20},{20,16},{24,28},{28,24},{1,5},{5... | collective-permute-start | bytes 49160 | tf_op jit(solution)/shard_map/ppermute | solution.py:472
  21.6 26.4 %collective-permute-start.6 = (f32[8,64,256]{2,1,0:T(8,128)S(1)}, f32[8,64,256]{2,1,0:T(8,128)S(1)}, u32[]{:S(2)}, u32[]{:S(2)}) collective-permute-start(f32[8,64,256]{2,1,0:T(8,128)S(1)} %shard_map.118), channel_id=1, source_target_pairs={{0,1},{2,5},{4,2},{6,6},{8,9},{10,13},{12,10},{14,14},{16,17},{18,... | collective-permute-start | bytes 1572872 | tf_op jit(solution)/shard_map/ppermute | solution.py:446
  23.6 27.0 %collective-permute-start.11 = (f32[8,64,256]{2,1,0:T(8,128)S(1)}, f32[8,64,256]{2,1,0:T(8,128)S(1)}, u32[]{:S(2)}, u32[]{:S(2)}) collective-permute-start(f32[8,64,256]{2,1,0:T(8,128)S(1)} %shard_map.118), channel_id=1, source_target_pairs={{1,1},{3,5},{5,2},{7,6},{9,9},{11,13},{13,10},{15,14},{17,17},{19,... | collective-permute-start | bytes 1572872 | tf_op jit(solution)/shard_map/ppermute | solution.py:446
  25.7 35.2 %collective-permute-start.13 = (f32[8,64,256]{2,1,0:T(8,128)S(1)}, f32[8,64,256]{2,1,0:T(8,128)S(1)}, u32[]{:S(2)}, u32[]{:S(2)}) collective-permute-start(f32[8,64,256]{2,1,0:T(8,128)S(1)} %shard_map.120), channel_id=1, source_target_pairs={{3,1},{1,5},{7,2},{5,6},{11,9},{9,13},{15,10},{13,14},{19,17},{17,... | collective-permute-start | bytes 1572872 | tf_op jit(solution)/shard_map/ppermute | solution.py:446
  26.4 35.9 %collective-permute-start.12 = (f32[8,64,256]{2,1,0:T(8,128)S(1)}, f32[8,64,256]{2,1,0:T(8,128)S(1)}, u32[]{:S(2)}, u32[]{:S(2)}) collective-permute-start(f32[8,64,256]{2,1,0:T(8,128)S(1)} %shard_map.120), channel_id=1, source_target_pairs={{2,1},{0,5},{6,2},{4,6},{10,9},{8,13},{14,10},{12,14},{18,17},{16,... | collective-permute-start | bytes 1572872 | tf_op jit(solution)/shard_map/ppermute | solution.py:446
  41.4 6.7 %collective-permute-start.5 = (f32[272,256]{1,0:T(8,128)S(1)}, f32[272,256]{1,0:T(8,128)S(1)}, u32[]{:S(2)}, u32[]{:S(2)}) collective-permute-start(f32[272,256]{1,0:T(8,128)S(1)} %get-tuple-element.25.own), channel_id=1, source_target_pairs={{5,1},{6,2},{13,9},{14,10},{21,17},{22,18},{29,25},{30,26}} | collective-permute-start | bytes 835592 | tf_op jit(solution)/shard_map/ppermute | solution.py:470
  48.3 16.1 %collective-permute-start.14 = (f32[272,256]{1,0:T(8,128)S(1)}, f32[272,256]{1,0:T(8,128)S(1)}, u32[]{:S(2)}, u32[]{:S(2)}) collective-permute-start(f32[272,256]{1,0:T(8,128)S(1)} %shard_map.119.own), channel_id=1, source_target_pairs={{1,2},{2,1},{9,10},{10,9},{17,18},{18,17},{25,26},{26,25}} | collective-permute-start | bytes 835592 | tf_op jit(solution)/shard_map/ppermute | solution.py:470
  49.0 26.8 %collective-permute-start.8 = (f32[8,64,256]{2,1,0:T(8,128)}, f32[8,64,256]{2,1,0:T(8,128)}, u32[]{:S(2)}, u32[]{:S(2)}) collective-permute-start(f32[8,64,256]{2,1,0:T(8,128)} %shard_map.113.rest_0_), channel_id=1, source_target_pairs={{1,1},{3,5},{5,2},{7,6},{9,9},{11,13},{13,10},{15,14},{17,17},{19,... | collective-permute-start | bytes 1572872 | tf_op jit(solution)/shard_map/ppermute | solution.py:446
  50.5 25.3 %collective-permute-start.7 = (f32[8,64,256]{2,1,0:T(8,128)}, f32[8,64,256]{2,1,0:T(8,128)}, u32[]{:S(2)}, u32[]{:S(2)}) collective-permute-start(f32[8,64,256]{2,1,0:T(8,128)} %shard_map.113.rest_0_), channel_id=1, source_target_pairs={{0,1},{2,5},{4,2},{6,6},{8,9},{10,13},{12,10},{14,14},{16,17},{18,... | collective-permute-start | bytes 1572872 | tf_op jit(solution)/shard_map/ppermute | solution.py:446
  60.9 15.0 %collective-permute-start.10 = (f32[8,64,256]{2,1,0:T(8,128)}, f32[8,64,256]{2,1,0:T(8,128)}, u32[]{:S(2)}, u32[]{:S(2)}) collective-permute-start(f32[8,64,256]{2,1,0:T(8,128)} %shard_map.114.rest_1_), channel_id=1, source_target_pairs={{3,1},{1,5},{7,2},{5,6},{11,9},{9,13},{15,10},{13,14},{19,17},{17,... | collective-permute-start | bytes 1572872 | tf_op jit(solution)/shard_map/ppermute | solution.py:446
  62.3 18.4 %collective-permute-start.9 = (f32[8,64,256]{2,1,0:T(8,128)}, f32[8,64,256]{2,1,0:T(8,128)}, u32[]{:S(2)}, u32[]{:S(2)}) collective-permute-start(f32[8,64,256]{2,1,0:T(8,128)} %shard_map.114.rest_1_), channel_id=1, source_target_pairs={{2,1},{0,5},{6,2},{4,6},{10,9},{8,13},{14,10},{12,14},{18,17},{16,... | collective-permute-start | bytes 1572872 | tf_op jit(solution)/shard_map/ppermute | solution.py:446
  65.1 7.0 %collective-permute-start.15 = (f32[272,256]{1,0:T(8,128)S(1)}, f32[272,256]{1,0:T(8,128)}, u32[]{:S(2)}, u32[]{:S(2)}) collective-permute-start(f32[272,256]{1,0:T(8,128)S(1)} %shard_map.121.after.own), channel_id=1, source_target_pairs={{1,9},{2,10},{9,1},{10,2},{17,25},{18,26},{25,17},{26,18}} | collective-permute-start | bytes 835592 | tf_op jit(solution)/shard_map/ppermute | solution.py:470
  73.5 0.9 collective-permute-start.16
  87.0 4.6 %collective-permute-start.17 = (f32[512,256]{1,0:T(8,128)S(1)}, f32[512,256]{1,0:T(8,128)S(1)}, u32[]{:S(2)}, u32[]{:S(2)}) collective-permute-start(f32[512,256]{1,0:T(8,128)S(1)} %get-tuple-element.33.own), channel_id=1, source_target_pairs={{5,1},{6,2},{13,9},{14,10},{21,17},{22,18},{29,25},{30,26}} | collective-permute-start | bytes 1572872 | tf_op jit(solution)/shard_map/ppermute | solution.py:470
  87.7 0.7 collective-permute-start.18
  92.3 2.3 %collective-permute-start.20 = (f32[512,256]{1,0:T(8,128)S(1)}, f32[512,256]{1,0:T(8,128)S(1)}, u32[]{:S(2)}, u32[]{:S(2)}) collective-permute-start(f32[512,256]{1,0:T(8,128)S(1)} %shard_map.128), channel_id=1, source_target_pairs={{1,2},{2,1},{9,10},{10,9},{17,18},{18,17},{25,26},{26,25}} | collective-permute-start | bytes 1572872 | tf_op jit(solution)/shard_map/ppermute | solution.py:470
  93.0 0.7 collective-permute-start.19
  93.9 0.8 collective-permute-start.21
  96.2 6.2 %collective-permute-start.24 = (f32[272,256]{1,0:T(8,128)}, f32[272,256]{1,0:T(8,128)S(1)}, u32[]{:S(2)}, u32[]{:S(2)}) collective-permute-start(f32[272,256]{1,0:T(8,128)} %get-tuple-element.38), channel_id=1, source_target_pairs={{17,9},{18,10},{25,1},{26,2}} | collective-permute-start | bytes 835592 | tf_op jit(solution)/shard_map/ppermute | solution.py:569
  96.9 5.6 %collective-permute-start.23 = (f32[272,256]{1,0:T(8,128)}, f32[272,256]{1,0:T(8,128)}, u32[]{:S(2)}, u32[]{:S(2)}) collective-permute-start(f32[272,256]{1,0:T(8,128)} %get-tuple-element.38), channel_id=1, source_target_pairs={{17,1},{18,2},{25,9},{26,10}} | collective-permute-start | bytes 835592 | tf_op jit(solution)/shard_map/ppermute | solution.py:569
  98.3 4.2 %collective-permute-start.22 = (f32[272,256]{1,0:T(8,128)}, f32[272,256]{1,0:T(8,128)}, u32[]{:S(2)}, u32[]{:S(2)}) collective-permute-start(f32[272,256]{1,0:T(8,128)} %get-tuple-element.38), channel_id=1, source_target_pairs={{9,1},{10,2},{25,17},{26,18}} | collective-permute-start | bytes 835592 | tf_op jit(solution)/shard_map/ppermute | solution.py:569
  99.7 2.8 %collective-permute-start.26 = (f32[256,256]{1,0:T(8,128)}, f32[256,256]{1,0:T(8,128)}, u32[]{:S(2)}, u32[]{:S(2)}) collective-permute-start(f32[256,256]{1,0:T(8,128)} %get-tuple-element.39), channel_id=1, source_target_pairs={{9,1},{10,2},{17,9},{18,10}} | collective-permute-start | bytes 786440 | tf_op jit(solution)/shard_map/ppermute | solution.py:569
  101.0 1.4 collective-permute-start.25
  105.6 0.7 collective-permute-start.27
  109.6 52.1 %collective-permute-start.28 = (f32[520,256]{1,0:T(8,128)S(1)}, f32[520,256]{1,0:T(8,128)S(1)}, u32[]{:S(2)}, u32[]{:S(2)}) collective-permute-start(f32[520,256]{1,0:T(8,128)S(1)} %get-tuple-element.42), channel_id=1, source_target_pairs={{1,0},{5,2},{2,4},{6,6},{9,8},{13,10},{10,12},{14,14},{17,16},{21,... | collective-permute-start | bytes 1597448 | tf_op jit(solution)/shard_map/ppermute | solution.py:455
  110.9 50.8 %collective-permute-start.29 = (f32[520,256]{1,0:T(8,128)S(1)}, f32[520,256]{1,0:T(8,128)S(1)}, u32[]{:S(2)}, u32[]{:S(2)}) collective-permute-start(f32[520,256]{1,0:T(8,128)S(1)} %get-tuple-element.43), channel_id=1, source_target_pairs={{1,1},{5,3},{2,5},{6,7},{9,9},{13,11},{10,13},{14,15},{17,17},{21,... | collective-permute-start | bytes 1597448 | tf_op jit(solution)/shard_map/ppermute | solution.py:455
  111.6 51.9 %collective-permute-start.30 = (f32[520,256]{1,0:T(8,128)S(1)}, f32[520,256]{1,0:T(8,128)S(1)}, u32[]{:S(2)}, u32[]{:S(2)}) collective-permute-start(f32[520,256]{1,0:T(8,128)S(1)} %get-tuple-element.44), channel_id=1, source_target_pairs={{1,2},{5,0},{2,6},{6,4},{9,10},{13,8},{10,14},{14,12},{17,18},{21,... | collective-permute-start | bytes 1597448 | tf_op jit(solution)/shard_map/ppermute | solution.py:455
  112.9 50.6 %collective-permute-start.31 = (f32[520,256]{1,0:T(8,128)S(1)}, f32[520,256]{1,0:T(8,128)S(1)}, u32[]{:S(2)}, u32[]{:S(2)}) collective-permute-start(f32[520,256]{1,0:T(8,128)S(1)} %get-tuple-element.45), channel_id=1, source_target_pairs={{1,3},{5,1},{2,7},{6,5},{9,11},{13,9},{10,15},{14,13},{17,19},{21,... | collective-permute-start | bytes 1597448 | tf_op jit(solution)/shard_map/ppermute | solution.py:455
  (23 other events, 130.7 us)
